TPU v7x, 128 devices: a whole 4x4x4 slice. The times are simulated.
128 devices in a mesh: dp: 32 (over x_hi, y, z), tensor: 4 (over x_lo, core).
Axes of the slice: x: 4 (x_hi: 2, x_lo: 2; x = x_hi * 2 + x_lo), y: 4, z: 4, core: 2. Of those that a mesh axis runs over, the one named last changes fastest.
Arguments:
- inputs: bfloat16 [32768, 640], P('dp'), may hold values from -6 to 6
- segments: int32 [32768], P('dp'), may hold values from 0 to 63, never falling along the last dimension, each value on 1 to 2048 neighbouring positions
- positions: int32 [32768], P('dp'), may hold values from 0 to 2047
- cotangent: bfloat16 [32768, 640], P('dp'), may hold values from -6 to 6
- w_query: bfloat16 [640, 1024], P(None, 'tensor'), may hold values from -0.25 to 0.25
- w_key: bfloat16 [640, 256], replicated, may hold values from -0.25 to 0.25
- w_value: bfloat16 [640, 256], replicated, may hold values from -0.25 to 0.25
- w_out: bfloat16 [1024, 640], P('tensor'), may hold values from -0.1875 to 0.1875
- w_gate: bfloat16 [640, 2048], P(None, 'tensor'), may hold values from -0.25 to 0.25
- w_up: bfloat16 [640, 2048], P(None, 'tensor'), may hold values from -0.25 to 0.25
- w_down: bfloat16 [2048, 640], P('tensor'), may hold values from -0.125 to 0.125
- g_attn_in: float32 [640], replicated, may hold values from 0.1 to 1.9
- g_attn_out: float32 [640], replicated, may hold values from 0.1 to 1.9
- g_ffn_in: float32 [640], replicated, may hold values from 0.1 to 1.9
- g_ffn_out: float32 [640], replicated, may hold values from 0.1 to 1.9
- g_query: float32 [256], replicated, may hold values from 0.1 to 1.9
- g_key: float32 [256], replicated, may hold values from 0.1 to 1.9
Outputs:
- output: bfloat16 [32768, 640], P('dp')
- input_grad: bfloat16 [32768, 640], P('dp')
- grad_query: float32 [640, 1024], P(None, 'tensor')
- grad_key: float32 [640, 256], replicated
- grad_value: float32 [640, 256], replicated
- grad_out: float32 [1024, 640], P('tensor')
- grad_gate: float32 [640, 2048], P(None, 'tensor')
- grad_up: float32 [640, 2048], P(None, 'tensor')
- grad_down: float32 [2048, 640], P('tensor')
- grad_attn_in: float32 [640], replicated
- grad_attn_out: float32 [640], replicated
- grad_ffn_in: float32 [640], replicated
- grad_ffn_out: float32 [640], replicated
- grad_qnorm: float32 [256], replicated
- grad_knorm: float32 [256], replicated
Inputs may be any that keep to these rules, and one draw needn't show every extreme that they name: `segments`: document numbers never fall along the tokens; a document holds at most 2048 tokens.
All inputs are finite; a program needn't handle non-finite values.
Results may differ from a plain program's by a relative error of at most 0.03.
Values may be sent and summed in bfloat16 or wider, within the bound.
A program may use at most 128 MiB of HBM per device.

v0:
```python
import math

import jax
import jax.numpy as jnp
from jax import lax
from jax.sharding import PartitionSpec as P

WINDOW = 512
LENGTH = 1024


EPSILON = 1e-06
ROPE_BASE = 10000.0
NEG_LARGE = -1e30


def in_blocks(x, dim, size):
    before, after = (x.shape[:dim], x.shape[dim + 1 :])
    return jnp.moveaxis(x.reshape(*before, size, -1, *after), dim, 0)


def sum_at_owner(x, axis, dim):
    size = lax.axis_size(axis)
    tiles = lax.all_to_all(in_blocks(x, dim, size), axis, 0, 0, tiled=True)
    return jnp.sum(tiles.astype(jnp.float32), axis=0)


def in_order(tiles, dim):
    tiles = jnp.moveaxis(tiles, 0, dim)
    lengths = tiles.shape
    return tiles.reshape(*lengths[:dim], lengths[dim] * lengths[dim + 1], *lengths[dim + 2 :])


def copy_for_each(x, axis):
    copies = jnp.broadcast_to(x, (lax.axis_size(axis), *x.shape))
    return lax.all_to_all(copies, axis, split_axis=0, concat_axis=0, tiled=True)


def collect(x, axis, dim):
    return in_order(copy_for_each(x, axis), dim)


def in_one_piece(arrays, axis, dim, along):
    both = jnp.concatenate(arrays, axis=along)
    out, at, gathered = (lax.all_gather(both, axis, axis=dim, tiled=True), 0, [])
    for a in arrays:
        gathered.append(lax.slice_in_dim(out, at, at + a.shape[along], axis=along))
        at += a.shape[along]
    return tuple(gathered)


def rms_scale(values, gain_vec):
    return (
        values * lax.rsqrt(jnp.mean(values * values, axis=-1, keepdims=True) + EPSILON) * gain_vec
    )


def gain_term(values, grad_vec):
    scaled = values * lax.rsqrt(jnp.mean(values * values, axis=-1, keepdims=True) + EPSILON)
    return jnp.sum(grad_vec * scaled, axis=0)


def rope_tables(positions, head_size):
    half_size = head_size // 2
    inv_freq = ROPE_BASE ** (-2.0 * jnp.arange(half_size, dtype=jnp.float32) / head_size)
    angles = positions.astype(jnp.float32)[:, None] * inv_freq[None, :]
    return (jnp.cos(angles), jnp.sin(angles))


def rotate(values, cosine, sine_table):
    half_size = values.shape[-1] // 2
    first_half = values[..., :half_size]
    second_half = values[..., half_size:]
    return jnp.concatenate(
        [
            first_half * cosine - second_half * sine_table,
            second_half * cosine + first_half * sine_table,
        ],
        axis=-1,
    )


def rotary_norm(raw_vec, gain_vec, cosine, sine_table):
    return rotate(rms_scale(raw_vec, gain_vec), cosine, sine_table)


def windows(blocks, fill_value):
    earlier = jnp.concatenate([jnp.full_like(blocks[:, :1], fill_value), blocks[:, :-1]], axis=1)
    return jnp.concatenate([earlier, blocks], axis=2)


def unwindow(grads, width):
    front_half = grads[:, :, :width]
    back_half = grads[:, :, width:]
    shifted = jnp.concatenate([front_half[:, 1:], jnp.zeros_like(front_half[:, :1])], axis=1)
    return back_half + shifted


def allowed_mask(seg_rows, seg_keys, width):
    row_ids = lax.broadcasted_iota(jnp.int32, (width, 2 * width), 0)
    key_ids = lax.broadcasted_iota(jnp.int32, (width, 2 * width), 1)
    in_window = (key_ids > row_ids) & (key_ids <= row_ids + width)
    return in_window & (seg_rows[:, None] == seg_keys[None, :])


def block_forward(block_item, score_scale):
    q_block, k_window, v_window, seg_rows, seg_keys = block_item
    width = q_block.shape[1]
    scores = (
        jnp.einsum("hqd,kd->hqk", q_block, k_window, preferred_element_type=jnp.float32)
        * score_scale
    )
    allowed = allowed_mask(seg_rows, seg_keys, width)[None]
    masked = jnp.where(allowed, scores, NEG_LARGE)
    row_max = jnp.max(masked, axis=-1, keepdims=True)
    expo_terms = jnp.where(allowed, jnp.exp(masked - row_max), 0.0)
    row_total = jnp.sum(expo_terms, axis=-1, keepdims=True)
    prob_low = (expo_terms / row_total).astype(jnp.bfloat16)
    block_out = jnp.einsum("hqk,kd->hqd", prob_low, v_window, preferred_element_type=jnp.float32)
    return (block_out, (row_max + jnp.log(row_total))[..., 0])


def block_backward(block_item, score_scale):
    q_block, k_window, v_window, seg_rows, seg_keys, log_totals, grad_block = block_item
    width = q_block.shape[1]
    scores = (
        jnp.einsum("hqd,kd->hqk", q_block, k_window, preferred_element_type=jnp.float32)
        * score_scale
    )
    allowed = allowed_mask(seg_rows, seg_keys, width)[None]
    prob_full = jnp.where(allowed, jnp.exp(scores - log_totals[..., None]), 0.0)
    grad_prob = jnp.einsum("hqd,kd->hqk", grad_block, v_window, preferred_element_type=jnp.float32)
    row_dot = jnp.sum(prob_full * grad_prob, axis=-1, keepdims=True)
    grad_scores = (prob_full * (grad_prob - row_dot)).astype(jnp.bfloat16)
    grad_q = (
        jnp.einsum("hqk,kd->hqd", grad_scores, k_window, preferred_element_type=jnp.float32)
        * score_scale
    )
    grad_k = (
        jnp.einsum("hqk,hqd->kd", grad_scores, q_block, preferred_element_type=jnp.float32)
        * score_scale
    )
    grad_v = jnp.einsum(
        "hqk,hqd->kd",
        prob_full.astype(jnp.bfloat16),
        grad_block,
        preferred_element_type=jnp.float32,
    )
    return (grad_q, grad_k, grad_v)


def local(
    inputs,
    segments,
    positions,
    cotangent,
    w_query,
    w_key,
    w_value,
    w_out,
    w_gate,
    w_up,
    w_down,
    g_attn_in,
    g_attn_out,
    g_ffn_in,
    g_ffn_out,
    g_query,
    g_key,
):
    row_count = inputs.shape[0]
    head_size = w_key.shape[1]
    heads_here = w_query.shape[1] // head_size
    seqs_here = row_count // LENGTH
    blocks_per = LENGTH // WINDOW
    block_total = seqs_here * blocks_per
    score_scale = 1.0 / math.sqrt(head_size)
    share_rows = row_count // lax.axis_size("tensor")
    first_row = lax.axis_index("tensor") * share_rows

    def my_rows(values):
        return lax.dynamic_slice_in_dim(values, first_row, share_rows, 0)

    whole_x = inputs.astype(jnp.float32)
    normed = rms_scale(whole_x, g_attn_in).astype(jnp.bfloat16)
    query_raw = jnp.dot(normed, w_query, preferred_element_type=jnp.float32)
    key_raw = jnp.dot(normed, w_key, preferred_element_type=jnp.float32)
    value_raw = jnp.dot(normed, w_value, preferred_element_type=jnp.float32)
    cosine, sine_table = rope_tables(positions, head_size)
    query_heads = query_raw.reshape(row_count, heads_here, head_size).transpose(1, 0, 2)
    q_rot, q_pull = jax.vjp(
        lambda raw_vec, gain_vec: rotary_norm(raw_vec, gain_vec, cosine, sine_table),
        query_heads,
        g_query,
    )
    k_rot, k_pull = jax.vjp(
        lambda raw_vec, gain_vec: rotary_norm(raw_vec, gain_vec, cosine, sine_table), key_raw, g_key
    )
    q_blocks = (
        q_rot.astype(jnp.bfloat16)
        .reshape(heads_here, block_total, WINDOW, head_size)
        .transpose(1, 0, 2, 3)
    )
    k_windows = windows(
        k_rot.astype(jnp.bfloat16).reshape(seqs_here, blocks_per, WINDOW, head_size), 0
    ).reshape(block_total, 2 * WINDOW, head_size)
    v_windows = windows(
        value_raw.astype(jnp.bfloat16).reshape(seqs_here, blocks_per, WINDOW, head_size), 0
    ).reshape(block_total, 2 * WINDOW, head_size)
    seg_rows = segments.reshape(block_total, WINDOW)
    seg_keys = windows(segments.reshape(seqs_here, blocks_per, WINDOW), -1).reshape(
        block_total, 2 * WINDOW
    )
    block_items = (q_blocks, k_windows, v_windows, seg_rows, seg_keys)
    heads_out, log_totals = lax.map(
        lambda block_item: block_forward(block_item, score_scale), block_items
    )
    heads_low = (
        heads_out.astype(jnp.bfloat16)
        .transpose(0, 2, 1, 3)
        .reshape(row_count, heads_here * head_size)
    )
    attn_term = jnp.dot(heads_low, w_out, preferred_element_type=jnp.float32)
    attn_sum = sum_at_owner(attn_term.astype(jnp.bfloat16), "tensor", 0)
    x_rows = my_rows(whole_x)
    attn_norm, attn_pull = jax.vjp(lambda values: rms_scale(values, g_attn_out), attn_sum)
    mid_rows = x_rows + attn_norm
    ffn_in, ffn_pull = jax.vjp(lambda values: rms_scale(values, g_ffn_in), mid_rows)
    ffn_low = collect(ffn_in.astype(jnp.bfloat16), "tensor", 0)
    gate_raw = jnp.dot(ffn_low, w_gate, preferred_element_type=jnp.float32)
    up_raw = jnp.dot(ffn_low, w_up, preferred_element_type=jnp.float32)
    hidden_full, act_pull = jax.vjp(
        lambda gate_in, up_in: jax.nn.gelu(gate_in, approximate=True) * up_in, gate_raw, up_raw
    )
    hidden = hidden_full.astype(jnp.bfloat16)
    ffn_term = jnp.dot(hidden, w_down, preferred_element_type=jnp.float32)
    ffn_sum = sum_at_owner(ffn_term.astype(jnp.bfloat16), "tensor", 0)
    cot_rows = my_rows(cotangent).astype(jnp.float32)
    out_norm, out_pull = jax.vjp(lambda values: rms_scale(values, g_ffn_out), ffn_sum)
    result = mid_rows + out_norm
    grad_ffn = out_pull(cot_rows)[0]
    output, grad_ffn_low = in_one_piece(
        (result.astype(jnp.bfloat16), grad_ffn.astype(jnp.bfloat16)), "tensor", 0, 1
    )
    grad_hidden = jnp.einsum("rd,fd->rf", grad_ffn_low, w_down, preferred_element_type=jnp.float32)
    grad_down = jnp.einsum("rf,rd->fd", hidden, grad_ffn_low, preferred_element_type=jnp.float32)
    grad_gate_full, grad_up_full = act_pull(grad_hidden)
    grad_gate_low = grad_gate_full.astype(jnp.bfloat16)
    grad_up_low = grad_up_full.astype(jnp.bfloat16)
    grad_gate = jnp.einsum("rd,rf->df", ffn_low, grad_gate_low, preferred_element_type=jnp.float32)
    grad_up = jnp.einsum("rd,rf->df", ffn_low, grad_up_low, preferred_element_type=jnp.float32)
    ffn_in_term = jnp.einsum(
        "rf,df->rd", grad_gate_low, w_gate, preferred_element_type=jnp.float32
    ) + jnp.einsum("rf,df->rd", grad_up_low, w_up, preferred_element_type=jnp.float32)
    ffn_in_grad = sum_at_owner(ffn_in_term.astype(jnp.bfloat16), "tensor", 0)
    grad_mid = cot_rows + ffn_pull(ffn_in_grad)[0]
    grad_attn = attn_pull(grad_mid)[0]
    grad_attn_low = collect(grad_attn.astype(jnp.bfloat16), "tensor", 0)
    grad_out = jnp.einsum("rh,rd->hd", heads_low, grad_attn_low, preferred_element_type=jnp.float32)
    grad_heads = jnp.einsum(
        "rd,hd->rh", grad_attn_low, w_out, preferred_element_type=jnp.float32
    ).astype(jnp.bfloat16)
    grad_blocks = grad_heads.reshape(block_total, WINDOW, heads_here, head_size).transpose(
        0, 2, 1, 3
    )
    grad_qb, grad_kw, grad_vw = lax.map(
        lambda block_item: block_backward(block_item, score_scale),
        block_items + (log_totals, grad_blocks),
    )
    grad_q_rot = grad_qb.transpose(1, 0, 2, 3).reshape(heads_here, row_count, head_size)
    grad_k_rot = unwindow(
        grad_kw.reshape(seqs_here, blocks_per, 2 * WINDOW, head_size), WINDOW
    ).reshape(row_count, head_size)
    grad_v_full = unwindow(
        grad_vw.reshape(seqs_here, blocks_per, 2 * WINDOW, head_size), WINDOW
    ).reshape(row_count, head_size)
    grad_query_raw, grad_qnorm = q_pull(grad_q_rot)
    grad_key_raw, grad_knorm = k_pull(grad_k_rot)
    grad_q_low = (
        grad_query_raw.transpose(1, 0, 2)
        .reshape(row_count, heads_here * head_size)
        .astype(jnp.bfloat16)
    )
    grad_k_low = grad_key_raw.astype(jnp.bfloat16)
    grad_v_low = grad_v_full.astype(jnp.bfloat16)
    grad_query = jnp.einsum("rd,rh->dh", normed, grad_q_low, preferred_element_type=jnp.float32)
    grad_key = jnp.einsum("rd,rh->dh", normed, grad_k_low, preferred_element_type=jnp.float32)
    grad_value = jnp.einsum("rd,rh->dh", normed, grad_v_low, preferred_element_type=jnp.float32)
    input_term = jnp.einsum("rh,dh->rd", grad_q_low, w_query, preferred_element_type=jnp.float32)
    input_term = input_term + jnp.einsum(
        "rh,dh->rd", grad_k_low, w_key, preferred_element_type=jnp.float32
    )
    input_term = input_term + jnp.einsum(
        "rh,dh->rd", grad_v_low, w_value, preferred_element_type=jnp.float32
    )
    input_sum = sum_at_owner(input_term.astype(jnp.bfloat16), "tensor", 0)
    x_grad_norm = jax.vjp(lambda values: rms_scale(values, g_attn_in), x_rows)[1](input_sum)[0]
    grad_rows = grad_mid + x_grad_norm
    gain_inputs = (x_rows, input_sum, attn_sum, grad_mid, mid_rows, ffn_in_grad, ffn_sum, cot_rows)
    input_grad = collect(grad_rows.astype(jnp.bfloat16), "tensor", 0)
    grad_attn_in = gain_term(gain_inputs[0], gain_inputs[1])
    grad_attn_out = gain_term(gain_inputs[2], gain_inputs[3])
    grad_ffn_in = gain_term(gain_inputs[4], gain_inputs[5])
    grad_ffn_out = gain_term(gain_inputs[6], gain_inputs[7])
    grad_query, grad_out, grad_gate, grad_up, grad_down = (
        lax.psum(grad_query.astype(jnp.bfloat16), "dp").astype(jnp.float32),
        lax.psum(grad_out.astype(jnp.bfloat16), "dp").astype(jnp.float32),
        lax.psum(grad_gate.astype(jnp.bfloat16), "dp").astype(jnp.float32),
        lax.psum(grad_up.astype(jnp.bfloat16), "dp").astype(jnp.float32),
        lax.psum(grad_down.astype(jnp.bfloat16), "dp").astype(jnp.float32),
    )
    summed_all = lax.psum(
        (
            grad_key,
            grad_value,
            grad_attn_in,
            grad_attn_out,
            grad_ffn_in,
            grad_ffn_out,
            grad_qnorm,
            grad_knorm,
        ),
        ("dp", "tensor"),
    )
    return (
        output,
        input_grad,
        grad_query,
        summed_all[0],
        summed_all[1],
        grad_out,
        grad_gate,
        grad_up,
        grad_down,
        summed_all[2],
        summed_all[3],
        summed_all[4],
        summed_all[5],
        summed_all[6],
        summed_all[7],
    )


def solution(mesh):
    placed = (
        P("dp", None),
        P("dp"),
        P("dp"),
        P("dp", None),
        P(None, "tensor"),
        P(),
        P(),
        P("tensor", None),
        P(None, "tensor"),
        P(None, "tensor"),
        P("tensor", None),
        P(),
        P(),
        P(),
        P(),
        P(),
        P(),
    )
    return jax.shard_map(
        local,
        mesh=mesh,
        in_specs=placed,
        out_specs=(
            P("dp", None),
            P("dp", None),
            P(None, "tensor"),
            P(),
            P(),
            P("tensor", None),
            P(None, "tensor"),
            P(None, "tensor"),
            P("tensor", None),
            P(),
            P(),
            P(),
            P(),
            P(),
            P(),
        ),
        check_vma=False,
    )
```

profile of v0, /device:TPU:1, one launch (start us, length us, event | category | flops | bytes accessed | tf_op | source)
XLA Modules:
  0.0 761.8 jit_solution(5090513711252032929)
XLA Ops:
  9.4 1.6 multiply_reduce_fusion.1
  11.1 2.1 convolution_convert_fusion.6
  15.2 2.4 fusion.97
  17.9 2.4 fusion.91
  22.3 10.3 %while.28 = (s32[]{:T(128)}, bf16[2,1,512,256]{3,2,1,0:T(8,128)(2,1)S(1)}, f32[2,1,512]{2,1,0:T(1,128)}, s32[2,512]{1,0:T(2,128)S(1)}, s32[2,1024]{1,0:T(2,128)S...) while((s32[]{:T(128)}, ...), condition=%wide.region_6.7_spmd.clone, body=%wide.region_3.6_spmd.sunk.clone | while | flops 552075264 | bytes 8220833 | solution.py:215
  22.3 2.0 fusion.189
  25.3 1.4 fusion.191
  27.5 2.0 fusion.189
  30.5 1.4 fusion.191
  32.6 2.6 convolution_convert_fusion
  35.2 5.7 all-to-all-start
  40.9 1.6 convert_element_type.144
  42.5 14.9 %all-to-all-done = bf16[4,256,640]{2,1,0:T(8,128)(2,1)} async-done(((bf16[4,256,640]{2,1,0:T(8,128)(2,1)}), bf16[4,256,640]{2,1,0:T(8,128)(2,1)}, u32[]{:S(2)}, u32[]{:S(2)}) %all-to-all-start) | async-done | bytes 1310752 | tf_op jit(solution)/shard_map/all_to_all | solution.py:24
  57.4 1.6 convert_reduce_fusion.3
  59.6 2.0 multiply_reduce_fusion.14
  62.4 19.7 %all_to_all.35 = bf16[4,256,640]{2,1,0:T(8,128)(2,1)S(1)} all-to-all(bf16[4,256,640]{2,1,0:T(8,128)(2,1)S(1)} %broadcast_in_dim.57), channel_id=1, replica_groups=mesh['dp'=32,'tensor'=4] {'tensor'}, dimensions={0} | all-to-all | bytes 2621440 | tf_op jit(solution)/shard_map/all_to_all | solution.py:36
  83.7 2.6 multiply_convert_fusion.3
  87.3 19.8 %all_to_all.36 = bf16[4,256,640]{2,1,0:T(8,128)(2,1)S(1)} all-to-all(bf16[4,256,640]{2,1,0:T(8,128)(2,1)S(1)} %bitcast.223), channel_id=1, replica_groups=mesh['dp'=32,'tensor'=4] {'tensor'}, dimensions={0} | all-to-all | bytes 2621440 | tf_op jit(solution)/shard_map/all_to_all | solution.py:24
  109.6 36.9 %all-gather.2.cloned.1.call-done = bf16[1024,1280]{1,0:T(8,128)(2,1)} async-done(((bf16[256,1280]{1,0:T(8,128)(2,1)}), bf16[1024,1280]{1,0:T(8,128)(2,1)}) %all-gather.2.cloned.1.call-update) | async-done | bytes 2621456 | tf_op jit(solution)/shard_map/all_gather | solution.py:45
  146.5 5.0 multiply_convert_fusion.2
  154.2 18.6 %all_to_all.37 = bf16[4,256,640]{2,1,0:T(8,128)(2,1)S(1)} all-to-all(bf16[4,256,640]{2,1,0:T(8,128)(2,1)S(1)} %bitcast.209), channel_id=1, replica_groups=mesh['dp'=32,'tensor'=4] {'tensor'}, dimensions={0} | all-to-all | bytes 2621440 | tf_op jit(solution)/shard_map/all_to_all | solution.py:24
  173.9 2.0 multiply_reduce_fusion.7
  177.3 5.3 all-to-all-start.4
  182.6 3.0 convolution_convert_fusion.3
  185.6 1.7 convolution_convert_fusion.4
  187.9 1.9 convolution_convert_fusion.2
  189.8 9.4 %all-to-all-done.4 = bf16[4,256,640]{2,1,0:T(8,128)(2,1)} async-done(((bf16[4,256,640]{2,1,0:T(8,128)(2,1)}), bf16[4,256,640]{2,1,0:T(8,128)(2,1)}, u32[]{:S(2)}, u32[]{:S(2)}) %all-to-all-start.4) | async-done | bytes 1310752 | tf_op jit(solution)/shard_map/all_to_all | solution.py:36
  199.1 2.7 convolution_convert_fusion.7
  201.9 2.0 convolution_convert_fusion.5
  203.9 15.6 %while.29 = (s32[]{:T(128)}, f32[2,1,512,256]{3,2,1,0:T(8,128)S(1)}, f32[2,1024,256]{2,1,0:T(8,128)}, f32[2,1024,256]{2,1,0:T(8,128)}, s32[2,512]{1,0:T(2,128)S(...) while((s32[]{:T(128)}, ...), condition=%wide.region_18.19_spmd.clone, body=%wide.region_16.18_spmd.sunk.clone | while | flops 1349910528 | bytes 58758412 | solution.py:266
  219.5 2.3 fusion.94
  223.5 1.5 convolution_convert_fusion.8
  225.1 1.8 fusion.118
  229.2 2.3 fusion.100
  233.1 2.1 fusion.119
  236.3 3.5 add_convert_fusion
  239.8 5.4 all-to-all-start.5
  245.2 18.8 %all-to-all-done.5 = bf16[4,256,640]{2,1,0:T(8,128)(2,1)} async-done(((bf16[4,256,640]{2,1,0:T(8,128)(2,1)}), bf16[4,256,640]{2,1,0:T(8,128)(2,1)}, u32[]{:S(2)}, u32[]{:S(2)}) %all-to-all-start.5) | async-done | bytes 1310752 | tf_op jit(solution)/shard_map/all_to_all | solution.py:24
  264.1 1.6 convert_reduce_fusion
  267.4 4.1 all-to-all-start.6
  271.5 2.7 fusion.113
  274.2 1.6 fusion.112
  275.8 2.5 slice.62
  278.3 71.3 %all-reduce.9 = (f32[640]{0:T(1024)}, f32[640]{0:T(1024)}, f32[640]{0:T(1024)}, f32[640]{0:T(1024)}, f32[256]{0:T(256)}, /*index=5*/f32[256]{0:T(256)}) all-reduce(f32[640]{0:T(1024)S(1)} %get-tuple-element.133, f32[640]{0:T(1024)S(1)} %copy-done.65, f32[640]{0:T(1024)S(1)} %copy-done.64, ...), channel_id=1, replica_groups=mesh['dp'=32,'tensor'=4] {'dp','tensor'}, use_global_device_ids=true, to_apply=%region_32.33 | all-reduce | flops 3072 | bytes 24576 | tf_op jit(solution)/shard_map/psum | solution.py:312
  349.6 226.8 %all-reduce.17.cloned.1.call-done = (bf16[640,256]{1,0:T(8,128)(2,1)}, bf16[256,640]{1,0:T(8,128)(2,1)}, bf16[640,512]{1,0:T(8,128)(2,1)}, bf16[640,512]{1,0:T(8,128)(2,1)}, bf16[512,640]{1,0:T(8,128)(2,1)}) async-done(((bf16[640,256]{1,0:T(8,128)(2,1)}, bf16[256,640]{1,0:T(8,128)(2,1)}, bf16[640,512]{1,0:T(8,128)(2,1)}, bf16[640,512]{1,0:T(8,128)(2,1)}, bf16[512,640]{1,0:T(8,128)(2,1)}), ...) | async-done | bytes 2621456 | tf_op jit(solution)/shard_map/psum | solution.py:306
  576.4 2.0 convert_element_type.173
  578.4 1.9 convert_element_type.175
  583.8 168.3 %all-reduce.15.cloned.1.call-done = (f32[640,256]{1,0:T(8,128)}, f32[640,256]{1,0:T(8,128)}) async-done(((f32[640,256]{1,0:T(8,128)}, f32[640,256]{1,0:T(8,128)}), (f32[640,256]{1,0:T(8,128)}, f32[640,256]{1,0:T(8,128)})) %all-reduce.15.cloned.1.call-update) | async-done | bytes 1310736 | tf_op jit(solution)/shard_map/psum | solution.py:312
  (290 shorter events, 51.9 us)
Async XLA Ops:
  7.2 79.1 %copy-start = (bf16[512,640]{1,0:T(8,128)(2,1)S(1)}, bf16[512,640]{1,0:T(8,128)(2,1)}, u32[]{:S(2)}) copy-start(bf16[512,640]{1,0:T(8,128)(2,1)} %param.31) | copy-start | bytes 1966084
  7.2 10.6 %copy-start.79 = (f32[128]{0:T(128)}, f32[128]{0:T(128)S(1)}, u32[]{:S(2)}) copy-start(f32[128]{0:T(128)S(1)} %multiply_power_fusion) | copy-start | bytes 1540
  11.1 3.0 copy-start.81
  14.9 2.7 copy-start.68
  14.9 2.9 copy-start.4
  15.0 2.7 copy-start.70
  15.0 2.6 copy-start.48
  35.2 22.2 %all-to-all-start = ((bf16[4,256,640]{2,1,0:T(8,128)(2,1)}), bf16[4,256,640]{2,1,0:T(8,128)(2,1)}, u32[]{:S(2)}, u32[]{:S(2)}) async-start(bf16[4,256,640]{2,1,0:T(8,128)(2,1)} %bitcast.29), calls=%async_computation | async-start | bytes 2621440 | tf_op jit(solution)/shard_map/all_to_all | solution.py:24
  40.9 105.6 %all-gather.2.cloned.1.call-start = ((), (), s32[]{:S(2)}) async-start(), calls=%async_computation.7 | async-start | bytes 3276800 | tf_op jit(solution)/shard_map/all_gather | solution.py:45
  57.4 4.8 copy-start.50
  62.3 19.8 %copy-start.36 = (bf16[640,512]{1,0:T(8,128)(2,1)S(1)}, bf16[640,512]{1,0:T(8,128)(2,1)}, u32[]{:S(2)}) copy-start(bf16[640,512]{1,0:T(8,128)(2,1)} %param.29) | copy-start | bytes 1966084
  83.7 2.6 copy-start.83
  86.3 20.9 %copy-start.84 = (bf16[1024,512]{1,0:T(8,128)(2,1)}, bf16[1024,512]{1,0:T(8,128)(2,1)S(1)}, u32[]{:S(2)}) copy-start(bf16[1024,512]{1,0:T(8,128)(2,1)S(1)} %get-tuple-element.220) | copy-start | bytes 3145732
  87.3 20.2 %copy-start.29 = (bf16[1024,640]{1,0:T(8,128)(2,1)S(1)}, bf16[1024,640]{1,0:T(8,128)(2,1)}, u32[]{:S(2)}) copy-start(bf16[1024,640]{1,0:T(8,128)(2,1)} %param.24) | copy-start | bytes 3932164
  87.3 20.2 %copy-start.60 = (f32[640]{0:T(1024)S(1)}, f32[640]{0:T(1024)}, u32[]{:S(2)}) copy-start(f32[640]{0:T(1024)} %param.35) | copy-start | bytes 7684
  146.5 5.1 copy-start.37
  154.2 18.9 %copy-start.51 = (f32[640]{0:T(1024)S(1)}, f32[640]{0:T(1024)}, u32[]{:S(2)}) copy-start(f32[640]{0:T(1024)} %param.34) | copy-start | bytes 7684
  154.2 18.9 %copy-start.59 = (f32[256]{0:T(256)S(1)}, f32[256]{0:T(256)}, u32[]{:S(2)}) copy-start(f32[256]{0:T(256)} %copy-done.58) | copy-start | bytes 3076
  173.1 2.9 copy-start.76
  176.1 6.5 copy-start.17
  177.3 21.8 %all-to-all-start.4 = ((bf16[4,256,640]{2,1,0:T(8,128)(2,1)}), bf16[4,256,640]{2,1,0:T(8,128)(2,1)}, u32[]{:S(2)}, u32[]{:S(2)}) async-start(bf16[4,256,640]{2,1,0:T(8,128)(2,1)} %broadcast_in_dim.61), calls=%async_computation.4 | async-start | bytes 2621440 | tf_op jit(solution)/shard_map/all_to_all | solution.py:36
  182.6 393.8 %all-reduce.17.cloned.1.call-start = ((), (), s32[]{:S(2)}) async-start(), calls=%async_computation.9 | async-start | bytes 5242880 | tf_op jit(solution)/shard_map/psum | solution.py:306
  182.6 3.0 copy-start.27
  199.1 2.8 copy-start.41
  199.1 4.7 copy-start.24
  199.1 4.8 copy-start.55
  203.9 15.6 %copy-start.80 = (f32[128]{0:T(128)S(1)}, f32[128]{0:T(128)}, u32[]{:S(2)}) copy-start(f32[128]{0:T(128)} %copy-done.79) | copy-start | bytes 1540
  219.5 2.8 copy-start.69
  225.1 3.0 copy-start.20
  229.0 2.4 copy-start.3
  229.0 2.4 copy-start.47
  229.0 2.4 copy-start.73
  229.1 2.8 copy-start.67
  239.8 5.4 copy-start.74
  239.8 25.9 %copy-start.6 = (f32[1024,640]{1,0:T(8,128)S(1)}, f32[1024,640]{1,0:T(8,128)}, u32[]{:S(2)}) copy-start(f32[1024,640]{1,0:T(8,128)} %convert_element_type.144) | copy-start | bytes 7864324
  239.8 24.3 %all-to-all-start.5 = ((bf16[4,256,640]{2,1,0:T(8,128)(2,1)}), bf16[4,256,640]{2,1,0:T(8,128)(2,1)}, u32[]{:S(2)}, u32[]{:S(2)}) async-start(bf16[4,256,640]{2,1,0:T(8,128)(2,1)} %bitcast.207), calls=%async_computation.5 | async-start | bytes 2621440 | tf_op jit(solution)/shard_map/all_to_all | solution.py:24
  245.2 20.7 %copy-start.8 = (f32[256,640]{1,0:T(8,128)S(1)}, f32[256,640]{1,0:T(8,128)}, u32[]{:S(2)}) copy-start(f32[256,640]{1,0:T(8,128)} %copy-done.7) | copy-start | bytes 1966084
  266.2 5.3 copy-start.11
  267.4 82.3 %all-to-all-start.6 = ((bf16[4,256,640]{2,1,0:T(8,128)(2,1)}), bf16[4,256,640]{2,1,0:T(8,128)(2,1)S(1)}, u32[]{:S(2)}, u32[]{:S(2)}) async-start(bf16[4,256,640]{2,1,0:T(8,128)(2,1)} %broadcast_in_dim.101), calls=%async_computation.6 | async-start | bytes 2621440 | tf_op jit(solution)/shard_map/all_to_all | solution.py:36
  271.5 2.7 copy-start.13
  271.5 480.7 %all-reduce.15.cloned.1.call-start = ((), (), s32[]{:S(2)}) async-start(), calls=%async_computation.8 | async-start | bytes 2621440 | tf_op jit(solution)/shard_map/psum | solution.py:312
  275.7 2.5 copy-start.63
  275.7 2.5 copy-start.64
  275.7 2.5 copy-start.65
  576.4 3.8 copy-start.35
  576.4 5.0 copy-start.34
  580.2 2.5 copy-start.33
  752.1 3.2 copy-start.1
  (52 other events, 76.5 us)
Sparse Core Ops, SparseCore 0:
  109.7 36.6 all-gather.1
  235.4 340.9 all-reduce.16
  581.9 170.1 all-reduce.14
where the time goes:
time: 763 us; the launch traced here: 762 us
  waiting for transfers between devices  475 us (62%)
  blocking collectives  129 us (17%)
  matrix products  55.3 us (7%)
  other arithmetic  39.8 us (5%)
  local copies, waits for them, and re-layouts  26.5 us (3%)
  starting transfers between devices  20.5 us (3%)
  between operations  14.7 us (2%)
    psum x1, waiting for transfers between devices, local(): lax.psum(grad_query.astype(jnp.bfloat16), 'dp').astype(jnp.float32)  227 us
    psum x1, waiting for transfers between devices, local(): lax.psum((grad_key, grad_value, grad_attn_in, grad_attn_out, grad_ffn_in,...  168 us
    psum x1, blocking collectives, local(): lax.psum((grad_key, grad_value, grad_attn_in, grad_attn_out, grad_ffn_in,...  71.3 us
    all_to_all x2, blocking collectives, sum_at_owner(): tiles = lax.all_to_all(in_blocks(x, dim, size), axis, 0, 0, tiled=True)  38.5 us
    all_gather x1, waiting for transfers between devices, in_one_piece(): lax.all_gather(both, axis, axis=dim, tiled=True)  36.9 us
    all_to_all x2, waiting for transfers between devices, sum_at_owner(): tiles = lax.all_to_all(in_blocks(x, dim, size), axis, 0, 0, tiled=True)  33.7 us
    all_to_all x1, blocking collectives, copy_for_each(): return lax.all_to_all(copies, axis, split_axis=0, concat_axis=0, tiled=True)  19.7 us
  transfers between devices with their start and end apart: 7, of which 6 were waited for; matrix products, arithmetic and copies ran while one was open for 4% of the time, Pallas kernels for 0%

commit v1 on v0

--- a/solution.py
+++ b/solution.py
@@ -3,7 +3,230 @@
 import jax
 import jax.numpy as jnp
 from jax import lax
+from jax.experimental import pallas as pl
+from jax.experimental.pallas import tpu as pltpu
 from jax.sharding import PartitionSpec as P
+
+MESH = pl.DeviceIdType.MESH
+BF = jnp.bfloat16
+F32 = jnp.float32
+VMEM = pl.BlockSpec(memory_space=pltpu.VMEM)
+VMEM_LIMIT = 60 * 1024 * 1024
+
+
+def neighbours():
+    dp = lax.axis_index("dp")
+    t = lax.axis_index("tensor")
+    z = lax.rem(dp, 4)
+    y = lax.rem(dp // 4, 4)
+    xh = dp // 16
+    xl = t // 2
+    core = lax.rem(t, 2)
+    ya = y + 1 - 2 * lax.rem(y, 2)
+    za = z + 1 - 2 * lax.rem(z, 2)
+    links = [
+        (dp + (ya - y) * 4, t),
+        (dp + (za - z), t),
+        (dp + (3 - 2 * y) * 4, t),
+        (dp + (3 - 2 * z), t),
+    ]
+    bits = [lax.rem((y + 1) // 2, 2), lax.rem((z + 1) // 2, 2), y // 2, z // 2]
+    across = (dp + 16 - 32 * xh, t)
+    sibling = (dp, t + 1 - 2 * core)
+    beside = (dp, t + 2 - 4 * xl)
+    return links, bits, across, sibling, beside, xl, core
+
+
+def greet(devices):
+    barrier = pltpu.get_barrier_semaphore()
+    for d in devices:
+        pl.semaphore_signal(barrier, inc=1, device_id=d, device_id_type=MESH)
+    pl.semaphore_wait(barrier, len(devices))
+
+
+def send(src, dst, ssem, rsem, device):
+    copy = pltpu.make_async_remote_copy(
+        src_ref=src, dst_ref=dst, send_sem=ssem, recv_sem=rsem, device_id=device, device_id_type=MESH
+    )
+    copy.start()
+    return copy
+
+
+class Reduction:
+    def __init__(self, bufs, recvs, outs, ssem, rsem, links, bits, across):
+        self.bufs, self.recvs, self.outs, self.ssem, self.rsem = bufs, recvs, outs, ssem, rsem
+        self.links, self.bits, self.across = links, bits, across
+        self.base = [jnp.int32(0)] * 4
+        self.bases = []
+        self.copies = None
+
+    def start(self, step):
+        copies = []
+        for p in range(4):
+            buf, recv = self.bufs[p], self.recvs[p]
+            ss, rs = self.ssem.at[p, step], self.rsem.at[p, step]
+            if step < 3:
+                n = 4 >> step
+                bit = self.bits[(p + step) % 4]
+                there = self.base[p] + (1 - bit) * n
+                self.base[p] = self.base[p] + bit * n
+                at = (0, 4, 6)[step]
+                src, dst, dev = buf.at[pl.ds(there, n)], recv.at[pl.ds(at, n)], self.links[(p + step) % 4]
+            elif step < 5:
+                dev = self.links[(p + 3) % 4] if step == 3 else self.across
+                src, dst = buf.at[pl.ds(self.base[p], 1)], recv.at[pl.ds(4 + step, 1)]
+            else:
+                s = 7 - step
+                n = 4 >> s
+                bit = self.bits[(p + s) % 4]
+                src = dst = self.outs[p].at[pl.ds(self.base[p], n)]
+                self.base[p] = self.base[p] - bit * n
+                dev = self.links[(p + s) % 4]
+            copies.append(send(src, dst, ss, rs, dev))
+        self.copies = copies
+
+    def finish(self, step):
+        for p in range(4):
+            buf, recv = self.bufs[p], self.recvs[p]
+            into = self.outs[p] if step == 4 else buf
+            self.copies[p].wait()
+            if step < 5:
+                n = (4, 2, 1, 1, 1)[step]
+                at = (0, 4, 6, 7, 8)[step]
+                base = self.base[p]
+
+                def add(i, carry):
+                    into[base + i] = (buf[base + i].astype(F32) + recv[at + i].astype(F32)).astype(BF)
+                    return carry
+
+                lax.fori_loop(0, n, add, 0)
+
+
+def sum_kernel(gate, up, down, query, out, kv, gains, a_out, o0, o1, o2, o3, kv_out, gains_out,
+               a_buf, b0, b1, b2, b3, a_recv, r0, r1, r2, r3, kv_work, kv_recv, g_recv, a_ss, a_rs, b_ss, b_rs, k_ss, k_rs, g_ss, g_rs):
+    links, bits, across, sibling, beside, xl, core = neighbours()
+    greet(links + [across, sibling, beside])
+    first = Reduction([a_buf.at[p] for p in range(4)], [a_recv.at[p] for p in range(4)],
+                      [a_out.at[p] for p in range(4)], a_ss, a_rs, links, bits, across)
+    second = Reduction([b0, b1, b2, b3], [r0, r1, r2, r3], [o0, o1, o2, o3], b_ss, b_rs, links, bits, across)
+    gains_out[...] = gains[...]
+
+    def swap_gains(i, device):
+        return send(gains_out, g_recv.at[i], g_ss.at[i], g_rs.at[i], device)
+
+    def add_gains(i, copy):
+        copy.wait()
+        gains_out[...] = gains_out[...] + g_recv[i]
+
+    kc = send(kv.at[pl.ds((1 - core) * 2, 2)], kv_recv.at[pl.ds(0, 2)], k_ss.at[0], k_rs.at[0], sibling)
+    gc = swap_gains(0, sibling)
+    for p in range(4):
+        cols = pl.ds(128 * p, 128)
+        for c in range(8):
+            a_buf[p, c, 0:80] = gate[80 * c:80 * c + 80, cols]
+            a_buf[p, c, 80:160] = up[80 * c:80 * c + 80, cols]
+            a_buf[p, c, 160:224] = down[64 * c:64 * c + 64, cols]
+    first.start(0)
+    kc.wait()
+    for i in range(2):
+        kv_work[i] = (kv[core * 2 + i].astype(F32) + kv_recv[i].astype(F32)).astype(BF)
+    kc = send(kv_work.at[pl.ds(1 - xl, 1)], kv_recv.at[pl.ds(2, 1)], k_ss.at[1], k_rs.at[1], beside)
+    add_gains(0, gc)
+    gc = swap_gains(1, beside)
+    for c in range(8):
+        for p, b in ((0, b0), (1, b1)):
+            b[c, 0:80] = query[80 * c:80 * c + 80, 128 * p:128 * p + 128]
+            b[c, 80:112] = out[32 * c:32 * c + 32, 128 * p:128 * p + 128]
+        b2[c, 80:112] = out[32 * c:32 * c + 32, 256:384]
+        b3[c, 0:64] = down[64 * c:64 * c + 64, 512:640]
+        b3[c, 64:96] = out[32 * c:32 * c + 32, 384:512]
+        b3[c, 96:128] = out[32 * c:32 * c + 32, 512:640]
+    kc.wait()
+    mine = core * 2 + xl
+    for c in range(8):
+        b2[c, 0:80] = (kv_work[xl, 80 * c:80 * c + 80].astype(F32) + kv_recv[2, 80 * c:80 * c + 80].astype(F32)).astype(BF)
+    second.start(0)
+    add_gains(1, gc)
+    for step in range(8):
+        if step < 5:
+            gc = swap_gains(2 + step, links[step] if step < 4 else across)
+        first.finish(step)
+        if step < 7:
+            first.start(step + 1)
+        second.finish(step)
+        if step < 7:
+            second.start(step + 1)
+        if step < 5:
+            add_gains(2 + step, gc)
+    for c in range(8):
+        kv_out[mine, 80 * c:80 * c + 80] = o2[c, 0:80]
+    kc = send(kv_out.at[pl.ds(mine, 1)], kv_out.at[pl.ds(mine, 1)], k_ss.at[2], k_rs.at[2], beside)
+    kc.wait()
+    kc = send(kv_out.at[pl.ds(core * 2, 2)], kv_out.at[pl.ds(core * 2, 2)], k_ss.at[3], k_rs.at[3], sibling)
+    kc.wait()
+
+
+def unpack_kernel(a, b0, b1, b2, b3, kv, gains, query, key, value, out, gate, up, down, g0, g1, g2, g3, g4, g5):
+    for p in range(4):
+        cols = slice(128 * p, 128 * p + 128)
+        for c in range(8):
+            gate[80 * c:80 * c + 80, cols] = a[p, c, 0:80].astype(F32)
+            up[80 * c:80 * c + 80, cols] = a[p, c, 80:160].astype(F32)
+            down[64 * c:64 * c + 64, cols] = a[p, c, 160:224].astype(F32)
+    for c in range(8):
+        for p, b in ((0, b0), (1, b1)):
+            query[80 * c:80 * c + 80, 128 * p:128 * p + 128] = b[c, 0:80].astype(F32)
+            out[32 * c:32 * c + 32, 128 * p:128 * p + 128] = b[c, 80:112].astype(F32)
+        out[32 * c:32 * c + 32, 256:384] = b2[c, 80:112].astype(F32)
+        down[64 * c:64 * c + 64, 512:640] = b3[c, 0:64].astype(F32)
+        out[32 * c:32 * c + 32, 384:512] = b3[c, 64:96].astype(F32)
+        out[32 * c:32 * c + 32, 512:640] = b3[c, 96:128].astype(F32)
+    for j in range(2):
+        key[:, 128 * j:128 * j + 128] = kv[j].astype(F32)
+        value[:, 128 * j:128 * j + 128] = kv[2 + j].astype(F32)
+    for i, g in enumerate((g0, g1, g2, g3)):
+        g[...] = gains[i:i + 1, :]
+    g4[...] = gains[4:5, 0:256]
+    g5[...] = gains[4:5, 256:512]
+
+
+def sum_grads(query, key, value, out, gate, up, down, gains):
+    kv = jnp.stack([key[:, :128], key[:, 128:], value[:, :128], value[:, 128:]])
+    sds = jax.ShapeDtypeStruct
+    dma = pltpu.SemaphoreType.DMA
+    stacks = pl.pallas_call(
+        sum_kernel,
+        out_shape=(sds((4, 8, 224, 128), BF), sds((8, 112, 128), BF), sds((8, 112, 128), BF), sds((8, 112, 128), BF),
+                   sds((8, 128, 128), BF), sds((4, 640, 128), BF), sds((8, 640), F32)),
+        in_specs=[VMEM] * 7,
+        out_specs=[VMEM] * 7,
+        scratch_shapes=[
+            pltpu.VMEM((4, 8, 224, 128), BF),
+            pltpu.VMEM((8, 112, 128), BF), pltpu.VMEM((8, 112, 128), BF), pltpu.VMEM((8, 112, 128), BF),
+            pltpu.VMEM((8, 128, 128), BF),
+            pltpu.VMEM((4, 9, 224, 128), BF),
+            pltpu.VMEM((9, 112, 128), BF), pltpu.VMEM((9, 112, 128), BF), pltpu.VMEM((9, 112, 128), BF),
+            pltpu.VMEM((9, 128, 128), BF),
+            pltpu.VMEM((2, 640, 128), BF),
+            pltpu.VMEM((3, 640, 128), BF),
+            pltpu.VMEM((7, 8, 640), F32),
+            dma((4, 8)), dma((4, 8)), dma((4, 8)), dma((4, 8)), dma((4,)), dma((4,)), dma((7,)), dma((7,)),
+        ],
+        compiler_params=pltpu.CompilerParams(collective_id=7, has_side_effects=True, vmem_limit_bytes=VMEM_LIMIT),
+        name="sum_grads",
+    )(gate, up, down, query, out, kv, gains)
+    outs = pl.pallas_call(
+        unpack_kernel,
+        out_shape=(sds((640, 256), F32), sds((640, 256), F32), sds((640, 256), F32), sds((256, 640), F32),
+                   sds((640, 512), F32), sds((640, 512), F32), sds((512, 640), F32),
+                   sds((1, 640), F32), sds((1, 640), F32), sds((1, 640), F32), sds((1, 640), F32),
+                   sds((1, 256), F32), sds((1, 256), F32)),
+        in_specs=[VMEM] * 7,
+        out_specs=[VMEM] * 13,
+        compiler_params=pltpu.CompilerParams(vmem_limit_bytes=VMEM_LIMIT),
+        name="unpack_grads",
+    )(*stacks)
+    return outs
 
 WINDOW = 512
 LENGTH = 1024
@@ -302,43 +525,27 @@
     grad_attn_out = gain_term(gain_inputs[2], gain_inputs[3])
     grad_ffn_in = gain_term(gain_inputs[4], gain_inputs[5])
     grad_ffn_out = gain_term(gain_inputs[6], gain_inputs[7])
-    grad_query, grad_out, grad_gate, grad_up, grad_down = (
-        lax.psum(grad_query.astype(jnp.bfloat16), "dp").astype(jnp.float32),
-        lax.psum(grad_out.astype(jnp.bfloat16), "dp").astype(jnp.float32),
-        lax.psum(grad_gate.astype(jnp.bfloat16), "dp").astype(jnp.float32),
-        lax.psum(grad_up.astype(jnp.bfloat16), "dp").astype(jnp.float32),
-        lax.psum(grad_down.astype(jnp.bfloat16), "dp").astype(jnp.float32),
-    )
-    summed_all = lax.psum(
-        (
-            grad_key,
-            grad_value,
+    gains = jnp.stack(
+        [
             grad_attn_in,
             grad_attn_out,
             grad_ffn_in,
             grad_ffn_out,
-            grad_qnorm,
-            grad_knorm,
-        ),
-        ("dp", "tensor"),
-    )
-    return (
-        output,
-        input_grad,
-        grad_query,
-        summed_all[0],
-        summed_all[1],
-        grad_out,
-        grad_gate,
-        grad_up,
-        grad_down,
-        summed_all[2],
-        summed_all[3],
-        summed_all[4],
-        summed_all[5],
-        summed_all[6],
-        summed_all[7],
-    )
+            jnp.concatenate([grad_qnorm, grad_knorm, jnp.zeros((128,), F32)]),
+        ]
+    )
+    gains = jnp.concatenate([gains, jnp.zeros((3, 640), F32)])
+    summed = sum_grads(
+        grad_query.astype(BF),
+        grad_key.astype(BF),
+        grad_value.astype(BF),
+        grad_out.astype(BF),
+        grad_gate.astype(BF),
+        grad_up.astype(BF),
+        grad_down.astype(BF),
+        gains,
+    )
+    return (output, input_grad, *summed[:7], *(g.reshape(-1) for g in summed[7:]))
 
 
 def solution(mesh):

time: 763 us -> 348 us (0.46)
  waiting for transfers between devices: 475 us -> 69.9 us
  blocking collectives: 129 us -> 58.2 us
  Pallas kernels: 0 us -> 69.5 us
    psum x2 -> x0, waiting for transfers between devices: 395 us -> none  [the longest x1 227 us: local(): lax.psum(grad_query.astype(jnp.bfloat16), 'dp').astype(jnp.float32)]
    psum x1 -> x0, blocking collectives: 71.3 us -> none  [local(): lax.psum((grad_key, grad_value, grad_attn_in, grad_attn_out, grad_ffn_in,...]
    pallas_call x0 -> x2, Pallas kernels: none -> 69.5 us  [the longest x1 64.5 us: sum_grads(): pl.pallas_call(sum_kernel, out_shape=(sds((4, 8, 224, 128), BF), sds((8,...]
    all_to_all x2, waiting for transfers between devices: 33.7 us -> 25 us  [sum_at_owner(): tiles = lax.all_to_all(in_blocks(x, dim, size), axis, 0, 0, tiled=True)]
  transfers between devices with their start and end apart: 7 -> 5, of which waited for: 6 -> 4; matrix products, arithmetic and copies ran while one was open for 4% -> 8% of each run, Pallas kernels for 0% -> 20%
where the time goes in v1:
time: 348 us; the launch traced here: 347 us
  waiting for transfers between devices  69.9 us (20%)
  Pallas kernels  69.5 us (20%)
  blocking collectives  58.2 us (17%)
  matrix products  50.8 us (15%)
  other arithmetic  40.8 us (12%)
  local copies, waits for them, and re-layouts  22.2 us (6%)
  starting transfers between devices  20 us (6%)
  between operations  15 us (4%)
    pallas_call x1, Pallas kernels, sum_grads(): pl.pallas_call(sum_kernel, out_shape=(sds((4, 8, 224, 128), BF), sds((8,...  64.5 us
    all_to_all x2, blocking collectives, sum_at_owner(): tiles = lax.all_to_all(in_blocks(x, dim, size), axis, 0, 0, tiled=True)  38.5 us
    all_gather x1, waiting for transfers between devices, in_one_piece(): lax.all_gather(both, axis, axis=dim, tiled=True)  36.9 us
    all_to_all x2, waiting for transfers between devices, sum_at_owner(): tiles = lax.all_to_all(in_blocks(x, dim, size), axis, 0, 0, tiled=True)  25 us
    all_to_all x1, blocking collectives, copy_for_each(): return lax.all_to_all(copies, axis, split_axis=0, concat_axis=0, tiled=True)  19.7 us
    all_to_all x2, starting transfers between devices, sum_at_owner(): tiles = lax.all_to_all(in_blocks(x, dim, size), axis, 0, 0, tiled=True)  10.9 us
    all_to_all x2, starting transfers between devices, copy_for_each(): return lax.all_to_all(copies, axis, split_axis=0, concat_axis=0, tiled=True)  9.06 us
    all_to_all x2, waiting for transfers between devices, copy_for_each(): return lax.all_to_all(copies, axis, split_axis=0, concat_axis=0, tiled=True)  7.97 us
  transfers between devices with their start and end apart: 5, of which 4 were waited for; matrix products, arithmetic and copies ran while one was open for 8% of the time, Pallas kernels for 20%

profile of v1, /device:TPU:1, one launch (start us, length us, event | category | flops | bytes accessed | tf_op | source)
XLA Modules:
  0.0 346.8 jit_solution(1047468500081635357)
XLA Ops:
  9.4 1.6 multiply_reduce_fusion.1
  11.1 2.1 convolution_convert_fusion.6
  15.2 2.4 fusion.97
  17.9 2.4 fusion.91
  22.2 10.3 %while.28 = (s32[]{:T(128)}, bf16[2,1,512,256]{3,2,1,0:T(8,128)(2,1)S(1)}, f32[2,1,512]{2,1,0:T(1,128)}, s32[2,512]{1,0:T(2,128)S(1)}, s32[2,1024]{1,0:T(2,128)S...) while((s32[]{:T(128)}, ...), condition=%wide.region_6.7_spmd.clone, body=%wide.region_3.6_spmd.sunk.clone | while | flops 552075264 | bytes 8220833 | solution.py:438
  22.3 2.0 fusion.187
  25.3 1.4 fusion.189
  27.4 2.0 fusion.187
  30.5 1.4 fusion.189
  32.6 2.8 convolution_convert_fusion
  35.4 5.7 %all-to-all-start = ((bf16[4,256,640]{2,1,0:T(8,128)(2,1)}), bf16[4,256,640]{2,1,0:T(8,128)(2,1)}, u32[]{:S(2)}, u32[]{:S(2)}) async-start(bf16[4,256,640]{2,1,0:T(8,128)(2,1)} %bitcast.29), calls=%async_computation | async-start | bytes 2621440 | tf_op jit(solution)/shard_map/all_to_all | solution.py:247
  41.1 1.7 convert_element_type.135
  42.7 14.8 %all-to-all-done = bf16[4,256,640]{2,1,0:T(8,128)(2,1)} async-done(((bf16[4,256,640]{2,1,0:T(8,128)(2,1)}), bf16[4,256,640]{2,1,0:T(8,128)(2,1)}, u32[]{:S(2)}, u32[]{:S(2)}) %all-to-all-start) | async-done | bytes 1310752 | tf_op jit(solution)/shard_map/all_to_all | solution.py:247
  57.6 1.6 convert_reduce_fusion.3
  59.3 1.4 multiply_reduce_fusion.14
  61.0 19.7 %all_to_all.35 = bf16[4,256,640]{2,1,0:T(8,128)(2,1)S(1)} all-to-all(bf16[4,256,640]{2,1,0:T(8,128)(2,1)S(1)} %broadcast_in_dim.61), channel_id=1, replica_groups=mesh['dp'=32,'tensor'=4] {'tensor'}, dimensions={0} | all-to-all | bytes 2621440 | tf_op jit(solution)/shard_map/all_to_all | solution.py:259
  82.2 2.6 multiply_convert_fusion.3
  85.9 19.8 %all_to_all.36 = bf16[4,256,640]{2,1,0:T(8,128)(2,1)S(1)} all-to-all(bf16[4,256,640]{2,1,0:T(8,128)(2,1)S(1)} %bitcast.234), channel_id=1, replica_groups=mesh['dp'=32,'tensor'=4] {'tensor'}, dimensions={0} | all-to-all | bytes 2621440 | tf_op jit(solution)/shard_map/all_to_all | solution.py:247
  107.6 36.9 %all-gather.2.cloned.1.call-done = bf16[1024,1280]{1,0:T(8,128)(2,1)} async-done(((bf16[256,1280]{1,0:T(8,128)(2,1)}), bf16[1024,1280]{1,0:T(8,128)(2,1)}) %all-gather.2.cloned.1.call-update) | async-done | bytes 2621456 | tf_op jit(solution)/shard_map/all_gather | solution.py:268
  144.4 5.0 %multiply_convert_fusion.2 = (bf16[1024,512]{1,0:T(8,128)(2,1)S(1)}, bf16[1024,512]{1,0:T(8,128)(2,1)S(1)}) fusion(f32[1024,512]{1,0:T(8,128)} %copy-done.70, f32[1024,512]{1,0:T(8,128)} %get-tuple-element.252, bf16[512,640]{1,0:T(8,128)(2,1)S(1)} %copy-done, bf16[1024,1280]{1,0:T(8,128)(2,1)} %all-gather.2.cloned.1.call-done), kind=kOutput, calls=%fused_computation.86 | convolution fusion | flops 683671552 | bytes 8257536 | tf_op jit(solution)/shard_map/rd,fd->rf/dot_general | solution.py:468
  152.1 18.6 %all_to_all.37 = bf16[4,256,640]{2,1,0:T(8,128)(2,1)S(1)} all-to-all(bf16[4,256,640]{2,1,0:T(8,128)(2,1)S(1)} %bitcast.218), channel_id=1, replica_groups=mesh['dp'=32,'tensor'=4] {'tensor'}, dimensions={0} | all-to-all | bytes 2621440 | tf_op jit(solution)/shard_map/all_to_all | solution.py:247
  171.8 2.0 multiply_reduce_fusion.7
  175.8 4.5 %all-to-all-start.4 = ((bf16[4,256,640]{2,1,0:T(8,128)(2,1)}), bf16[4,256,640]{2,1,0:T(8,128)(2,1)S(1)}, u32[]{:S(2)}, u32[]{:S(2)}) async-start(bf16[4,256,640]{2,1,0:T(8,128)(2,1)} %broadcast_in_dim.65), calls=%async_computation.4 | async-start | bytes 2621440 | tf_op jit(solution)/shard_map/all_to_all | solution.py:259
  181.5 2.5 slice.78
  184.0 3.0 convolution_convert_fusion.3.up
  187.1 1.7 convolution_convert_fusion.4.gate
  188.8 8.0 %all-to-all-done.4 = bf16[4,256,640]{2,1,0:T(8,128)(2,1)S(1)} async-done(((bf16[4,256,640]{2,1,0:T(8,128)(2,1)}), bf16[4,256,640]{2,1,0:T(8,128)(2,1)S(1)}, u32[]{:S(2)}, u32[]{:S(2)}) %all-to-all-start.4) | async-done | bytes 1310752 | tf_op jit(solution)/shard_map/all_to_all | solution.py:259
  196.8 1.8 convolution_convert_fusion.5
  198.6 14.4 %while.29 = (s32[]{:T(128)}, f32[2,1,512,256]{3,2,1,0:T(8,128)}, f32[2,1024,256]{2,1,0:T(8,128)}, f32[2,1024,256]{2,1,0:T(8,128)}, s32[2,512]{1,0:T(2,128)S(1)},...) while((s32[]{:T(128)}, f32[2,1,512,256]{3,2,1,0:T(8,128)}, ...), condition=%wide.region_18.19_spmd.clone, body=%wide.region_16.18_spmd.sunk.clone | while | flops 1349910528 | bytes 50369804 | solution.py:489
  201.2 1.3 copy-done.20
  204.3 1.6 fusion.200
  208.5 1.3 copy-done.20
  211.5 1.5 fusion.200
  213.0 3.8 %fusion.94 = (f32[1,1024,128]{2,1,0:T(8,128)S(1)}, f32[1,1024,128]{2,1,0:T(8,128)S(1)}) fusion(f32[1,1024,256]{2,1,0:T(8,128)} %bitcast.239, f32[128]{0:T(128)S(1)} %copy-done.67, f32[1024]{0:T(1024)S(1)} %convert_element_type.137), kind=kLoop, calls=%fused_computation.183 | loop fusion | flops 1048576 | bytes 2101760 | tf_op jit(solution)/shard_map/transpose(jvp())/add_any | solution.py:299
  219.7 1.4 slice_add_fusion.1
  221.2 2.3 fusion.100
  226.4 1.7 add_convert_fusion
  228.1 5.3 %all-to-all-start.5 = ((bf16[4,256,640]{2,1,0:T(8,128)(2,1)}), bf16[4,256,640]{2,1,0:T(8,128)(2,1)}, u32[]{:S(2)}, u32[]{:S(2)}) async-start(bf16[4,256,640]{2,1,0:T(8,128)(2,1)} %bitcast.44), calls=%async_computation.5 | async-start | bytes 2621440 | tf_op jit(solution)/shard_map/all_to_all | solution.py:247
  233.4 3.3 convolution_convert_fusion.2.down
  238.2 1.5 convolution_convert_fusion.8
  239.7 10.2 %all-to-all-done.5 = bf16[4,256,640]{2,1,0:T(8,128)(2,1)} async-done(((bf16[4,256,640]{2,1,0:T(8,128)(2,1)}), bf16[4,256,640]{2,1,0:T(8,128)(2,1)}, u32[]{:S(2)}, u32[]{:S(2)}) %all-to-all-start.5) | async-done | bytes 1310752 | tf_op jit(solution)/shard_map/all_to_all | solution.py:247
  249.9 1.6 convert_reduce_fusion
  253.2 4.5 %all-to-all-start.6 = ((bf16[4,256,640]{2,1,0:T(8,128)(2,1)}), bf16[4,256,640]{2,1,0:T(8,128)(2,1)S(1)}, u32[]{:S(2)}, u32[]{:S(2)}) async-start(bf16[4,256,640]{2,1,0:T(8,128)(2,1)} %broadcast_in_dim.107), calls=%async_computation.6 | async-start | bytes 2621440 | tf_op jit(solution)/shard_map/all_to_all | solution.py:259
  258.9 1.8 pad_maximum_fusion.1.kv
  260.7 1.3 convolution_convert_fusion.9.out
  262.0 1.5 convolution_convert_fusion.10.query
  264.2 64.5 %sum_grads.1 = (bf16[4,8,224,128]{3,2,1,0:T(8,128)(2,1)}, bf16[8,112,128]{2,1,0:T(8,128)(2,1)}, bf16[8,112,128]{2,1,0:T(8,128)(2,1)}, bf16[8,112,128]{2,1,0:T(8,...) custom-call(bf16[640,512]{1,0:T(8,128)(2,1)} %convolution_convert_fusion.4.gate, ...), custom_call_target="tpu_custom_call" | custom-call | tf_op jit(solution)/shard_map/sum_grads/pallas_call | solution.py:197
  328.7 5.0 %unpack_grads.1 = (f32[640,256]{1,0:T(8,128)}, f32[640,256]{1,0:T(8,128)}, f32[640,256]{1,0:T(8,128)}, f32[256,640]{1,0:T(8,128)}, f32[640,512]{1,0:T(8,128)}, /...) custom-call(bf16[4,8,224,128]{3,2,1,0:T(8,128)(2,1)} %get-tuple-elem, ...), custom_call_target="tpu_custom_call" | custom-call | tf_op jit(solution)/shard_map/unpack_grads/pallas_call | solution.py:218
  (268 shorter events, 46.6 us)
Async XLA Ops:
  7.2 77.7 %copy-start = (bf16[512,640]{1,0:T(8,128)(2,1)S(1)}, bf16[512,640]{1,0:T(8,128)(2,1)}, u32[]{:S(2)}) copy-start(bf16[512,640]{1,0:T(8,128)(2,1)} %param.31) | copy-start | bytes 1966084
  7.2 10.6 %copy-start.66 = (f32[128]{0:T(128)}, f32[128]{0:T(128)S(1)}, u32[]{:S(2)}) copy-start(f32[128]{0:T(128)S(1)} %multiply_power_fusion) | copy-start | bytes 1540
  11.1 3.0 copy-start.68
  14.9 2.7 copy-start.56
  14.9 2.9 copy-start.4
  32.6 2.8 copy-start.14
  35.4 22.2 %all-to-all-start = ((bf16[4,256,640]{2,1,0:T(8,128)(2,1)}), bf16[4,256,640]{2,1,0:T(8,128)(2,1)}, u32[]{:S(2)}, u32[]{:S(2)}) async-start(bf16[4,256,640]{2,1,0:T(8,128)(2,1)} %bitcast.29), calls=%async_computation | async-start | bytes 2621440 | tf_op jit(solution)/shard_map/all_to_all | solution.py:247
  41.1 103.4 %all-gather.2.cloned.1.call-start = ((), (), s32[]{:S(2)}) async-start(), calls=%async_computation.7 | async-start | bytes 3276800 | tf_op jit(solution)/shard_map/all_gather | solution.py:268
  42.7 16.5 %copy-start.45 = (f32[640]{0:T(1024)S(1)}, f32[640]{0:T(1024)}, u32[]{:S(2)}) copy-start(f32[640]{0:T(1024)} %param.33) | copy-start | bytes 7684
  42.7 18.0 %copy-start.44 = (f32[640]{0:T(1024)S(1)}, f32[640]{0:T(1024)}, u32[]{:S(2)}) copy-start(f32[640]{0:T(1024)} %param.34) | copy-start | bytes 7684
  60.7 119.7 %copy-start.64 = (f32[256]{0:T(256)}, f32[256]{0:T(256)S(1)}, u32[]{:S(2)}) copy-start(f32[256]{0:T(256)S(1)} %get-tuple-element.232) | copy-start | bytes 3076
  60.9 19.8 %copy-start.30 = (bf16[640,512]{1,0:T(8,128)(2,1)S(1)}, bf16[640,512]{1,0:T(8,128)(2,1)}, u32[]{:S(2)}) copy-start(bf16[640,512]{1,0:T(8,128)(2,1)} %param.29) | copy-start | bytes 1966084
  84.9 20.9 %copy-start.71 = (bf16[1024,512]{1,0:T(8,128)(2,1)}, bf16[1024,512]{1,0:T(8,128)(2,1)S(1)}, u32[]{:S(2)}) copy-start(bf16[1024,512]{1,0:T(8,128)(2,1)S(1)} %get-tuple-element.251) | copy-start | bytes 3145732
  85.8 20.2 %copy-start.29 = (bf16[1024,640]{1,0:T(8,128)(2,1)S(1)}, bf16[1024,640]{1,0:T(8,128)(2,1)}, u32[]{:S(2)}) copy-start(bf16[1024,640]{1,0:T(8,128)(2,1)} %param.24) | copy-start | bytes 3932164
  85.9 20.2 %copy-start.49 = (f32[640]{0:T(1024)S(1)}, f32[640]{0:T(1024)}, u32[]{:S(2)}) copy-start(f32[640]{0:T(1024)} %param.35) | copy-start | bytes 7684
  144.4 5.1 %copy-start.31 = (bf16[640,512]{1,0:T(8,128)(2,1)S(1)}, bf16[640,512]{1,0:T(8,128)(2,1)}, u32[]{:S(2)}) copy-start(bf16[640,512]{1,0:T(8,128)(2,1)} %param.29) | copy-start | bytes 1966084
  175.8 21.0 %all-to-all-start.4 = ((bf16[4,256,640]{2,1,0:T(8,128)(2,1)}), bf16[4,256,640]{2,1,0:T(8,128)(2,1)S(1)}, u32[]{:S(2)}, u32[]{:S(2)}) async-start(bf16[4,256,640]{2,1,0:T(8,128)(2,1)} %broadcast_in_dim.65), calls=%async_computation.4 | async-start | bytes 2621440 | tf_op jit(solution)/shard_map/all_to_all | solution.py:259
  180.4 3.7 %copy-start.19 = (bf16[4,256,640]{2,1,0:T(8,128)(2,1)S(1)}, bf16[4,256,640]{2,1,0:T(8,128)(2,1)}, u32[]{:S(2)}) copy-start(bf16[4,256,640]{2,1,0:T(8,128)(2,1)} %copy-done.18) | copy-start | bytes 3932164
  184.0 3.0 copy-start.27
  188.8 9.8 %copy-start.34 = (bf16[2,1,512,256]{3,2,1,0:T(8,128)(2,1)S(1)}, bf16[2,1,512,256]{3,2,1,0:T(8,128)(2,1)}, u32[]{:S(2)}) copy-start(bf16[2,1,512,256]{3,2,1,0:T(8,128)(2,1)} %get-tuple-element.520) | copy-start | bytes 1572868
  188.8 9.8 %copy-start.48 = (f32[2,1,512]{2,1,0:T(1,128)S(1)}, f32[2,1,512]{2,1,0:T(1,128)}, u32[]{:S(2)}) copy-start(f32[2,1,512]{2,1,0:T(1,128)} %get-tuple-element.457) | copy-start | bytes 12292
  198.6 14.5 %copy-start.67 = (f32[128]{0:T(128)S(1)}, f32[128]{0:T(128)}, u32[]{:S(2)}) copy-start(f32[128]{0:T(128)} %copy-done.66) | copy-start | bytes 1540
  213.0 3.8 %copy-start.5 = (f32[1024,256]{1,0:T(8,128)S(1)}, f32[1024,256]{1,0:T(8,128)}, u32[]{:S(2)}) copy-start(f32[1024,256]{1,0:T(8,128)} %copy-done.4) | copy-start | bytes 3145732
  213.0 3.9 %copy-start.43 = (f32[1024]{0:T(1024)S(1)}, f32[1024]{0:T(1024)}, u32[]{:S(2)}) copy-start(f32[1024]{0:T(1024)} %copy-done.42) | copy-start | bytes 12292
  213.0 3.9 %copy-start.60 = (f32[256]{0:T(256)S(1)}, f32[256]{0:T(256)}, u32[]{:S(2)}) copy-start(f32[256]{0:T(256)} %param.36) | copy-start | bytes 3076
  213.0 4.3 %copy-start.57 = (f32[1024]{0:T(1024)S(1)}, f32[1024]{0:T(1024)}, u32[]{:S(2)}) copy-start(f32[1024]{0:T(1024)} %copy-done.56) | copy-start | bytes 12292
  217.7 7.4 %copy-start.12 = (bf16[1024,256]{1,0:T(8,128)(2,1)}, bf16[1024,256]{1,0:T(8,128)(2,1)S(1)}, u32[]{:S(2)}) copy-start(bf16[1024,256]{1,0:T(8,128)(2,1)S(1)} %fusion.103) | copy-start | bytes 1572868
  219.7 3.8 %copy-start.3 = (f32[1024,256]{1,0:T(8,128)S(1)}, f32[1024,256]{1,0:T(8,128)}, u32[]{:S(2)}) copy-start(f32[1024,256]{1,0:T(8,128)} %copy-done.2) | copy-start | bytes 3145732
  219.7 3.8 %copy-start.41 = (f32[1024]{0:T(1024)S(1)}, f32[1024]{0:T(1024)}, u32[]{:S(2)}) copy-start(f32[1024]{0:T(1024)} %copy-done.40) | copy-start | bytes 12292
  219.7 3.8 %copy-start.62 = (f32[256]{0:T(256)S(1)}, f32[256]{0:T(256)}, u32[]{:S(2)}) copy-start(f32[256]{0:T(256)} %param.37) | copy-start | bytes 3076
  221.2 2.8 copy-start.55
  228.1 5.3 %copy-start.72 = (bf16[1024,512]{1,0:T(8,128)(2,1)S(1)}, bf16[1024,512]{1,0:T(8,128)(2,1)}, u32[]{:S(2)}) copy-start(bf16[1024,512]{1,0:T(8,128)(2,1)} %copy-done.71) | copy-start | bytes 3145732
  228.1 21.8 %all-to-all-start.5 = ((bf16[4,256,640]{2,1,0:T(8,128)(2,1)}), bf16[4,256,640]{2,1,0:T(8,128)(2,1)}, u32[]{:S(2)}, u32[]{:S(2)}) async-start(bf16[4,256,640]{2,1,0:T(8,128)(2,1)} %bitcast.44), calls=%async_computation.5 | async-start | bytes 2621440 | tf_op jit(solution)/shard_map/all_to_all | solution.py:247
  233.4 3.3 copy-start.52
  233.4 3.3 copy-start.53
  233.4 3.3 copy-start.10
  233.4 3.3 copy-start.51
  233.4 3.3 copy-start.69
  238.2 13.3 %copy-start.6 = (f32[1024,640]{1,0:T(8,128)S(1)}, f32[1024,640]{1,0:T(8,128)}, u32[]{:S(2)}) copy-start(f32[1024,640]{1,0:T(8,128)} %convert_element_type.135) | copy-start | bytes 7864324
  238.2 13.3 %copy-start.63 = (f32[256]{0:T(256)S(1)}, f32[256]{0:T(256)}, u32[]{:S(2)}) copy-start(f32[256]{0:T(256)} %fusion.111) | copy-start | bytes 3076
  239.7 12.1 %copy-start.65 = (f32[256]{0:T(256)S(1)}, f32[256]{0:T(256)}, u32[]{:S(2)}) copy-start(f32[256]{0:T(256)} %copy-done.64) | copy-start | bytes 3076
  239.7 12.1 %copy-start.8 = (f32[256,640]{1,0:T(8,128)S(1)}, f32[256,640]{1,0:T(8,128)}, u32[]{:S(2)}) copy-start(f32[256,640]{1,0:T(8,128)} %copy-done.7) | copy-start | bytes 1966084
  253.2 7.6 %copy-start.15 = (bf16[2,1,512,256]{3,2,1,0:T(8,128)(2,1)S(1)}, bf16[2,1,512,256]{3,2,1,0:T(8,128)(2,1)}, u32[]{:S(2)}) copy-start(bf16[2,1,512,256]{3,2,1,0:T(8,128)(2,1)} %copy-done.14) | copy-start | bytes 1572868
  253.2 7.6 %copy-start.17 = (bf16[4,256,640]{2,1,0:T(8,128)(2,1)S(1)}, bf16[4,256,640]{2,1,0:T(8,128)(2,1)}, u32[]{:S(2)}) copy-start(bf16[4,256,640]{2,1,0:T(8,128)(2,1)} %copy-done.16) | copy-start | bytes 3932164
  253.2 85.7 %all-to-all-start.6 = ((bf16[4,256,640]{2,1,0:T(8,128)(2,1)}), bf16[4,256,640]{2,1,0:T(8,128)(2,1)S(1)}, u32[]{:S(2)}, u32[]{:S(2)}) async-start(bf16[4,256,640]{2,1,0:T(8,128)(2,1)} %broadcast_in_dim.107), calls=%async_computation.6 | async-start | bytes 2621440 | tf_op jit(solution)/shard_map/all_to_all | solution.py:259
  257.7 4.3 %copy-start.11 = (bf16[1024,640]{1,0:T(8,128)(2,1)S(1)}, bf16[1024,640]{1,0:T(8,128)(2,1)}, u32[]{:S(2)}) copy-start(bf16[1024,640]{1,0:T(8,128)(2,1)} %param.21) | copy-start | bytes 3932164
  257.7 4.3 %copy-start.13 = (bf16[1024,256]{1,0:T(8,128)(2,1)S(1)}, bf16[1024,256]{1,0:T(8,128)(2,1)}, u32[]{:S(2)}) copy-start(bf16[1024,256]{1,0:T(8,128)(2,1)} %copy-done.12) | copy-start | bytes 1572868
  328.7 11.2 %copy-start.1 = (bf16[512,640]{1,0:T(8,128)(2,1)S(1)}, bf16[512,640]{1,0:T(8,128)(2,1)}, u32[]{:S(2)}) copy-start(bf16[512,640]{1,0:T(8,128)(2,1)} %param.31) | copy-start | bytes 1966084
  (37 other events, 54.5 us)
Sparse Core Ops, SparseCore 0:
  107.7 36.6 all-gather.1

commit v2 on v1

--- a/solution.py
+++ b/solution.py
@@ -237,6 +237,223 @@
 NEG_LARGE = -1e30
 
 
+NC = 4
+CR = 1024 // NC
+OW = CR // 4
+C0 = 0.7978845608028654
+C1 = 0.044715
+
+
+def nt(a, b):
+    return lax.dot_general(a, b, (((1,), (1,)), ((), ())), preferred_element_type=F32)
+
+
+def tn(a, b):
+    return lax.dot_general(a, b, (((0,), (0,)), ((), ())), preferred_element_type=F32)
+
+
+def nn(a, b):
+    return jnp.dot(a, b, preferred_element_type=F32)
+
+
+def inv_rms(v):
+    return lax.rsqrt(jnp.mean(v * v, axis=-1, keepdims=True) + EPSILON)
+
+
+def rms_back(v, r, du):
+    return r * du - v * (r * r * r * jnp.mean(du * v, axis=-1, keepdims=True))
+
+
+class Tensor:
+    def __init__(self, sibling, beside, xl, core, ssem, rsem):
+        self.sibling, self.beside, self.xl, self.core = sibling, beside, xl, core
+        self.own = core * 2 + xl
+        self.ssem, self.rsem = ssem, rsem
+        self.used = 0
+
+    def send(self, src, dst, device):
+        i = self.used
+        self.used += 1
+        return send(src, dst, self.ssem.at[i], self.rsem.at[i], device)
+
+    def sum_a(self, part, recv):
+        return self.send(part.at[pl.ds((1 - self.core) * 2, 2)], recv, self.sibling)
+
+    def sum_b(self, copy, part, recv, out, recv2):
+        copy.wait()
+        there = self.core * 2 + 1 - self.xl
+        out[...] = (part[there].astype(F32) + recv[1 - self.xl].astype(F32)).astype(BF)
+        return self.send(out, recv2, self.beside)
+
+    def sum_c(self, copy, part, recv, recv2):
+        copy.wait()
+        return part[self.own].astype(F32) + recv[self.xl].astype(F32) + recv2[...].astype(F32)
+
+    def gather_a(self, buf):
+        block = buf.at[self.own]
+        return self.send(block, block, self.beside), self.send(block, block, self.sibling)
+
+    def gather_b(self, copies, buf):
+        copies[0].wait()
+        block = buf.at[self.core * 2 + 1 - self.xl]
+        return copies[1], self.send(block, block, self.sibling)
+
+    def gather_c(self, copies):
+        for c in copies:
+            c.wait()
+
+
+def ffn_kernel(attn, x, cot, wg, wu, wd, g_ao, g_fi, g_fo,
+               output, dattn, dmid_out, grad_gate, grad_up, grad_down, gains,
+               ffn_g, dffn_g, hid, act_a, act_b, dgate, dup, part2, part3, attn_own, mid_own,
+               recv_a, recv_b, sent_b, ssem, rsem):
+    _, _, _, sibling, beside, xl, core = neighbours()
+    greet([sibling, beside])
+    t = Tensor(sibling, beside, xl, core, ssem, rsem)
+    own = t.own
+    state = [dict() for _ in range(NC)]
+    for i in range(3):
+        state[0]["g%d" % i] = None
+
+    def rs_a(e, part):
+        def run(c):
+            state[c]["a"] = t.sum_a(part.at[c], recv_a.at[e, c])
+        return run
+
+    def rs_b(e, part):
+        def run(c):
+            state[c]["b"] = t.sum_b(state[c]["a"], part.at[c], recv_a.at[e, c], sent_b.at[e, c], recv_b.at[e, c])
+        return run
+
+    def rs_c(e, part, c):
+        return t.sum_c(state[c]["b"], part.at[c], recv_a.at[e, c], recv_b.at[e, c])
+
+    def mid_stage(c):
+        a = rs_c(0, attn, c)
+        attn_own[c] = a
+        mid = x[c, own].astype(F32) + a * inv_rms(a) * g_ao[...]
+        mid_own[c] = mid
+        ffn_g[c, own] = (mid * inv_rms(mid) * g_fi[...]).astype(BF)
+        state[c]["g"] = t.gather_a(ffn_g.at[c])
+
+    def forward(buf, key):
+        def run(c):
+            state[c][key] = t.gather_b(state[c][key], buf.at[c])
+        return run
+
+    def up_stage(c):
+        t.gather_c(state[c]["g"])
+        f = ffn_g[c].reshape(CR, 640)
+        gate = nn(f, wg[...])
+        up = nn(f, wu[...])
+        th = jnp.tanh(C0 * (gate + C1 * gate * gate * gate))
+        half = 0.5 * (1.0 + th)
+        act = gate * half
+        slope = half + 0.5 * gate * (1.0 - th * th) * (C0 * (1.0 + 3.0 * C1 * gate * gate))
+        act_a[c] = up * slope
+        act_b[c] = act
+        h = (act * up).astype(BF)
+        hid[c] = h
+        part2[c] = nn(h, wd[...]).astype(BF).reshape(4, OW, 640)
+        rs_a(1, part2)(c)
+
+    def out_stage(c):
+        s = rs_c(1, part2, c)
+        r = inv_rms(s)
+        ct = cot[c, own].astype(F32)
+        dffn_g[c, own] = rms_back(s, r, ct * g_fo[...]).astype(BF)
+        state[c]["g"] = t.gather_a(dffn_g.at[c])
+        output[c, own] = (mid_own[c] + s * r * g_fo[...]).astype(BF)
+        state[c]["o"] = t.gather_a(output.at[c])
+        gains[2:3, :] = gains[2:3, :] + jnp.sum(ct * s * r, axis=0, keepdims=True)
+
+    def down_stage(c):
+        t.gather_c(state[c]["g"])
+        d = dffn_g[c].reshape(CR, 640)
+        dh = nt(d, wd[...])
+        dg = (dh * act_a[c]).astype(BF)
+        du = (dh * act_b[c]).astype(BF)
+        dgate[c] = dg
+        dup[c] = du
+        part3[c] = (nt(dg, wg[...]) + nt(du, wu[...])).astype(BF).reshape(4, OW, 640)
+        rs_a(2, part3)(c)
+
+    def attn_stage(c):
+        d = rs_c(2, part3, c)
+        mid, a = mid_own[c], attn_own[c]
+        r = inv_rms(mid)
+        gains[1:2, :] = gains[1:2, :] + jnp.sum(d * mid * r, axis=0, keepdims=True)
+        dmid = cot[c, own].astype(F32) + rms_back(mid, r, d * g_fi[...])
+        dmid_out[c] = dmid
+        r = inv_rms(a)
+        gains[0:1, :] = gains[0:1, :] + jnp.sum(dmid * a * r, axis=0, keepdims=True)
+        dattn[c, own] = rms_back(a, r, dmid * g_ao[...]).astype(BF)
+        state[c]["g"] = t.gather_a(dattn.at[c])
+
+    def last(c):
+        t.gather_c(state[c]["o"])
+        t.gather_c(state[c]["g"])
+
+    def weights_down():
+        grad_down[...] = tn(hid[...].reshape(1024, 512), dffn_g[...].reshape(1024, 640)).astype(BF)
+
+    def weights_gate():
+        grad_gate[...] = tn(ffn_g[...].reshape(1024, 640), dgate[...].reshape(1024, 512)).astype(BF)
+
+    def weights_up():
+        grad_up[...] = tn(ffn_g[...].reshape(1024, 640), dup[...].reshape(1024, 512)).astype(BF)
+
+    gains[...] = jnp.zeros_like(gains)
+    stages = [
+        rs_a(0, attn), rs_b(0, attn), mid_stage, forward(ffn_g, "g"), up_stage,
+        rs_b(1, part2), out_stage, forward(dffn_g, "g"), down_stage,
+        rs_b(2, part3), forward(output, "o"), attn_stage, forward(dattn, "g"), last,
+    ]
+    work = sorted(((s + SKEW * c, s, c) for s in range(len(stages)) for c in range(NC)), key=lambda w: (w[0], w[2]))
+    end = len(stages) - 1 + SKEW * (NC - 1)
+    fill = {(9, NC - 1): weights_down, (11, NC - 1): weights_gate, (12, NC - 1): weights_up}
+    for _, s, c in work:
+        if s == 9 and c == NC - 1:
+            stages[s](c)
+            weights_down()
+        elif s == 11 and c == NC - 1:
+            stages[s](c)
+            weights_gate()
+        elif s == 12 and c == NC - 1:
+            stages[s](c)
+            weights_up()
+        else:
+            stages[s](c)
+
+
+SKEW = 1
+
+
+def ffn_block(attn_term, x, cot, wg, wu, wd, g_ao, g_fi, g_fo):
+    sds = jax.ShapeDtypeStruct
+    dma = pltpu.SemaphoreType.DMA
+    blocks = (NC, 4, OW, 640)
+    count = NC * (3 * 2 + 4 * 3)
+    v = pltpu.VMEM
+    outs = pl.pallas_call(
+        ffn_kernel,
+        out_shape=(sds(blocks, BF), sds(blocks, BF), sds((NC, OW, 640), F32), sds((640, 512), BF), sds((640, 512), BF),
+                   sds((512, 640), BF), sds((8, 640), F32)),
+        in_specs=[VMEM] * 9,
+        out_specs=[VMEM] * 7,
+        scratch_shapes=[
+            v(blocks, BF), v(blocks, BF), v((NC, CR, 512), BF), v((NC, CR, 512), F32), v((NC, CR, 512), F32),
+            v((NC, CR, 512), BF), v((NC, CR, 512), BF), v(blocks, BF), v(blocks, BF), v((NC, OW, 640), F32),
+            v((NC, OW, 640), F32), v((3, NC, 2, OW, 640), BF), v((3, NC, OW, 640), BF), v((3, NC, OW, 640), BF),
+            dma((count,)), dma((count,)),
+        ],
+        compiler_params=pltpu.CompilerParams(collective_id=3, has_side_effects=True, vmem_limit_bytes=VMEM_LIMIT),
+        name="ffn_block",
+    )(attn_term.reshape(blocks), x.reshape(blocks), cot.reshape(blocks), wg, wu, wd,
+      g_ao.reshape(1, 640), g_fi.reshape(1, 640), g_fo.reshape(1, 640))
+    return outs
+
+
 def in_blocks(x, dim, size):
     before, after = (x.shape[:dim], x.shape[dim + 1 :])
     return jnp.moveaxis(x.reshape(*before, size, -1, *after), dim, 0)
@@ -398,12 +615,6 @@
     blocks_per = LENGTH // WINDOW
     block_total = seqs_here * blocks_per
     score_scale = 1.0 / math.sqrt(head_size)
-    share_rows = row_count // lax.axis_size("tensor")
-    first_row = lax.axis_index("tensor") * share_rows
-
-    def my_rows(values):
-        return lax.dynamic_slice_in_dim(values, first_row, share_rows, 0)
-
     whole_x = inputs.astype(jnp.float32)
     normed = rms_scale(whole_x, g_attn_in).astype(jnp.bfloat16)
     query_raw = jnp.dot(normed, w_query, preferred_element_type=jnp.float32)
@@ -444,41 +655,13 @@
         .reshape(row_count, heads_here * head_size)
     )
     attn_term = jnp.dot(heads_low, w_out, preferred_element_type=jnp.float32)
-    attn_sum = sum_at_owner(attn_term.astype(jnp.bfloat16), "tensor", 0)
-    x_rows = my_rows(whole_x)
-    attn_norm, attn_pull = jax.vjp(lambda values: rms_scale(values, g_attn_out), attn_sum)
-    mid_rows = x_rows + attn_norm
-    ffn_in, ffn_pull = jax.vjp(lambda values: rms_scale(values, g_ffn_in), mid_rows)
-    ffn_low = collect(ffn_in.astype(jnp.bfloat16), "tensor", 0)
-    gate_raw = jnp.dot(ffn_low, w_gate, preferred_element_type=jnp.float32)
-    up_raw = jnp.dot(ffn_low, w_up, preferred_element_type=jnp.float32)
-    hidden_full, act_pull = jax.vjp(
-        lambda gate_in, up_in: jax.nn.gelu(gate_in, approximate=True) * up_in, gate_raw, up_raw
-    )
-    hidden = hidden_full.astype(jnp.bfloat16)
-    ffn_term = jnp.dot(hidden, w_down, preferred_element_type=jnp.float32)
-    ffn_sum = sum_at_owner(ffn_term.astype(jnp.bfloat16), "tensor", 0)
-    cot_rows = my_rows(cotangent).astype(jnp.float32)
-    out_norm, out_pull = jax.vjp(lambda values: rms_scale(values, g_ffn_out), ffn_sum)
-    result = mid_rows + out_norm
-    grad_ffn = out_pull(cot_rows)[0]
-    output, grad_ffn_low = in_one_piece(
-        (result.astype(jnp.bfloat16), grad_ffn.astype(jnp.bfloat16)), "tensor", 0, 1
-    )
-    grad_hidden = jnp.einsum("rd,fd->rf", grad_ffn_low, w_down, preferred_element_type=jnp.float32)
-    grad_down = jnp.einsum("rf,rd->fd", hidden, grad_ffn_low, preferred_element_type=jnp.float32)
-    grad_gate_full, grad_up_full = act_pull(grad_hidden)
-    grad_gate_low = grad_gate_full.astype(jnp.bfloat16)
-    grad_up_low = grad_up_full.astype(jnp.bfloat16)
-    grad_gate = jnp.einsum("rd,rf->df", ffn_low, grad_gate_low, preferred_element_type=jnp.float32)
-    grad_up = jnp.einsum("rd,rf->df", ffn_low, grad_up_low, preferred_element_type=jnp.float32)
-    ffn_in_term = jnp.einsum(
-        "rf,df->rd", grad_gate_low, w_gate, preferred_element_type=jnp.float32
-    ) + jnp.einsum("rf,df->rd", grad_up_low, w_up, preferred_element_type=jnp.float32)
-    ffn_in_grad = sum_at_owner(ffn_in_term.astype(jnp.bfloat16), "tensor", 0)
-    grad_mid = cot_rows + ffn_pull(ffn_in_grad)[0]
-    grad_attn = attn_pull(grad_mid)[0]
-    grad_attn_low = collect(grad_attn.astype(jnp.bfloat16), "tensor", 0)
+    output, grad_attn_low, grad_mid, grad_gate, grad_up, grad_down, ffn_gains = ffn_block(
+        attn_term.astype(BF), inputs, cotangent, w_gate, w_up, w_down, g_attn_out, g_ffn_in, g_ffn_out
+    )
+    output = output.reshape(row_count, -1)
+    grad_attn_low = grad_attn_low.reshape(row_count, -1)
+    t_index = lax.axis_index("tensor")
+    owner = lax.rem(t_index, 2) * 2 + t_index // 2
     grad_out = jnp.einsum("rh,rd->hd", heads_low, grad_attn_low, preferred_element_type=jnp.float32)
     grad_heads = jnp.einsum(
         "rd,hd->rh", grad_attn_low, w_out, preferred_element_type=jnp.float32
@@ -516,33 +699,32 @@
     input_term = input_term + jnp.einsum(
         "rh,dh->rd", grad_v_low, w_value, preferred_element_type=jnp.float32
     )
-    input_sum = sum_at_owner(input_term.astype(jnp.bfloat16), "tensor", 0)
+    owned = lambda v: lax.dynamic_index_in_dim(v.reshape(NC, 4, OW, 640), owner, 1, False).reshape(256, 640)
+    term = input_term.astype(jnp.bfloat16).reshape(NC, 4, OW, 640)
+    term = term.transpose(1, 0, 2, 3).reshape(2, 2, 256, 640).transpose(1, 0, 2, 3).reshape(1024, 640)
+    input_sum = sum_at_owner(term, "tensor", 0)
+    x_rows = owned(whole_x)
     x_grad_norm = jax.vjp(lambda values: rms_scale(values, g_attn_in), x_rows)[1](input_sum)[0]
-    grad_rows = grad_mid + x_grad_norm
-    gain_inputs = (x_rows, input_sum, attn_sum, grad_mid, mid_rows, ffn_in_grad, ffn_sum, cot_rows)
+    grad_rows = grad_mid.reshape(256, 640) + x_grad_norm
     input_grad = collect(grad_rows.astype(jnp.bfloat16), "tensor", 0)
-    grad_attn_in = gain_term(gain_inputs[0], gain_inputs[1])
-    grad_attn_out = gain_term(gain_inputs[2], gain_inputs[3])
-    grad_ffn_in = gain_term(gain_inputs[4], gain_inputs[5])
-    grad_ffn_out = gain_term(gain_inputs[6], gain_inputs[7])
-    gains = jnp.stack(
+    input_grad = input_grad.reshape(2, 2, NC, OW, 640).transpose(2, 1, 0, 3, 4).reshape(1024, 640)
+    grad_attn_in = gain_term(x_rows, input_sum)
+    gains = jnp.concatenate(
         [
-            grad_attn_in,
-            grad_attn_out,
-            grad_ffn_in,
-            grad_ffn_out,
-            jnp.concatenate([grad_qnorm, grad_knorm, jnp.zeros((128,), F32)]),
+            grad_attn_in[None],
+            ffn_gains[:3],
+            jnp.concatenate([grad_qnorm, grad_knorm, jnp.zeros((128,), F32)])[None],
+            jnp.zeros((3, 640), F32),
         ]
     )
-    gains = jnp.concatenate([gains, jnp.zeros((3, 640), F32)])
     summed = sum_grads(
         grad_query.astype(BF),
         grad_key.astype(BF),
         grad_value.astype(BF),
         grad_out.astype(BF),
-        grad_gate.astype(BF),
-        grad_up.astype(BF),
-        grad_down.astype(BF),
+        grad_gate,
+        grad_up,
+        grad_down,
         gains,
     )
     return (output, input_grad, *summed[:7], *(g.reshape(-1) for g in summed[7:]))

time: 348 us -> 248 us (0.71)
  Pallas kernels: 69.5 us -> 142 us
  waiting for transfers between devices: 69.9 us -> 10.4 us
  blocking collectives: 58.2 us -> 0 us
  matrix products: 50.8 us -> 28.7 us
  between operations: 15 us -> 1.16 us
  starting transfers between devices: 20 us -> 8.78 us
  other arithmetic: 40.8 us -> 31.8 us
    pallas_call x0 -> x1, Pallas kernels: none -> 73 us  [ffn_block(): pl.pallas_call(ffn_kernel, out_shape=(sds(blocks, BF), sds(blocks, BF), s...]
    all_to_all x3 -> x0, blocking collectives: 58.2 us -> none  [the longest x2 38.5 us: sum_at_owner(): tiles = lax.all_to_all(in_blocks(x, dim, size), axis, 0, 0, tiled=True)]
    all_gather x1 -> x0, waiting for transfers between devices: 36.9 us -> none  [in_one_piece(): lax.all_gather(both, axis, axis=dim, tiled=True)]
    dot_general x9 -> x0, matrix products: 19.7 us -> none  [the longest x1 5.03 us: local(): jnp.einsum('rd,fd->rf', grad_ffn_low, w_down, preferred_element_type=jnp....]
    all_to_all x2 -> x1, waiting for transfers between devices: 25 us -> 10.4 us  [sum_at_owner(): tiles = lax.all_to_all(in_blocks(x, dim, size), axis, 0, 0, tiled=True)]
    all_to_all x2 -> x1, waiting for transfers between devices: 7.97 us -> 0.01 us  [copy_for_each(): return lax.all_to_all(copies, axis, split_axis=0, concat_axis=0, tiled=True)]
    all_to_all x2 -> x1, starting transfers between devices: 10.9 us -> 4.4 us  [sum_at_owner(): tiles = lax.all_to_all(in_blocks(x, dim, size), axis, 0, 0, tiled=True)]
    all_to_all x2 -> x1, starting transfers between devices: 9.06 us -> 4.38 us  [copy_for_each(): return lax.all_to_all(copies, axis, split_axis=0, concat_axis=0, tiled=True)]
  transfers between devices with their start and end apart: 5 -> 2, of which waited for: 4 -> 1; matrix products, arithmetic and copies ran while one was open for 8% -> 7% of each run, Pallas kernels for 20% -> 28%
where the time goes in v2:
time: 248 us; the launch traced here: 247 us
  Pallas kernels  142 us (57%)
  other arithmetic  31.8 us (13%)
  matrix products  28.7 us (12%)
  local copies, waits for them, and re-layouts  23.1 us (9%)
  waiting for transfers between devices  10.4 us (4%)
  starting transfers between devices  8.78 us (4%)
    pallas_call x1, Pallas kernels, ffn_block(): pl.pallas_call(ffn_kernel, out_shape=(sds(blocks, BF), sds(blocks, BF), s...  73 us
    pallas_call x1, Pallas kernels, sum_grads(): pl.pallas_call(sum_kernel, out_shape=(sds((4, 8, 224, 128), BF), sds((8,...  64.1 us
    all_to_all x1, waiting for transfers between devices, sum_at_owner(): tiles = lax.all_to_all(in_blocks(x, dim, size), axis, 0, 0, tiled=True)  10.4 us
    while x20, local copies, waits for them, and re-layouts  8.52 us
    pallas_call x4, other arithmetic, sum_grads(): pl.pallas_call(unpack_kernel, out_shape=(sds((640, 256), F32), sds((640,...  5.24 us
    pallas_call x1, Pallas kernels, sum_grads(): pl.pallas_call(unpack_kernel, out_shape=(sds((640, 256), F32), sds((640,...  4.97 us
  transfers between devices with their start and end apart: 2, of which 1 were waited for; matrix products, arithmetic and copies ran while one was open for 7% of the time, Pallas kernels for 28%

profile of v2, /device:TPU:1, one launch (start us, length us, event | category | flops | bytes accessed | tf_op | source)
XLA Modules:
  0.0 246.8 jit_solution(6330003870157800419)
XLA Ops:
  2.2 1.3 reshape.509.g_ao
  3.4 1.3 reshape.510.g_fi
  4.7 1.3 reshape.511.g_fo
  6.7 1.6 multiply_reduce_fusion.1
  8.4 2.1 convolution_convert_fusion.2
  12.4 2.4 fusion.81
  15.0 2.4 fusion.75
  17.4 1.1 fusion.50
  18.6 9.2 %while.28 = (s32[]{:T(128)}, bf16[2,1,512,256]{3,2,1,0:T(8,128)(2,1)S(1)}, f32[2,1,512]{2,1,0:T(1,128)S(1)}, s32[2,512]{1,0:T(2,128)S(1)}, s32[2,1024]{1,0:T(2,1...) while((s32[]{:T(128)}, ...), condition=%wide.region_6.7_spmd.clone, body=%wide.region_3.6_spmd.sunk.clone | while | flops 552075264 | bytes 8188009 | solution.py:649
  18.7 1.9 fusion.151
  20.6 1.0 fusion.152
  21.6 1.4 fusion.153
  23.2 1.9 fusion.151
  25.1 1.0 fusion.152
  26.1 1.4 fusion.153
  27.8 2.8 %convolution_convert_fusion = bf16[1024,640]{1,0:T(8,128)(2,1)} fusion(bf16[1024,256]{1,0:T(8,128)(2,1)S(1)} %bitcast.237, bf16[256,640]{1,0:T(8,128)(2,1)} %param.28), kind=kOutput, calls=%fused_computation.74 | convolution fusion | flops 336199680 | bytes 2162688 | tf_op jit(solution)/shard_map/dot_general | solution.py:657
  30.6 73.0 %ffn_block.1 = (bf16[4,4,64,640]{3,2,1,0:T(8,128)(2,1)}, bf16[4,4,64,640]{3,2,1,0:T(8,128)(2,1)}, f32[4,64,640]{2,1,0:T(8,128)}, bf16[640,512]{1,0:T(8,128)(2,1)...) custom-call(bf16[4,4,64,640]{3,2,1,0:T(8,128)(2,1)} %bitcast.229, ...), custom_call_target="tpu_custom_call" | custom-call | tf_op jit(solution)/shard_map/ffn_block/pallas_call | solution.py:438
  103.7 1.9 convolution_convert_fusion.1
  105.6 15.6 %while.29 = (s32[]{:T(128)}, f32[2,1,512,256]{3,2,1,0:T(8,128)S(1)}, f32[2,1024,256]{2,1,0:T(8,128)}, f32[2,1024,256]{2,1,0:T(8,128)}, s32[2,512]{1,0:T(2,128)S(...) while((s32[]{:T(128)}, ...), condition=%wide.region_9.10_spmd.clone, body=%wide.region_7.9_spmd.sunk.clone | while | flops 1349910528 | bytes 58758412 | solution.py:672
  107.1 1.2 multiply_reduce_fusion.11
  108.5 1.3 copy-done.11
  110.8 0.9 copy-done.14
  112.2 1.3 copy-done.15
  114.8 1.2 multiply_reduce_fusion.11
  116.2 1.3 copy-done.11
  119.9 1.3 copy-done.15
  121.2 2.3 fusion.78
  126.2 2.3 fusion.84
  132.2 1.2 copy.48
  133.4 4.4 %all-to-all-start = ((bf16[4,256,640]{2,1,0:T(8,128)(2,1)}), bf16[4,256,640]{2,1,0:T(8,128)(2,1)}, u32[]{:S(2)}, u32[]{:S(2)}) async-start(bf16[4,256,640]{2,1,0:T(8,128)(2,1)} %bitcast.49), calls=%async_computation | async-start | bytes 2621440 | tf_op jit(solution)/shard_map/all_to_all | solution.py:464
  137.8 1.8 bitcast_convert_fusion
  139.6 1.2 multiply_reduce_fusion.8
  143.9 10.4 %all-to-all-done = bf16[4,256,640]{2,1,0:T(8,128)(2,1)} async-done(((bf16[4,256,640]{2,1,0:T(8,128)(2,1)}), bf16[4,256,640]{2,1,0:T(8,128)(2,1)}, u32[]{:S(2)}, u32[]{:S(2)}) %all-to-all-start) | async-done | bytes 1310752 | tf_op jit(solution)/shard_map/all_to_all | solution.py:464
  154.3 1.6 convert_reduce_fusion
  156.2 1.4 fusion.73
  157.6 1.2 broadcast_in_dim.84
  158.7 4.4 %all-to-all-start.1 = ((bf16[4,256,640]{2,1,0:T(8,128)(2,1)}), bf16[4,256,640]{2,1,0:T(8,128)(2,1)S(1)}, u32[]{:S(2)}, u32[]{:S(2)}) async-start(bf16[4,256,640]{2,1,0:T(8,128)(2,1)} %broadcast_in_dim.84), calls=%async_computation.1 | async-start | bytes 2621440 | tf_op jit(solution)/shard_map/all_to_all | solution.py:476
  163.2 2.1 pad_maximum_fusion.kv
  165.3 2.8 %convolution_convert_fusion.5.out = bf16[256,640]{1,0:T(8,128)(2,1)} fusion(bf16[1024,256]{1,0:T(8,128)(2,1)} %bitcast.238, bf16[1024,640]{1,0:T(8,128)(2,1)} %bitcast.262), kind=kOutput, calls=%fused_computation.81 | convolution fusion | flops 335708160 | bytes 2162688 | tf_op jit(solution)/shard_map/rh,rd->hd/dot_general | solution.py:665
  168.1 1.5 convolution_convert_fusion.6.query
  170.3 64.1 %sum_grads.1 = (bf16[4,8,224,128]{3,2,1,0:T(8,128)(2,1)}, bf16[8,112,128]{2,1,0:T(8,128)(2,1)}, bf16[8,112,128]{2,1,0:T(8,128)(2,1)}, bf16[8,112,128]{2,1,0:T(8,...) custom-call(bf16[640,512]{1,0:T(8,128)(2,1)} %get-tuple-element.152.gate, ...), custom_call_target="tpu_custom_call" | custom-call | tf_op jit(solution)/shard_map/sum_grads/pallas_call | solution.py:197
  234.4 5.0 %unpack_grads.1 = (f32[640,256]{1,0:T(8,128)}, f32[640,256]{1,0:T(8,128)}, f32[640,256]{1,0:T(8,128)}, f32[256,640]{1,0:T(8,128)}, f32[640,512]{1,0:T(8,128)}, /...) custom-call(bf16[4,8,224,128]{3,2,1,0:T(8,128)(2,1)} %get-tuple-elem, ...), custom_call_target="tpu_custom_call" | custom-call | tf_op jit(solution)/shard_map/unpack_grads/pallas_call | solution.py:218
  239.3 1.4 reduce.15
  240.7 1.3 reduce.16
  242.0 1.3 reduce.17
  243.3 1.3 reduce.18
  244.6 1.2 copy.50
  245.8 1.1 copy.79
  (138 shorter events, 21.6 us)
Async XLA Ops:
  0.6 9.9 %copy-start = (bf16[640,256]{1,0:T(8,128)(2,1)S(1)}, bf16[640,256]{1,0:T(8,128)(2,1)}, u32[]{:S(2)}) copy-start(bf16[640,256]{1,0:T(8,128)(2,1)} %param.26) | copy-start | bytes 983044
  8.3 2.2 copy-start.1
  8.3 2.2 copy-start.22
  10.5 1.0 copy-start.20
  11.3 1.2 copy-start.3
  11.3 0.9 copy-start.24
  12.2 2.9 %copy-start.5 = (f32[1024,256]{1,0:T(8,128)}, f32[1024,256]{1,0:T(8,128)S(1)}, u32[]{:S(2)}) copy-start(f32[1024,256]{1,0:T(8,128)S(1)} %get-tuple-element.276) | copy-start | bytes 3145732
  12.2 2.6 %copy-start.23 = (f32[256]{0:T(256)S(1)}, f32[256]{0:T(256)}, u32[]{:S(2)}) copy-start(f32[256]{0:T(256)} %param.36) | copy-start | bytes 3076
  27.8 75.8 %copy-start.9 = (bf16[2,1,512,256]{3,2,1,0:T(8,128)(2,1)}, bf16[2,1,512,256]{3,2,1,0:T(8,128)(2,1)S(1)}, u32[]{:S(2)}) copy-start(bf16[2,1,512,256]{3,2,1,0:T(8,128)(2,1)S(1)} %get-tuple-element.144) | copy-start | bytes 1572868
  30.6 73.0 %copy-start.19 = (bf16[256,640]{1,0:T(8,128)(2,1)S(1)}, bf16[256,640]{1,0:T(8,128)(2,1)}, u32[]{:S(2)}) copy-start(bf16[256,640]{1,0:T(8,128)(2,1)} %param.28) | copy-start | bytes 983044
  105.8 1.2 copy-start.17
  108.2 1.6 copy-start.11
  109.8 1.9 copy-start.14
  110.3 1.8 copy-start.12
  112.2 1.4 copy-start.15
  113.5 1.2 copy-start.17
  115.9 1.6 copy-start.11
  117.5 1.9 copy-start.14
  118.0 1.8 copy-start.12
  119.9 1.4 copy-start.15
  121.2 2.3 copy-start.6
  123.5 1.6 copy-start.13
  124.3 1.7 copy-start.16
  126.1 2.4 copy-start.4
  129.3 1.8 copy-start.7
  129.3 1.2 copy-start.21
  130.5 1.0 copy-start.18
  132.2 5.6 %copy-start.2 = (bf16[1024,640]{1,0:T(8,128)(2,1)S(1)}, bf16[1024,640]{1,0:T(8,128)(2,1)}, u32[]{:S(2)}) copy-start(bf16[1024,640]{1,0:T(8,128)(2,1)} %param.21) | copy-start | bytes 3932164
  133.4 20.9 %all-to-all-start = ((bf16[4,256,640]{2,1,0:T(8,128)(2,1)}), bf16[4,256,640]{2,1,0:T(8,128)(2,1)}, u32[]{:S(2)}, u32[]{:S(2)}) async-start(bf16[4,256,640]{2,1,0:T(8,128)(2,1)} %bitcast.49), calls=%async_computation | async-start | bytes 2621440 | tf_op jit(solution)/shard_map/all_to_all | solution.py:464
  137.8 3.1 %copy-start.25 = (f32[8,640]{1,0:T(8,128)S(1)}, f32[8,640]{1,0:T(8,128)}, u32[]{:S(2)}) copy-start(f32[8,640]{1,0:T(8,128)} %get-tuple-element.155) | copy-start | bytes 61444
  140.9 1.5 copy-start.8
  158.7 85.9 %all-to-all-start.1 = ((bf16[4,256,640]{2,1,0:T(8,128)(2,1)}), bf16[4,256,640]{2,1,0:T(8,128)(2,1)S(1)}, u32[]{:S(2)}, u32[]{:S(2)}) async-start(bf16[4,256,640]{2,1,0:T(8,128)(2,1)} %broadcast_in_dim.84), calls=%async_computation.1 | async-start | bytes 2621440 | tf_op jit(solution)/shard_map/all_to_all | solution.py:476
  239.3 6.4 %copy-start.10 = (bf16[4,4,64,640]{3,2,1,0:T(8,128)(2,1)S(1)}, bf16[4,4,64,640]{3,2,1,0:T(8,128)(2,1)}, u32[]{:S(2)}) copy-start(bf16[4,4,64,640]{3,2,1,0:T(8,128)(2,1)} %get-tuple-element.145) | copy-start | bytes 3932164

commit v3 on v2

v3 whole, which is shorter than its diff:
```python
import jax, jax.numpy as jnp
from jax import lax
from jax.experimental import pallas as pl
from jax.experimental.pallas import tpu as pltpu
from jax.sharding import PartitionSpec as P

WINDOW = 512
EPSILON = 1e-06
ROPE_BASE = 10000.0
NEG_LARGE = -1e30

MESH = pl.DeviceIdType.MESH
BF = jnp.bfloat16
F32 = jnp.float32
VMEM = pl.BlockSpec(memory_space=pltpu.VMEM)
VMEM_LIMIT = 60 * 1024 * 1024


def neighbours():
    dp = lax.axis_index("dp")
    t = lax.axis_index("tensor")
    z = lax.rem(dp, 4)
    y = lax.rem(dp // 4, 4)
    xh = dp // 16
    xl = t // 2
    core = lax.rem(t, 2)
    ya = y + 1 - 2 * lax.rem(y, 2)
    za = z + 1 - 2 * lax.rem(z, 2)
    links = [
        (dp + (ya - y) * 4, t),
        (dp + (za - z), t),
        (dp + (3 - 2 * y) * 4, t),
        (dp + (3 - 2 * z), t),
    ]
    bits = [lax.rem((y + 1) // 2, 2), lax.rem((z + 1) // 2, 2), y // 2, z // 2]
    across = (dp + 16 - 32 * xh, t)
    sibling = (dp, t + 1 - 2 * core)
    beside = (dp, t + 2 - 4 * xl)
    return links, bits, across, sibling, beside, xl, core


def greet(devices):
    barrier = pltpu.get_barrier_semaphore()
    for d in devices:
        pl.semaphore_signal(barrier, inc=1, device_id=d, device_id_type=MESH)
    pl.semaphore_wait(barrier, len(devices))


def send(src, dst, ssem, rsem, device):
    copy = pltpu.make_async_remote_copy(
        src_ref=src, dst_ref=dst, send_sem=ssem, recv_sem=rsem, device_id=device, device_id_type=MESH
    )
    copy.start()
    return copy


class Reduction:
    def __init__(self, ins, bufs, recvs, outs, ssem, rsem, links, bits, across):
        self.ins, self.bufs, self.recvs, self.outs, self.ssem, self.rsem = ins, bufs, recvs, outs, ssem, rsem
        self.links, self.bits, self.across = links, bits, across
        self.base = [jnp.int32(0)] * 4
        self.bases = []
        self.copies = None

    def start(self, step):
        copies = []
        for p in range(4):
            buf, recv = (self.ins if step == 0 else self.bufs)[p], self.recvs[p]
            ss, rs = self.ssem.at[p, step], self.rsem.at[p, step]
            if step < 3:
                n = 4 >> step
                bit = self.bits[(p + step) % 4]
                there = self.base[p] + (1 - bit) * n
                self.base[p] = self.base[p] + bit * n
                at = (0, 4, 6)[step]
                src, dst, dev = buf.at[pl.ds(there, n)], recv.at[pl.ds(at, n)], self.links[(p + step) % 4]
            elif step < 5:
                dev = self.links[(p + 3) % 4] if step == 3 else self.across
                src, dst = buf.at[pl.ds(self.base[p], 1)], recv.at[pl.ds(4 + step, 1)]
            else:
                s = 7 - step
                n = 4 >> s
                bit = self.bits[(p + s) % 4]
                src = dst = self.outs[p].at[pl.ds(self.base[p], n)]
                self.base[p] = self.base[p] - bit * n
                dev = self.links[(p + s) % 4]
            copies.append(send(src, dst, ss, rs, dev))
        self.copies = copies

    def finish(self, step):
        for p in range(4):
            buf, recv = self.bufs[p], self.recvs[p]
            into = self.outs[p] if step == 4 else buf
            buf = self.ins[p] if step == 0 else buf
            self.copies[p].wait()
            if step < 5:
                n = (4, 2, 1, 1, 1)[step]
                at = (0, 4, 6, 7, 8)[step]
                base = self.base[p]

                def add(i, carry):
                    into[base + i] = (buf[base + i].astype(F32) + recv[at + i].astype(F32)).astype(BF)
                    return carry

                lax.fori_loop(0, n, add, 0)


NC = 4
CR = 1024 // NC
OW = CR // 4
C0 = 0.7978845608028654
C1 = 0.044715


def nt(a, b):
    return lax.dot_general(a, b, (((1,), (1,)), ((), ())), preferred_element_type=F32)


def tn(a, b):
    return lax.dot_general(a, b, (((0,), (0,)), ((), ())), preferred_element_type=F32)


def nn(a, b):
    return jnp.dot(a, b, preferred_element_type=F32)


def inv_rms(v):
    return lax.rsqrt(jnp.mean(v * v, axis=-1, keepdims=True) + EPSILON)


def rms_back(v, r, du):
    return r * du - v * (r * r * r * jnp.mean(du * v, axis=-1, keepdims=True))


class Tensor:
    def __init__(self, sibling, beside, xl, core, ssem, rsem):
        self.sibling, self.beside, self.xl, self.core = sibling, beside, xl, core
        self.own = core * 2 + xl
        self.ssem, self.rsem = ssem, rsem
        self.used = 0

    def send(self, src, dst, device):
        i = self.used
        self.used += 1
        return send(src, dst, self.ssem.at[i], self.rsem.at[i], device)

    def sum_a(self, part, recv):
        return self.send(part.at[pl.ds((1 - self.core) * 2, 2)], recv, self.sibling)

    def sum_b(self, copy, part, recv, out, recv2):
        copy.wait()
        there = self.core * 2 + 1 - self.xl
        out[...] = (part[there].astype(F32) + recv[1 - self.xl].astype(F32)).astype(BF)
        return self.send(out, recv2, self.beside)

    def sum_c(self, copy, part, recv, recv2):
        copy.wait()
        return part[self.own].astype(F32) + recv[self.xl].astype(F32) + recv2[...].astype(F32)

    def gather_a(self, buf):
        block = buf.at[self.own]
        return self.send(block, block, self.beside), self.send(block, block, self.sibling)

    def gather_b(self, copies, buf):
        copies[0].wait()
        block = buf.at[self.core * 2 + 1 - self.xl]
        return copies[1], self.send(block, block, self.sibling)

    def gather_c(self, copies):
        for c in copies:
            c.wait()


def turn(v, cosine, sine):
    a, b = v[:, :128], v[:, 128:]
    return jnp.concatenate([a * cosine - b * sine, b * cosine + a * sine], axis=-1)


def turn_back(v, cosine, sine):
    a, b = v[:, :128], v[:, 128:]
    return jnp.concatenate([a * cosine + b * sine, b * cosine - a * sine], axis=-1)


def key_range(i):
    first = max(0, (i - 2) * CR)
    return first, (i + 1) * CR - first


def forward_kernel(x, cot, segs, cos_t, sin_t, wq, wk, wv, wo, wg, wu, wd, g_in, g_ao, g_fi, g_fo, g_q, g_k,
               output, dattn, dmid_out, grads, down4, gains, normed, q_raw, k_raw, q, k, v, prob, heads,
               attn, ffn_g, dffn_g, hid, act_a, act_b, dgate, dup, part2, part3, attn_own, mid_own,
               recv_a, recv_b, sent_b, ssem, rsem):
    _, _, _, sibling, beside, xl, core = neighbours()
    greet([sibling, beside])
    t = Tensor(sibling, beside, xl, core, ssem, rsem)
    own = t.own
    state = [dict() for _ in range(NC)]

    def rs_a(e, part):
        def run(c):
            state[c]["a"] = t.sum_a(part.at[c], recv_a.at[e, c])
        return run

    def rs_b(e, part):
        def run(c):
            state[c]["b"] = t.sum_b(state[c]["a"], part.at[c], recv_a.at[e, c], sent_b.at[e, c], recv_b.at[e, c])
        return run

    def rs_c(e, part, c):
        return t.sum_c(state[c]["b"], part.at[c], recv_a.at[e, c], recv_b.at[e, c])

    def attention_stage(c):
        rows = slice(c * CR, c * CR + CR)
        xv = x[c].reshape(CR, 640).astype(F32)
        n = (xv * inv_rms(xv) * vec(g_in)).astype(BF)
        normed[rows] = n
        cosine, sine = cos_t[rows], sin_t[rows]
        raw = nn(n, wq[...])
        q_raw[rows] = raw
        q_low = turn(raw * inv_rms(raw) * vec(g_q), cosine, sine).astype(BF)
        q[rows] = q_low
        raw = nn(n, wk[...])
        k_raw[rows] = raw
        k[rows] = turn(raw * inv_rms(raw) * vec(g_k), cosine, sine).astype(BF)
        v[rows] = nn(n, wv[...]).astype(BF)
        first, size = key_range(c)
        keys = slice(first, first + size)
        scores = nt(q_low, k[keys]) * 0.0625
        gap = c * CR - first + lax.broadcasted_iota(jnp.int32, (CR, size), 0) - lax.broadcasted_iota(jnp.int32, (CR, size), 1)
        seg_rows = jnp.broadcast_to(segs[:, rows], (128, CR)).T[:, :1]
        allowed = (gap >= 0) & (gap < WINDOW) & (seg_rows == segs[:, keys])
        masked = jnp.where(allowed, scores, NEG_LARGE)
        e = jnp.where(allowed, jnp.exp(masked - jnp.max(masked, axis=-1, keepdims=True)), 0.0)
        p = e / jnp.sum(e, axis=-1, keepdims=True)
        prob[c, :, 0:size] = p
        h = nn(p.astype(BF), v[keys]).astype(BF)
        heads[rows] = h
        attn[c] = nn(h, wo[...]).astype(BF).reshape(4, OW, 640)
        rs_a(0, attn)(c)

    def mid_stage(c):
        a = rs_c(0, attn, c)
        attn_own[c] = a
        mid = x[c, own].astype(F32) + a * inv_rms(a) * vec(g_ao)
        mid_own[c] = mid
        ffn_g[c, own] = (mid * inv_rms(mid) * vec(g_fi)).astype(BF)
        state[c]["g"] = t.gather_a(ffn_g.at[c])

    def forward(buf, key):
        def run(c):
            state[c][key] = t.gather_b(state[c][key], buf.at[c])
        return run

    def up_stage(c):
        t.gather_c(state[c]["g"])
        f = ffn_g[c].reshape(CR, 640)
        gate = nn(f, wg[...])
        up = nn(f, wu[...])
        th = jnp.tanh(C0 * (gate + C1 * gate * gate * gate))
        half = 0.5 * (1.0 + th)
        act = gate * half
        slope = half + 0.5 * gate * (1.0 - th * th) * (C0 * (1.0 + 3.0 * C1 * gate * gate))
        act_a[c] = up * slope
        act_b[c] = act
        h = (act * up).astype(BF)
        hid[c] = h
        part2[c] = nn(h, wd[...]).astype(BF).reshape(4, OW, 640)
        rs_a(1, part2)(c)

    def out_stage(c):
        s = rs_c(1, part2, c)
        r = inv_rms(s)
        ct = cot[c, own].astype(F32)
        dffn_g[c, own] = rms_back(s, r, ct * vec(g_fo)).astype(BF)
        state[c]["g"] = t.gather_a(dffn_g.at[c])
        output[c, own] = (mid_own[c] + s * r * vec(g_fo)).astype(BF)
        state[c]["o"] = t.gather_a(output.at[c])
        gains[2:3, :] = gains[2:3, :] + jnp.sum(ct * s * r, axis=0, keepdims=True)

    def down_stage(c):
        t.gather_c(state[c]["g"])
        d = dffn_g[c].reshape(CR, 640)
        dh = nt(d, wd[...])
        dg = (dh * act_a[c]).astype(BF)
        du = (dh * act_b[c]).astype(BF)
        dgate[c] = dg
        dup[c] = du
        part3[c] = (nt(dg, wg[...]) + nt(du, wu[...])).astype(BF).reshape(4, OW, 640)
        rs_a(2, part3)(c)

    def attn_stage(c):
        d = rs_c(2, part3, c)
        mid, a = mid_own[c], attn_own[c]
        r = inv_rms(mid)
        gains[1:2, :] = gains[1:2, :] + jnp.sum(d * mid * r, axis=0, keepdims=True)
        dmid = cot[c, own].astype(F32) + rms_back(mid, r, d * vec(g_fi))
        dmid_out[c] = dmid
        r = inv_rms(a)
        gains[0:1, :] = gains[0:1, :] + jnp.sum(dmid * a * r, axis=0, keepdims=True)
        dattn[c, own] = rms_back(a, r, dmid * vec(g_ao)).astype(BF)
        state[c]["g"] = t.gather_a(dattn.at[c])

    def last(c):
        t.gather_c(state[c]["o"])
        t.gather_c(state[c]["g"])

    def weights_down():
        g = tn(hid[...].reshape(1024, 512), dffn_g[...].reshape(1024, 640)).astype(BF)
        for s in range(8):
            for p in range(4):
                grads[p, s, 160:224] = g[64 * s:64 * s + 64, 128 * p:128 * p + 128]
        down4[...] = g[:, 512:640]

    def weights_gate():
        g = tn(ffn_g[...].reshape(1024, 640), dgate[...].reshape(1024, 512)).astype(BF)
        for s in range(8):
            for p in range(4):
                grads[p, s, 0:80] = g[80 * s:80 * s + 80, 128 * p:128 * p + 128]

    def weights_up():
        g = tn(ffn_g[...].reshape(1024, 640), dup[...].reshape(1024, 512)).astype(BF)
        for s in range(8):
            for p in range(4):
                grads[p, s, 80:160] = g[80 * s:80 * s + 80, 128 * p:128 * p + 128]

    gains[...] = jnp.zeros_like(gains)
    stages = [
        attention_stage, rs_b(0, attn), mid_stage, forward(ffn_g, "g"), up_stage,
        rs_b(1, part2), out_stage, forward(dffn_g, "g"), down_stage,
        rs_b(2, part3), forward(output, "o"), attn_stage, forward(dattn, "g"), last,
    ]
    work = sorted(((s + SKEW * c, s, c) for s in range(len(stages)) for c in range(NC)), key=lambda w: (w[0], w[2]))
    fill = {9: weights_down, 11: weights_gate, 12: weights_up}
    for _, s, c in work:
        stages[s](c)
        if c == NC - 1 and s in fill:
            fill[s]()


def vec(g):
    return g[...]


SKEW = 1


def forward_part(x, cot, segs, cos_t, sin_t, weights, gains):
    sds = jax.ShapeDtypeStruct
    dma = pltpu.SemaphoreType.DMA
    blocks = (NC, 4, OW, 640)
    count = NC * (3 * 2 + 4 * 3)
    v = pltpu.VMEM
    return pl.pallas_call(
        forward_kernel,
        out_shape=(sds(blocks, BF), sds(blocks, BF), sds((NC, OW, 640), F32), sds((4, 8, 224, 128), BF),
                   sds((512, 128), BF), sds((8, 640), F32), sds((1024, 640), BF), sds((1024, 256), F32),
                   sds((1024, 256), F32), sds((1024, 256), BF), sds((1024, 256), BF), sds((1024, 256), BF),
                   sds((NC, CR, 768), F32), sds((1024, 256), BF)),
        in_specs=[VMEM] * 18,
        out_specs=[VMEM] * 14,
        scratch_shapes=[
            v(blocks, BF),
            v(blocks, BF), v(blocks, BF), v((NC, CR, 512), BF), v((NC, CR, 512), F32), v((NC, CR, 512), F32),
            v((NC, CR, 512), BF), v((NC, CR, 512), BF), v(blocks, BF), v(blocks, BF), v((NC, OW, 640), F32),
            v((NC, OW, 640), F32), v((3, NC, 2, OW, 640), BF), v((3, NC, OW, 640), BF), v((3, NC, OW, 640), BF),
            dma((count,)), dma((count,)),
        ],
        compiler_params=pltpu.CompilerParams(collective_id=3, has_side_effects=True, vmem_limit_bytes=VMEM_LIMIT),
        name="forward_part",
    )(x, cot, segs, cos_t, sin_t, *weights, *gains)


def backward_kernel(dattn, dmid, x, heads, prob, q, k, v, q_raw, k_raw, cos_t, sin_t, normed, wq, wk, wv, wo, g_in, g_q, g_k,
                grads, down4, gains, in_grad, a_out, o0, o1, o2, o3, kv_out, gains_out,
                dk, dv, dqkv, part, recv_a, recv_b, sent_b, a_buf, b0, b1, b2, b3, a_recv, r0, r1, r2, r3,
                kv, kv_work, kv_recv, g_recv,
                ssem, rsem, a_ss, a_rs, b_ss, b_rs, k_ss, k_rs, g_ss, g_rs):
    links, bits, across, sibling, beside, xl, core = neighbours()
    greet(links + [across, sibling, beside])
    t = Tensor(sibling, beside, xl, core, ssem, rsem)
    own = t.own
    state = [dict() for _ in range(NC)]
    first = Reduction([grads.at[p] for p in range(4)], [a_buf.at[p] for p in range(4)], [a_recv.at[p] for p in range(4)],
                      [a_out.at[p] for p in range(4)], a_ss, a_rs, links, bits, across)
    bs = [b0, b1, b2, b3]
    second = Reduction(bs, bs, [r0, r1, r2, r3], [o0, o1, o2, o3], b_ss, b_rs, links, bits, across)
    first.start(0)
    gains_out[...] = gains[...]

    def block(i):
        rows = slice(i * CR, i * CR + CR)
        start, size = key_range(i)
        dh = nt(dattn[i].reshape(CR, 640), wo[...]).astype(BF)
        p = prob[i, :, 0:size]
        dp = nt(dh, v[start:start + size])
        ds = (p * (dp - jnp.sum(p * dp, axis=-1, keepdims=True))).astype(BF)
        dq = nn(ds, k[start:start + size]) * 0.0625
        dk_add = tn(ds, q[rows]) * 0.0625
        dv_add = tn(p.astype(BF), dh)
        fresh = size if i == NC - 1 else (CR if i == NC - 2 else 0)
        if fresh:
            dk[start:start + fresh] = dk_add[:fresh]
            dv[start:start + fresh] = dv_add[:fresh]
        if fresh < size:
            dk[start + fresh:start + size] = dk[start + fresh:start + size] + dk_add[fresh:]
            dv[start + fresh:start + size] = dv[start + fresh:start + size] + dv_add[fresh:]
        cosine, sine = cos_t[rows], sin_t[rows]
        raws = []
        for d, raw, g, at in ((dq, q_raw[rows], g_q, 0), (dk[rows], k_raw[rows], g_k, 256)):
            du = turn_back(d, cosine, sine)
            r = inv_rms(raw)
            gains_out[4:5, at:at + 256] = gains_out[4:5, at:at + 256] + jnp.sum(du * raw * r, axis=0, keepdims=True)
            raws.append(rms_back(raw, r, du * vec(g)).astype(BF))
        raws.append(dv[rows].astype(BF))
        for j in range(3):
            dqkv[rows, 256 * j:256 * j + 256] = raws[j]
        term = nt(raws[0], wq[...]) + nt(raws[1], wk[...]) + nt(raws[2], wv[...])
        part[i] = term.astype(BF).reshape(4, OW, 640)
        state[i]["a"] = t.sum_a(part.at[i], recv_a.at[i])

    def rs_b(i):
        state[i]["b"] = t.sum_b(state[i]["a"], part.at[i], recv_a.at[i], sent_b.at[i], recv_b.at[i])

    def in_stage(i):
        d = t.sum_c(state[i]["b"], part.at[i], recv_a.at[i], recv_b.at[i])
        xv = x[i, own].astype(F32)
        r = inv_rms(xv)
        gains_out[3:4, :] = gains_out[3:4, :] + jnp.sum(d * xv * r, axis=0, keepdims=True)
        in_grad[i, own] = (dmid[i] + rms_back(xv, r, d * vec(g_in))).astype(BF)
        state[i]["g"] = t.gather_a(in_grad.at[i])

    def forward(i):
        state[i]["g"] = t.gather_b(state[i]["g"], in_grad.at[i])

    def swap_gains(i, device):
        return send(gains_out, g_recv.at[i], g_ss.at[i], g_rs.at[i], device)

    def add_gains(i, copy):
        copy.wait()
        gains_out[...] = gains_out[...] + g_recv[i]

    def out_weights():
        g = tn(heads[...], dattn[...].reshape(1024, 640)).astype(BF)
        for c in range(8):
            rows = slice(32 * c, 32 * c + 32)
            b0[c, 80:112] = g[rows, 0:128]
            b1[c, 80:112] = g[rows, 128:256]
            b2[c, 80:112] = g[rows, 256:384]
            b3[c, 0:64] = down4[64 * c:64 * c + 64, :]
            b3[c, 64:96] = g[rows, 384:512]
            b3[c, 96:128] = g[rows, 512:640]

    def next_step(red, step):
        red.finish(step)
        if step < 7:
            red.start(step + 1)

    block(3)
    out_weights()
    rs_b(3)
    block(2)
    next_step(first, 0)
    in_stage(3)
    rs_b(2)
    block(1)
    forward(3)
    in_stage(2)
    rs_b(1)
    next_step(first, 1)
    block(0)
    forward(2)
    in_stage(1)
    next_step(first, 2)
    g = tn(normed[...], dqkv[...]).astype(BF)
    for j in range(4):
        kv[j] = g[:, 256 + 128 * j:384 + 128 * j]
    kc = send(kv.at[pl.ds((1 - core) * 2, 2)], kv_recv.at[pl.ds(0, 2)], k_ss.at[0], k_rs.at[0], sibling)
    rs_b(0)
    for c in range(8):
        b0[c, 0:80] = g[80 * c:80 * c + 80, 0:128]
        b1[c, 0:80] = g[80 * c:80 * c + 80, 128:256]
    forward(1)
    kc.wait()
    for i in range(2):
        kv_work[i] = (kv[core * 2 + i].astype(F32) + kv_recv[i].astype(F32)).astype(BF)
    kc = send(kv_work.at[pl.ds(1 - xl, 1)], kv_recv.at[pl.ds(2, 1)], k_ss.at[1], k_rs.at[1], beside)
    next_step(first, 3)
    in_stage(0)
    gc = swap_gains(0, sibling)
    kc.wait()
    mine = core * 2 + xl
    for c in range(8):
        b2[c, 0:80] = (kv_work[xl, 80 * c:80 * c + 80].astype(F32) + kv_recv[2, 80 * c:80 * c + 80].astype(F32)).astype(BF)
    second.start(0)
    forward(0)
    add_gains(0, gc)
    gc = swap_gains(1, beside)
    next_step(first, 4)
    for step in range(8):
        next_step(second, step)
        if step < 3:
            next_step(first, 5 + step)
        if step < 6:
            add_gains(1 + step, gc)
            if step < 5:
                gc = swap_gains(2 + step, (links + [across])[step])
    for c in range(8):
        kv_out[mine, 80 * c:80 * c + 80] = o2[c, 0:80]
    kc = send(kv_out.at[pl.ds(mine, 1)], kv_out.at[pl.ds(mine, 1)], k_ss.at[2], k_rs.at[2], beside)
    for i in range(NC):
        t.gather_c(state[i]["g"])
    kc.wait()
    kc = send(kv_out.at[pl.ds(core * 2, 2)], kv_out.at[pl.ds(core * 2, 2)], k_ss.at[3], k_rs.at[3], sibling)
    kc.wait()


def unpack_kernel(a, b0, b1, b2, b3, kv, gains, query, key, value, out, gate, up, down, g0, g1, g2, g3, g4, g5):
    for p in range(4):
        cols = slice(128 * p, 128 * p + 128)
        for c in range(8):
            gate[80 * c:80 * c + 80, cols] = a[p, c, 0:80].astype(F32)
            up[80 * c:80 * c + 80, cols] = a[p, c, 80:160].astype(F32)
            down[64 * c:64 * c + 64, cols] = a[p, c, 160:224].astype(F32)
    for c in range(8):
        for p, b in ((0, b0), (1, b1)):
            query[80 * c:80 * c + 80, 128 * p:128 * p + 128] = b[c, 0:80].astype(F32)
            out[32 * c:32 * c + 32, 128 * p:128 * p + 128] = b[c, 80:112].astype(F32)
        out[32 * c:32 * c + 32, 256:384] = b2[c, 80:112].astype(F32)
        down[64 * c:64 * c + 64, 512:640] = b3[c, 0:64].astype(F32)
        out[32 * c:32 * c + 32, 384:512] = b3[c, 64:96].astype(F32)
        out[32 * c:32 * c + 32, 512:640] = b3[c, 96:128].astype(F32)
    for j in range(2):
        key[:, 128 * j:128 * j + 128] = kv[j].astype(F32)
        value[:, 128 * j:128 * j + 128] = kv[2 + j].astype(F32)
    for i, g in ((3, g0), (0, g1), (1, g2), (2, g3)):
        g[...] = gains[i, :]
    g4[...] = gains[4, 0:256]
    g5[...] = gains[4, 256:512]


def backward_part(*operands):
    sds = jax.ShapeDtypeStruct
    dma = pltpu.SemaphoreType.DMA
    v = pltpu.VMEM
    blocks = (NC, 4, OW, 640)
    count = NC * 5
    stacks = pl.pallas_call(
        backward_kernel,
        out_shape=(sds(blocks, BF), sds((4, 8, 224, 128), BF), sds((8, 112, 128), BF), sds((8, 112, 128), BF),
                   sds((8, 112, 128), BF), sds((8, 128, 128), BF), sds((4, 640, 128), BF), sds((8, 640), F32)),
        in_specs=[VMEM] * len(operands),
        out_specs=[VMEM] * 8,
        scratch_shapes=[
            v((1024, 256), F32), v((1024, 256), F32), v((1024, 768), BF), v(blocks, BF),
            v((NC, 2, OW, 640), BF), v((NC, OW, 640), BF), v((NC, OW, 640), BF),
            v((4, 8, 224, 128), BF),
            v((8, 112, 128), BF), v((8, 112, 128), BF), v((8, 112, 128), BF), v((8, 128, 128), BF),
            v((4, 9, 224, 128), BF),
            v((9, 112, 128), BF), v((9, 112, 128), BF), v((9, 112, 128), BF), v((9, 128, 128), BF),
            v((4, 640, 128), BF), v((2, 640, 128), BF), v((3, 640, 128), BF), v((7, 8, 640), F32),
            dma((count,)), dma((count,)),
            dma((4, 8)), dma((4, 8)), dma((4, 8)), dma((4, 8)), dma((4,)), dma((4,)), dma((7,)), dma((7,)),
        ],
        compiler_params=pltpu.CompilerParams(collective_id=7, has_side_effects=True, vmem_limit_bytes=VMEM_LIMIT),
        name="backward_part",
    )(*operands)
    outs = pl.pallas_call(
        unpack_kernel,
        out_shape=(sds((640, 256), F32), sds((640, 256), F32), sds((640, 256), F32), sds((256, 640), F32),
                   sds((640, 512), F32), sds((640, 512), F32), sds((512, 640), F32),
                   sds((640,), F32), sds((640,), F32), sds((640,), F32), sds((640,), F32),
                   sds((256,), F32), sds((256,), F32)),
        in_specs=[VMEM] * 7,
        out_specs=[VMEM] * 13,
        compiler_params=pltpu.CompilerParams(vmem_limit_bytes=VMEM_LIMIT),
        name="unpack_grads",
    )(*stacks[1:])
    return stacks[0], outs


def rope_tables(positions, head_size):
    half_size = head_size // 2
    inv_freq = ROPE_BASE ** (-2.0 * jnp.arange(half_size, dtype=jnp.float32) / head_size)
    angles = positions.astype(jnp.float32)[:, None] * inv_freq[None, :]
    return (jnp.cos(angles), jnp.sin(angles))


def local(
    inputs,
    segments,
    positions,
    cotangent,
    w_query,
    w_key,
    w_value,
    w_out,
    w_gate,
    w_up,
    w_down,
    g_attn_in,
    g_attn_out,
    g_ffn_in,
    g_ffn_out,
    g_query,
    g_key,
):
    blocks = (NC, 4, OW, 640)
    x = inputs.reshape(blocks)
    cos_t, sin_t = rope_tables(positions, 256)
    (output, dattn, dmid, grads, down4, gains, normed, q_raw, k_raw, q, k, v, prob, heads) = forward_part(
        x,
        cotangent.reshape(blocks),
        segments.reshape(1, 1024),
        cos_t,
        sin_t,
        (w_query, w_key, w_value, w_out, w_gate, w_up, w_down),
        (g_attn_in, g_attn_out, g_ffn_in, g_ffn_out, g_query, g_key),
    )
    input_grad, summed = backward_part(
        dattn, dmid, x, heads, prob, q, k, v, q_raw, k_raw, cos_t, sin_t, normed,
        w_query, w_key, w_value, w_out, g_attn_in, g_query, g_key, grads, down4, gains,
    )
    return (output.reshape(1024, 640), input_grad.reshape(1024, 640), *summed)


def solution(mesh):
    placed = (
        P("dp", None),
        P("dp"),
        P("dp"),
        P("dp", None),
        P(None, "tensor"),
        P(),
        P(),
        P("tensor", None),
        P(None, "tensor"),
        P(None, "tensor"),
        P("tensor", None),
        P(),
        P(),
        P(),
        P(),
        P(),
        P(),
    )
    return jax.shard_map(
        local,
        mesh=mesh,
        in_specs=placed,
        out_specs=(
            P("dp", None),
            P("dp", None),
            P(None, "tensor"),
            P(),
            P(),
            P("tensor", None),
            P(None, "tensor"),
            P(None, "tensor"),
            P("tensor", None),
            P(),
            P(),
            P(),
            P(),
            P(),
            P(),
        ),
        check_vma=False,
    )
```

time: 248 us -> 174 us (0.70)
  matrix products: 28.7 us -> 0 us
  other arithmetic: 31.8 us -> 3.73 us
  Pallas kernels: 142 us -> 167 us
  local copies, waits for them, and re-layouts: 23.1 us -> 2.84 us
  waiting for transfers between devices: 10.4 us -> 0 us
  starting transfers between devices: 8.78 us -> 0 us
    dot_general x26 -> x0, matrix products: 28.7 us -> none  [the longest x2 3.82 us: block_forward(): jnp.einsum('hqd,kd->hqk', q_block, k_window, preferred_element_type=jnp.f...]
    pallas_call x3, Pallas kernels: 142 us -> 167 us  [the longest x1 84.6 us: backward_part(): pl.pallas_call(backward_kernel, out_shape=(sds(blocks, BF), sds((4, 8, 22...]
    all_to_all x2 -> x0, waiting for transfers between devices: 10.4 us -> none  [the longest x1 10.4 us: sum_at_owner(): tiles = lax.all_to_all(in_blocks(x, dim, size), axis, 0, 0, tiled=True)]
    all_to_all x2 -> x0, starting transfers between devices: 8.78 us -> none  [the longest x1 4.4 us: sum_at_owner(): tiles = lax.all_to_all(in_blocks(x, dim, size), axis, 0, 0, tiled=True)]
    while x20 -> x0, local copies, waits for them, and re-layouts: 8.52 us -> none
    reduce_sum x8 -> x0, other arithmetic: 7.6 us -> none  [the longest x2 2.86 us: rms_scale(): jnp.mean(values * values, axis=-1, keepdims=True) + EPSILON]
    another operation x6 -> x0, other arithmetic: 6.79 us -> none
    reshape x6 -> x0, local copies, waits for them, and re-layouts: 5.35 us -> none  [the longest x1 1.27 us: ffn_block(): g_ao.reshape(1, 640)]
  transfers between devices with their start and end apart: 2 -> 0, of which waited for: 1 -> 0; matrix products, arithmetic and copies ran while one was open for 7% -> 0% of each run, Pallas kernels for 28% -> 0%
where the time goes in v3:
time: 174 us
  Pallas kernels  167 us (96%)
  other arithmetic  3.73 us (2%)
  local copies, waits for them, and re-layouts  2.84 us (2%)
    pallas_call x1, Pallas kernels, backward_part(): pl.pallas_call(backward_kernel, out_shape=(sds(blocks, BF), sds((4, 8, 22...  84.6 us
    pallas_call x1, Pallas kernels, forward_part(): pl.pallas_call(forward_kernel, out_shape=(sds(blocks, BF), sds(blocks, BF...  77.2 us
    pallas_call x1, Pallas kernels, backward_part(): pl.pallas_call(unpack_kernel, out_shape=(sds((640, 256), F32), sds((640,...  5.05 us

profile of v3, /device:TPU:1, one launch (start us, length us, event | category | flops | bytes accessed | tf_op | source)
XLA Modules:
  0.0 174.1 jit_solution(7393551403678734656)
XLA Ops:
  0.7 0.7 convert_element_type.3
  1.4 3.0 %multiply_sine_fusion = (f32[1024,128]{1,0:T(8,128)}, f32[1024,128]{1,0:T(8,128)}) fusion(f32[128]{0:T(128)S(1)} %multiply_power_fusion, f32[1024]{0:T(1024)S(1)} %convert_element_type.3), kind=kLoop, calls=%fused_computation | loop fusion | flops 131072 | bytes 1053184 | tf_op jit(solution)/shard_map/sin | solution.py:585
  4.4 77.2 %forward_part.1 = (bf16[4,4,64,640]{3,2,1,0:T(8,128)(2,1)}, bf16[4,4,64,640]{3,2,1,0:T(8,128)(2,1)}, f32[4,64,640]{2,1,0:T(8,128)}, bf16[4,8,224,128]{3,2,1,0:T(...) custom-call(bf16[4,4,64,640]{3,2,1,0:T(8,128)(2,1)} %bitcast.5, ...), custom_call_target="tpu_custom_call" | custom-call | tf_op jit(solution)/shard_map/forward_part/pallas_call | solution.py:353
  81.6 84.6 %backward_part.1 = (bf16[4,4,64,640]{3,2,1,0:T(8,128)(2,1)}, bf16[4,8,224,128]{3,2,1,0:T(8,128)(2,1)}, bf16[8,112,128]{2,1,0:T(8,128)(2,1)}, bf16[8,112,128]{2,1...) custom-call(bf16[4,4,64,640]{3,2,1,0:T(8,128)(2,1)} %get-tuple-eleme, ...), custom_call_target="tpu_custom_call" | custom-call | tf_op jit(solution)/shard_map/backward_part/pallas_call | solution.py:547
  166.2 0.0 copy-start
  166.2 5.1 %unpack_grads.1 = (f32[640,256]{1,0:T(8,128)}, f32[640,256]{1,0:T(8,128)}, f32[640,256]{1,0:T(8,128)}, f32[256,640]{1,0:T(8,128)}, f32[640,512]{1,0:T(8,128)}, /...) custom-call(bf16[4,8,224,128]{3,2,1,0:T(8,128)(2,1)} %get-tuple-elem, ...), custom_call_target="tpu_custom_call" | custom-call | tf_op jit(solution)/shard_map/unpack_grads/pallas_call | solution.py:567
  171.3 0.0 copy-done
  171.3 0.0 copy-start.1
  171.3 1.1 copy.34
  172.4 0.7 copy-done.1
  173.1 1.1 copy.35
  (1 shorter events, 0.0 us)
Async XLA Ops:
  166.2 5.1 %copy-start = (bf16[4,4,64,640]{3,2,1,0:T(8,128)(2,1)S(1)}, bf16[4,4,64,640]{3,2,1,0:T(8,128)(2,1)}, u32[]{:S(2)}) copy-start(bf16[4,4,64,640]{3,2,1,0:T(8,128)(2,1)} %get-tuple-element.50) | copy-start | bytes 3932164
  171.3 1.8 %copy-start.1 = (bf16[4,4,64,640]{3,2,1,0:T(8,128)(2,1)S(1)}, bf16[4,4,64,640]{3,2,1,0:T(8,128)(2,1)}, u32[]{:S(2)}) copy-start(bf16[4,4,64,640]{3,2,1,0:T(8,128)(2,1)} %get-tuple-element.64) | copy-start | bytes 3932164

commit v4 on v3

v4 whole, which is shorter than its diff:
```python
import jax, jax.numpy as jnp
from jax import lax
from jax.experimental import pallas as pl
from jax.experimental.pallas import tpu as pltpu
from jax.sharding import PartitionSpec as P

WINDOW = 512
EPSILON = 1e-06
ROPE_BASE = 10000.0
NEG_LARGE = -1e30

MESH = pl.DeviceIdType.MESH
BF = jnp.bfloat16
F32 = jnp.float32
VMEM = pl.BlockSpec(memory_space=pltpu.VMEM)
VMEM_LIMIT = 60 * 1024 * 1024


def neighbours():
    dp = lax.axis_index("dp")
    t = lax.axis_index("tensor")
    z = lax.rem(dp, 4)
    y = lax.rem(dp // 4, 4)
    xh = dp // 16
    xl = t // 2
    core = lax.rem(t, 2)
    ya = y + 1 - 2 * lax.rem(y, 2)
    za = z + 1 - 2 * lax.rem(z, 2)
    links = [
        (dp + (ya - y) * 4, t),
        (dp + (za - z), t),
        (dp + (3 - 2 * y) * 4, t),
        (dp + (3 - 2 * z), t),
    ]
    bits = [lax.rem((y + 1) // 2, 2), lax.rem((z + 1) // 2, 2), y // 2, z // 2]
    across = (dp + 16 - 32 * xh, t)
    sibling = (dp, t + 1 - 2 * core)
    beside = (dp, t + 2 - 4 * xl)
    return links, bits, across, sibling, beside, xl, core


def greet(devices):
    barrier = pltpu.get_barrier_semaphore()
    for d in devices:
        pl.semaphore_signal(barrier, inc=1, device_id=d, device_id_type=MESH)
    pl.semaphore_wait(barrier, len(devices))


def send(src, dst, ssem, rsem, device):
    copy = pltpu.make_async_remote_copy(
        src_ref=src, dst_ref=dst, send_sem=ssem, recv_sem=rsem, device_id=device, device_id_type=MESH
    )
    copy.start()
    return copy


class Reduction:
    def __init__(self, ins, bufs, recvs, outs, ssem, rsem, links, bits, across):
        self.ins, self.bufs, self.recvs, self.outs, self.ssem, self.rsem = ins, bufs, recvs, outs, ssem, rsem
        self.links, self.bits, self.across = links, bits, across
        self.base = [jnp.int32(0)] * 4
        self.bases = []
        self.copies = None

    def start(self, step):
        copies = []
        for p in range(4):
            buf, recv = (self.ins if step == 0 else self.bufs)[p], self.recvs[p]
            ss, rs = self.ssem.at[p, step], self.rsem.at[p, step]
            if step < 3:
                n = 4 >> step
                bit = self.bits[(p + step) % 4]
                there = self.base[p] + (1 - bit) * n
                self.base[p] = self.base[p] + bit * n
                at = (0, 4, 6)[step]
                src, dst, dev = buf.at[pl.ds(there, n)], recv.at[pl.ds(at, n)], self.links[(p + step) % 4]
            elif step < 5:
                dev = self.links[(p + 3) % 4] if step == 3 else self.across
                src, dst = buf.at[pl.ds(self.base[p], 1)], recv.at[pl.ds(4 + step, 1)]
            else:
                s = 7 - step
                n = 4 >> s
                bit = self.bits[(p + s) % 4]
                src = dst = self.outs[p].at[pl.ds(self.base[p], n)]
                self.base[p] = self.base[p] - bit * n
                dev = self.links[(p + s) % 4]
            copies.append(send(src, dst, ss, rs, dev))
        self.copies = copies

    def finish(self, step):
        for p in range(4):
            buf, recv = self.bufs[p], self.recvs[p]
            into = self.outs[p] if step == 4 else buf
            buf = self.ins[p] if step == 0 else buf
            self.copies[p].wait()
            if step < 5:
                n = (4, 2, 1, 1, 1)[step]
                at = (0, 4, 6, 7, 8)[step]
                base = self.base[p]

                def add(i, carry):
                    into[base + i] = (buf[base + i].astype(F32) + recv[at + i].astype(F32)).astype(BF)
                    return carry

                lax.fori_loop(0, n, add, 0)


NC = 4
CR = 1024 // NC
OW = CR // 2
C0 = 0.7978845608028654
C1 = 0.044715


def nt(a, b):
    return lax.dot_general(a, b, (((1,), (1,)), ((), ())), preferred_element_type=F32)


def tn(a, b):
    return lax.dot_general(a, b, (((0,), (0,)), ((), ())), preferred_element_type=F32)


def nn(a, b):
    return jnp.dot(a, b, preferred_element_type=F32)


def inv_rms(v):
    return lax.rsqrt(jnp.mean(v * v, axis=-1, keepdims=True) + EPSILON)


def rms_back(v, r, du):
    return r * du - v * (r * r * r * jnp.mean(du * v, axis=-1, keepdims=True))


def turn(v, cosine, sine):
    a, b = v[:, :128], v[:, 128:]
    return jnp.concatenate([a * cosine - b * sine, b * cosine + a * sine], axis=-1)


def turn_back(v, cosine, sine):
    a, b = v[:, :128], v[:, 128:]
    return jnp.concatenate([a * cosine + b * sine, b * cosine - a * sine], axis=-1)


def key_range(i):
    first = max(0, (i - 2) * CR)
    return first, (i + 1) * CR - first


def vec(g):
    return g[...]


class KeyValue:
    def __init__(self, kv, work, recv, last, out, ssem, rsem, links, bits, across, sibling, beside, xl, core):
        self.kv, self.work, self.recv, self.last, self.out, self.ssem, self.rsem = kv, work, recv, last, out, ssem, rsem
        self.xl, self.core = xl, core
        self.mine = core * 2 + xl
        self.b0, self.b1 = bits[0], bits[1]
        self.at = self.b0 * 2 + self.b1
        self.devices = [sibling, beside, links[0], links[1], links[2], links[3], across, links[1], links[0], beside, sibling]

    def start(self, step):
        work, recv, last, out, at, b0, mine = self.work, self.recv, self.last, self.out, self.at, self.b0, self.mine
        if step == 0:
            src, dst = self.kv.at[pl.ds((1 - self.core) * 2, 2)], recv.at[pl.ds(0, 2)]
        elif step == 1:
            src, dst = work.at[1 - self.xl], recv.at[2]
        elif step == 2:
            src, dst = last.at[pl.ds((1 - b0) * 2, 2)], recv.at[3, pl.ds(0, 2)]
        elif step == 3:
            src, dst = last.at[b0 * 2 + 1 - self.b1], recv.at[3, 2]
        elif step == 4:
            src, dst = last.at[at], recv.at[3, 3]
        elif step < 7:
            src, dst = last.at[at], recv.at[4, step - 5]
        elif step == 7:
            src = dst = out.at[mine, at]
        elif step == 8:
            src = dst = out.at[mine, pl.ds(b0 * 2, 2)]
        elif step == 9:
            src = dst = out.at[mine]
        else:
            src = dst = out.at[pl.ds(self.core * 2, 2)]
        self.copy = send(src, dst, self.ssem.at[step], self.rsem.at[step], self.devices[step])

    def finish(self, step):
        self.copy.wait()
        kv, work, recv, last, at = self.kv, self.work, self.recv, self.last, self.at
        if step == 0:
            for i in range(2):
                work[i] = (kv[self.core * 2 + i].astype(F32) + recv[i].astype(F32)).astype(BF)
        elif step == 1:
            last[...] = (work[self.xl].astype(F32) + recv[2].astype(F32)).astype(BF)
        elif step == 2:
            for i in range(2):
                last[self.b0 * 2 + i] = (last[self.b0 * 2 + i].astype(F32) + recv[3, i].astype(F32)).astype(BF)
        elif step < 5:
            last[at] = (last[at].astype(F32) + recv[3, step - 1].astype(F32)).astype(BF)
        elif step == 5:
            last[at] = (last[at].astype(F32) + recv[4, 0].astype(F32)).astype(BF)
        elif step == 6:
            self.out[self.mine, at] = (last[at].astype(F32) + recv[4, 1].astype(F32)).astype(BF)


def layer_kernel(x, cot, segs, cos_t, sin_t, wq, wk, wv, wo, wg, wu, wd, g_in, g_ao, g_fi, g_fo, g_q, g_k,
                 output, in_grad, a_out, o0, o1, o2, o3, kv_out, gains,
                 normed, q_raw, k_raw, q, k, v, prob, heads, part, ffn_g, dffn_g, dattn, hid, act_a, act_b, dgate, dup,
                 attn_own, mid_own, recv_a, recv_b, dk, dv, dqkv,
                 a_buf, b0, b1, b2, b3, a_recv, r0, r1, r2, r3, kv, kv_work, kv_recv, kv_last, g_recv,
                 ssem, rsem, a_ss, a_rs, b_ss, b_rs, k_ss, k_rs, g_ss, g_rs):
    links, bits, across, sibling, beside, xl, core = neighbours()
    greet(links + [across, sibling, beside])
    own = core
    state = [dict() for _ in range(NC)]
    used = [0]

    def post(src, dst, device):
        i = used[0]
        used[0] += 1
        return send(src, dst, ssem.at[i], rsem.at[i], device)

    def share(e, c):
        state[c]["a"] = post(part.at[e, c, 1 - own], recv_a.at[e, c], sibling)

    def exchange(e):
        def run(c):
            state[c]["a"].wait()
            part[e, c, own] = (part[e, c, own].astype(F32) + recv_a[e, c].astype(F32)).astype(BF)
            state[c]["b"] = post(part.at[e, c, own], recv_b.at[e, c], beside)
        return run

    def total(e, c):
        state[c]["b"].wait()
        return part[e, c, own].astype(F32) + recv_b[e, c].astype(F32)

    def give(buf, c):
        return post(buf.at[c, own], buf.at[c, own], sibling)

    def keys_stage():
        for c in range(NC - 1, -1, -1):
            rows = slice(c * CR, c * CR + CR)
            xv = x[c].reshape(CR, 640).astype(F32)
            n = (xv * inv_rms(xv) * vec(g_in)).astype(BF)
            normed[rows] = n
            raw = nn(n, wk[...])
            k_raw[rows] = raw
            k[rows] = turn(raw * inv_rms(raw) * vec(g_k), cos_t[rows], sin_t[rows]).astype(BF)
            v[rows] = nn(n, wv[...]).astype(BF)

    def attention_stage(c):
        rows = slice(c * CR, c * CR + CR)
        raw = nn(normed[rows], wq[...])
        q_raw[rows] = raw
        q_low = turn(raw * inv_rms(raw) * vec(g_q), cos_t[rows], sin_t[rows]).astype(BF)
        q[rows] = q_low
        first, size = key_range(c)
        keys = slice(first, first + size)
        scores = nt(q_low, k[keys]) * 0.0625
        gap = c * CR - first + lax.broadcasted_iota(jnp.int32, (CR, size), 0) - lax.broadcasted_iota(jnp.int32, (CR, size), 1)
        seg_rows = jnp.broadcast_to(segs[:, rows], (128, CR)).T[:, :1]
        allowed = (gap >= 0) & (gap < WINDOW) & (seg_rows == segs[:, keys])
        masked = jnp.where(allowed, scores, NEG_LARGE)
        e = jnp.where(allowed, jnp.exp(masked - jnp.max(masked, axis=-1, keepdims=True)), 0.0)
        p = e / jnp.sum(e, axis=-1, keepdims=True)
        prob[c, :, 0:size] = p
        h = nn(p.astype(BF), v[keys]).astype(BF)
        heads[rows] = h
        part[0, c] = nn(h, wo[...]).astype(BF).reshape(2, OW, 640)
        share(0, c)

    def mid_stage(c):
        a = total(0, c)
        attn_own[c] = a
        mid = x[c, own].astype(F32) + a * inv_rms(a) * vec(g_ao)
        mid_own[c] = mid
        ffn_g[c, own] = (mid * inv_rms(mid) * vec(g_fi)).astype(BF)
        state[c]["g"] = give(ffn_g, c)

    def up_stage(c):
        state[c]["g"].wait()
        f = ffn_g[c].reshape(CR, 640)
        gate = nn(f, wg[...])
        up = nn(f, wu[...])
        th = jnp.tanh(C0 * (gate + C1 * gate * gate * gate))
        half = 0.5 * (1.0 + th)
        act = gate * half
        slope = half + 0.5 * gate * (1.0 - th * th) * (C0 * (1.0 + 3.0 * C1 * gate * gate))
        act_a[c] = up * slope
        act_b[c] = act
        h = (act * up).astype(BF)
        hid[c] = h
        part[1, c] = nn(h, wd[...]).astype(BF).reshape(2, OW, 640)
        share(1, c)

    def out_stage(c):
        s = total(1, c)
        r = inv_rms(s)
        ct = cot[c, own].astype(F32)
        dffn_g[c, own] = rms_back(s, r, ct * vec(g_fo)).astype(BF)
        state[c]["g"] = give(dffn_g, c)
        output[c, own] = (mid_own[c] + s * r * vec(g_fo)).astype(BF)
        state[c]["o"] = give(output, c)
        gains[2:3, :] = gains[2:3, :] + jnp.sum(ct * s * r, axis=0, keepdims=True)

    def down_stage(c):
        state[c]["g"].wait()
        d = dffn_g[c].reshape(CR, 640)
        dh = nt(d, wd[...])
        dg = (dh * act_a[c]).astype(BF)
        du = (dh * act_b[c]).astype(BF)
        dgate[c] = dg
        dup[c] = du
        part[2, c] = (nt(dg, wg[...]) + nt(du, wu[...])).astype(BF).reshape(2, OW, 640)
        share(2, c)

    def attn_stage(c):
        d = total(2, c)
        mid, a = mid_own[c], attn_own[c]
        r = inv_rms(mid)
        gains[1:2, :] = gains[1:2, :] + jnp.sum(d * mid * r, axis=0, keepdims=True)
        dmid = cot[c, own].astype(F32) + rms_back(mid, r, d * vec(g_fi))
        mid_own[c] = dmid
        r = inv_rms(a)
        gains[0:1, :] = gains[0:1, :] + jnp.sum(dmid * a * r, axis=0, keepdims=True)
        dattn[c, own] = rms_back(a, r, dmid * vec(g_ao)).astype(BF)
        state[c]["g"] = give(dattn, c)

    def back_stage(i):
        state[i]["g"].wait()
        rows = slice(i * CR, i * CR + CR)
        start, size = key_range(i)
        dh = nt(dattn[i].reshape(CR, 640), wo[...]).astype(BF)
        p = prob[i, :, 0:size]
        dp = nt(dh, v[start:start + size])
        ds = (p * (dp - jnp.sum(p * dp, axis=-1, keepdims=True))).astype(BF)
        dq = nn(ds, k[start:start + size]) * 0.0625
        dk_add = tn(ds, q[rows]) * 0.0625
        dv_add = tn(p.astype(BF), dh)
        fresh = size if i == NC - 1 else (CR if i == NC - 2 else 0)
        if fresh:
            dk[start:start + fresh] = dk_add[:fresh]
            dv[start:start + fresh] = dv_add[:fresh]
        if fresh < size:
            dk[start + fresh:start + size] = dk[start + fresh:start + size] + dk_add[fresh:]
            dv[start + fresh:start + size] = dv[start + fresh:start + size] + dv_add[fresh:]
        cosine, sine = cos_t[rows], sin_t[rows]
        raws = []
        for d, raw, g, at in ((dq, q_raw[rows], g_q, 0), (dk[rows], k_raw[rows], g_k, 256)):
            du = turn_back(d, cosine, sine)
            r = inv_rms(raw)
            gains[4:5, at:at + 256] = gains[4:5, at:at + 256] + jnp.sum(du * raw * r, axis=0, keepdims=True)
            raws.append(rms_back(raw, r, du * vec(g)).astype(BF))
        raws.append(dv[rows].astype(BF))
        for j in range(3):
            dqkv[rows, 256 * j:256 * j + 256] = raws[j]
        term = nt(raws[0], wq[...]) + nt(raws[1], wk[...]) + nt(raws[2], wv[...])
        part[3, i] = term.astype(BF).reshape(2, OW, 640)
        share(3, i)

    def in_stage(i):
        d = total(3, i)
        xv = x[i, own].astype(F32)
        r = inv_rms(xv)
        gains[3:4, :] = gains[3:4, :] + jnp.sum(d * xv * r, axis=0, keepdims=True)
        in_grad[i, own] = (mid_own[i] + rms_back(xv, r, d * vec(g_in))).astype(BF)
        state[i]["g"] = give(in_grad, i)

    def weights_down():
        g = tn(hid[...].reshape(1024, 512), dffn_g[...].reshape(1024, 640)).astype(BF)
        for s in range(8):
            for p in range(4):
                a_buf[p, s, 160:224] = g[64 * s:64 * s + 64, 128 * p:128 * p + 128]
            b2[s, 0:64] = g[64 * s:64 * s + 64, 512:640]

    def weights_ffn(source, at):
        g = tn(ffn_g[...].reshape(1024, 640), source[...].reshape(1024, 512)).astype(BF)
        for s in range(8):
            for p in range(4):
                a_buf[p, s, at:at + 80] = g[80 * s:80 * s + 80, 128 * p:128 * p + 128]

    def weights_out():
        g = tn(heads[...], dattn[...].reshape(1024, 640)).astype(BF)
        for c in range(8):
            rows = slice(32 * c, 32 * c + 32)
            b0[c, 80:112] = g[rows, 0:128]
            b1[c, 80:112] = g[rows, 128:256]
            b2[c, 64:96] = g[rows, 256:384]
            b3[c, 0:32] = g[rows, 384:512]
            b3[c, 32:64] = g[rows, 512:640]

    def weights_in():
        g = tn(normed[...], dqkv[...]).astype(BF)
        for j in range(4):
            kv[j] = g[:, 256 + 128 * j:384 + 128 * j].reshape(4, 160, 128)
        for c in range(8):
            b0[c, 0:80] = g[80 * c:80 * c + 80, 0:128]
            b1[c, 0:80] = g[80 * c:80 * c + 80, 128:256]

    bufs = [a_buf.at[p] for p in range(4)]
    first = Reduction(bufs, bufs, [a_recv.at[p] for p in range(4)], [a_out.at[p] for p in range(4)], a_ss, a_rs, links, bits, across)
    bufs = [b0, b1, b2, b3]
    second = Reduction(bufs, bufs, [r0, r1, r2, r3], [o0, o1, o2, o3], b_ss, b_rs, links, bits, across)
    third = KeyValue(kv, kv_work, kv_recv, kv_last, kv_out, k_ss, k_rs, links, bits, across, sibling, beside, xl, core)
    done = {}

    def begin(red):
        red.start(0)
        done[id(red)] = 0

    def advance(red, steps):
        at = done[id(red)]
        if at < steps:
            red.finish(at)
            at += 1
            if at < steps:
                red.start(at)
            done[id(red)] = at

    gains[...] = jnp.zeros_like(gains)
    keys_stage()
    stages = [
        attention_stage, exchange(0), mid_stage, up_stage, exchange(1), out_stage, down_stage, exchange(2), attn_stage,
        back_stage, exchange(3), in_stage,
    ]
    after = AFTER
    for tick in range(len(stages) + NC - 1):
        for p in range(NC):
            s = tick - p
            if 0 <= s < len(stages):
                stages[s](NC - 1 - p)
                for job in after.get((s, p), ()):
                    if job == "down":
                        weights_down()
                    elif job == "gate":
                        weights_ffn(dgate, 0)
                    elif job == "up":
                        weights_ffn(dup, 80)
                        begin(first)
                    elif job == "out":
                        weights_out()
                    elif job == "in":
                        weights_in()
                        begin(third)
                        begin(second)
                    elif job == "1":
                        advance(first, 8)
                    elif job == "2":
                        advance(second, 8)
                    elif job == "3":
                        advance(third, 11)
    gains[0:4, :] = gains[0:4, :] * 0.5
    order = [sibling, beside] + links + [across]
    for i in range(11):
        if i < 7:
            gc = send(gains, g_recv.at[i], g_ss.at[i], g_rs.at[i], order[i])
        advance(third, 11)
        advance(second, 8)
        advance(first, 8)
        if i < 7:
            gc.wait()
            gains[...] = gains[...] + g_recv[i]
    for c in range(NC):
        state[c]["o"].wait()
        state[c]["g"].wait()


AFTER = {
    (6, 3): ("down", "gate", "up"),
    (9, 1): ("1",),
    (9, 2): ("1",),
    (9, 3): ("out", "in", "1"),
    (10, 3): ("1", "3"),
    (11, 2): ("2", "3"),
    (11, 3): ("1", "2", "3"),
}


def unpack_kernel(a, b0, b1, b2, b3, kv, gains, query, key, value, out, gate, up, down, g0, g1, g2, g3, g4, g5):
    for p in range(4):
        cols = slice(128 * p, 128 * p + 128)
        for c in range(8):
            gate[80 * c:80 * c + 80, cols] = a[p, c, 0:80].astype(F32)
            up[80 * c:80 * c + 80, cols] = a[p, c, 80:160].astype(F32)
            down[64 * c:64 * c + 64, cols] = a[p, c, 160:224].astype(F32)
    for c in range(8):
        for p, b in ((0, b0), (1, b1)):
            query[80 * c:80 * c + 80, 128 * p:128 * p + 128] = b[c, 0:80].astype(F32)
            out[32 * c:32 * c + 32, 128 * p:128 * p + 128] = b[c, 80:112].astype(F32)
        out[32 * c:32 * c + 32, 256:384] = b2[c, 64:96].astype(F32)
        down[64 * c:64 * c + 64, 512:640] = b2[c, 0:64].astype(F32)
        out[32 * c:32 * c + 32, 384:512] = b3[c, 0:32].astype(F32)
        out[32 * c:32 * c + 32, 512:640] = b3[c, 32:64].astype(F32)
    for j in range(2):
        key[:, 128 * j:128 * j + 128] = kv[j].reshape(640, 128).astype(F32)
        value[:, 128 * j:128 * j + 128] = kv[2 + j].reshape(640, 128).astype(F32)
    for i, g in ((3, g0), (0, g1), (1, g2), (2, g3)):
        g[...] = gains[i, :]
    g4[...] = gains[4, 0:256]
    g5[...] = gains[4, 256:512]


def layer(*operands):
    sds = jax.ShapeDtypeStruct
    dma = pltpu.SemaphoreType.DMA
    v = pltpu.VMEM
    blocks = (NC, 2, OW, 640)
    half = (NC, OW, 640)
    count = NC * 12
    stacks = pl.pallas_call(
        layer_kernel,
        out_shape=(sds(blocks, BF), sds(blocks, BF), sds((4, 8, 224, 128), BF), sds((8, 112, 128), BF), sds((8, 112, 128), BF),
                   sds((8, 96, 128), BF), sds((8, 64, 128), BF), sds((4, 4, 160, 128), BF), sds((8, 640), F32)),
        in_specs=[VMEM] * len(operands),
        out_specs=[VMEM] * 9,
        scratch_shapes=[
            v((1024, 640), BF), v((1024, 256), F32), v((1024, 256), F32), v((1024, 256), BF), v((1024, 256), BF),
            v((1024, 256), BF), v((NC, CR, 768), F32), v((1024, 256), BF), v((4, *blocks), BF), v(blocks, BF), v(blocks, BF),
            v(blocks, BF), v((NC, CR, 512), BF), v((NC, CR, 512), F32), v((NC, CR, 512), F32), v((NC, CR, 512), BF),
            v((NC, CR, 512), BF), v(half, F32), v(half, F32), v((4, *half), BF), v((4, *half), BF),
            v((1024, 256), F32), v((1024, 256), F32), v((1024, 768), BF),
            v((4, 8, 224, 128), BF),
            v((8, 112, 128), BF), v((8, 112, 128), BF), v((8, 96, 128), BF), v((8, 64, 128), BF),
            v((4, 9, 224, 128), BF),
            v((9, 112, 128), BF), v((9, 112, 128), BF), v((9, 96, 128), BF), v((9, 64, 128), BF),
            v((4, 4, 160, 128), BF), v((2, 4, 160, 128), BF), v((5, 4, 160, 128), BF), v((4, 160, 128), BF),
            v((7, 8, 640), F32),
            dma((count + 16,)), dma((count + 16,)),
            dma((4, 8)), dma((4, 8)), dma((4, 8)), dma((4, 8)), dma((11,)), dma((11,)), dma((7,)), dma((7,)),
        ],
        compiler_params=pltpu.CompilerParams(collective_id=7, has_side_effects=True, vmem_limit_bytes=VMEM_LIMIT),
        name="layer",
    )(*operands)
    outs = pl.pallas_call(
        unpack_kernel,
        out_shape=(sds((640, 256), F32), sds((640, 256), F32), sds((640, 256), F32), sds((256, 640), F32),
                   sds((640, 512), F32), sds((640, 512), F32), sds((512, 640), F32),
                   sds((640,), F32), sds((640,), F32), sds((640,), F32), sds((640,), F32),
                   sds((256,), F32), sds((256,), F32)),
        in_specs=[VMEM] * 7,
        out_specs=[VMEM] * 13,
        compiler_params=pltpu.CompilerParams(vmem_limit_bytes=VMEM_LIMIT),
        name="unpack_grads",
    )(*stacks[2:])
    return stacks[0], stacks[1], outs


def rope_tables(positions, head_size):
    half_size = head_size // 2
    inv_freq = ROPE_BASE ** (-2.0 * jnp.arange(half_size, dtype=jnp.float32) / head_size)
    angles = positions.astype(jnp.float32)[:, None] * inv_freq[None, :]
    return (jnp.cos(angles), jnp.sin(angles))


def local(
    inputs,
    segments,
    positions,
    cotangent,
    w_query,
    w_key,
    w_value,
    w_out,
    w_gate,
    w_up,
    w_down,
    g_attn_in,
    g_attn_out,
    g_ffn_in,
    g_ffn_out,
    g_query,
    g_key,
):
    blocks = (NC, 2, OW, 640)
    cos_t, sin_t = rope_tables(positions, 256)
    output, input_grad, summed = layer(
        inputs.reshape(blocks), cotangent.reshape(blocks), segments.reshape(1, 1024), cos_t, sin_t,
        w_query, w_key, w_value, w_out, w_gate, w_up, w_down,
        g_attn_in, g_attn_out, g_ffn_in, g_ffn_out, g_query, g_key,
    )
    return (output.reshape(1024, 640), input_grad.reshape(1024, 640), *summed)


def solution(mesh):
    placed = (
        P("dp", None),
        P("dp"),
        P("dp"),
        P("dp", None),
        P(None, "tensor"),
        P(),
        P(),
        P("tensor", None),
        P(None, "tensor"),
        P(None, "tensor"),
        P("tensor", None),
        P(),
        P(),
        P(),
        P(),
        P(),
        P(),
    )
    return jax.shard_map(
        local,
        mesh=mesh,
        in_specs=placed,
        out_specs=(
            P("dp", None),
            P("dp", None),
            P(None, "tensor"),
            P(),
            P(),
            P("tensor", None),
            P(None, "tensor"),
            P(None, "tensor"),
            P("tensor", None),
            P(),
            P(),
            P(),
            P(),
            P(),
            P(),
        ),
        check_vma=False,
    )
```

time: 174 us -> 145 us (0.83)
  Pallas kernels: 167 us -> 137 us
    pallas_call x3 -> x2, Pallas kernels: 167 us -> 137 us  [the longest x1 132 us: layer(): pl.pallas_call(layer_kernel, out_shape=(sds(blocks, BF), sds(blocks, BF),...]
where the time goes in v4:
time: 145 us; the launch traced here: 144 us
  Pallas kernels  137 us (94%)
  other arithmetic  3.73 us (3%)
  local copies, waits for them, and re-layouts  2.84 us (2%)
    pallas_call x1, Pallas kernels, layer(): pl.pallas_call(layer_kernel, out_shape=(sds(blocks, BF), sds(blocks, BF),...  132 us
    pallas_call x1, Pallas kernels, layer(): pl.pallas_call(unpack_kernel, out_shape=(sds((640, 256), F32), sds((640,...  5 us
    sin x1, other arithmetic, rope_tables(): return (jnp.cos(angles), jnp.sin(angles))  3.03 us

profile of v4, /device:TPU:1, one launch (start us, length us, event | category | flops | bytes accessed | tf_op | source)
XLA Modules:
  0.0 144.2 jit_solution(16267171043451602523)
XLA Ops:
  0.7 0.7 convert_element_type.3
  1.4 3.0 %multiply_sine_fusion = (f32[1024,128]{1,0:T(8,128)}, f32[1024,128]{1,0:T(8,128)}) fusion(f32[128]{0:T(128)S(1)} %multiply_power_fusion, f32[1024]{0:T(1024)S(1)} %convert_element_type.3), kind=kLoop, calls=%fused_computation | loop fusion | flops 131072 | bytes 1053184 | tf_op jit(solution)/shard_map/sin | solution.py:552
  4.4 132.0 %layer.1 = (bf16[4,2,128,640]{3,2,1,0:T(8,128)(2,1)}, bf16[4,2,128,640]{3,2,1,0:T(8,128)(2,1)}, bf16[4,8,224,128]{3,2,1,0:T(8,128)(2,1)}, bf16[8,112,128]{2,1,0:...) custom-call(bf16[4,2,128,640]{3,2,1,0:T(8,128)(2,1)} %bitcast.7, ...), custom_call_target="tpu_custom_call" | custom-call | tf_op jit(solution)/shard_map/layer/pallas_call | solution.py:510
  136.4 0.0 copy-start.1
  136.4 5.0 %unpack_grads.1 = (f32[640,256]{1,0:T(8,128)}, f32[640,256]{1,0:T(8,128)}, f32[640,256]{1,0:T(8,128)}, f32[256,640]{1,0:T(8,128)}, f32[640,512]{1,0:T(8,128)}, /...) custom-call(bf16[4,8,224,128]{3,2,1,0:T(8,128)(2,1)} %get-tuple-elem, ...), custom_call_target="tpu_custom_call" | custom-call | tf_op jit(solution)/shard_map/unpack_grads/pallas_call | solution.py:534
  141.4 0.0 copy-done.1
  141.4 0.0 copy-start
  141.4 1.1 copy.34
  142.5 0.7 copy-done
  143.2 1.1 copy.35
  (1 shorter events, 0.0 us)
Async XLA Ops:
  136.4 5.0 %copy-start.1 = (bf16[4,2,128,640]{3,2,1,0:T(8,128)(2,1)S(1)}, bf16[4,2,128,640]{3,2,1,0:T(8,128)(2,1)}, u32[]{:S(2)}) copy-start(bf16[4,2,128,640]{3,2,1,0:T(8,128)(2,1)} %get-tuple-element.37) | copy-start | bytes 3932164
  141.4 1.8 %copy-start = (bf16[4,2,128,640]{3,2,1,0:T(8,128)(2,1)S(1)}, bf16[4,2,128,640]{3,2,1,0:T(8,128)(2,1)}, u32[]{:S(2)}) copy-start(bf16[4,2,128,640]{3,2,1,0:T(8,128)(2,1)} %get-tuple-element.38) | copy-start | bytes 3932164

commit v5 on v4

--- a/solution.py
+++ b/solution.py
@@ -36,7 +36,8 @@
     across = (dp + 16 - 32 * xh, t)
     sibling = (dp, t + 1 - 2 * core)
     beside = (dp, t + 2 - 4 * xl)
-    return links, bits, across, sibling, beside, xl, core
+    corner = (dp + 16 - 32 * xh, t + 2 - 4 * xl)
+    return links, bits, across, sibling, beside, corner, xl, core
 
 
 def greet(devices):
@@ -55,54 +56,65 @@
 
 
 class Reduction:
-    def __init__(self, ins, bufs, recvs, outs, ssem, rsem, links, bits, across):
-        self.ins, self.bufs, self.recvs, self.outs, self.ssem, self.rsem = ins, bufs, recvs, outs, ssem, rsem
-        self.links, self.bits, self.across = links, bits, across
-        self.base = [jnp.int32(0)] * 4
-        self.bases = []
-        self.copies = None
-
-    def start(self, step):
-        copies = []
-        for p in range(4):
-            buf, recv = (self.ins if step == 0 else self.bufs)[p], self.recvs[p]
-            ss, rs = self.ssem.at[p, step], self.rsem.at[p, step]
+    def __init__(self, ids, bufs, recvs, outs, ssem, rsem, links, bits, across, more=()):
+        self.ids, self.bufs, self.recvs, self.outs, self.ssem, self.rsem = ids, bufs, recvs, outs, ssem, rsem
+        self.links, self.bits, self.across, self.more = links, bits, across, more
+        self.base = [jnp.int32(0)] * len(ids)
+        self.at = 0
+
+    def start(self):
+        step = self.at
+        self.copies = []
+        for i, p in enumerate(self.ids):
+            buf, recv = self.bufs[i], self.recvs[i]
+            ss, rs = self.ssem.at[i, step], self.rsem.at[i, step]
             if step < 3:
                 n = 4 >> step
                 bit = self.bits[(p + step) % 4]
-                there = self.base[p] + (1 - bit) * n
-                self.base[p] = self.base[p] + bit * n
+                there = self.base[i] + (1 - bit) * n
+                self.base[i] = self.base[i] + bit * n
                 at = (0, 4, 6)[step]
                 src, dst, dev = buf.at[pl.ds(there, n)], recv.at[pl.ds(at, n)], self.links[(p + step) % 4]
             elif step < 5:
                 dev = self.links[(p + 3) % 4] if step == 3 else self.across
-                src, dst = buf.at[pl.ds(self.base[p], 1)], recv.at[pl.ds(4 + step, 1)]
+                src, dst = buf.at[self.base[i]], recv.at[4 + step]
             else:
                 s = 7 - step
                 n = 4 >> s
                 bit = self.bits[(p + s) % 4]
-                src = dst = self.outs[p].at[pl.ds(self.base[p], n)]
-                self.base[p] = self.base[p] - bit * n
+                src = dst = self.outs[i].at[pl.ds(self.base[i], n)]
+                self.base[i] = self.base[i] - bit * n
                 dev = self.links[(p + s) % 4]
-            copies.append(send(src, dst, ss, rs, dev))
-        self.copies = copies
-
-    def finish(self, step):
-        for p in range(4):
-            buf, recv = self.bufs[p], self.recvs[p]
-            into = self.outs[p] if step == 4 else buf
-            buf = self.ins[p] if step == 0 else buf
-            self.copies[p].wait()
-            if step < 5:
-                n = (4, 2, 1, 1, 1)[step]
-                at = (0, 4, 6, 7, 8)[step]
-                base = self.base[p]
-
-                def add(i, carry):
-                    into[base + i] = (buf[base + i].astype(F32) + recv[at + i].astype(F32)).astype(BF)
+            self.copies.append(send(src, dst, ss, rs, dev))
+            if step == 4:
+                for j, dev in enumerate(self.more):
+                    self.copies.append(send(buf.at[self.base[i], pl.ds(0, 80)], recv.at[9 + j, pl.ds(0, 80)],
+                                            self.ssem.at[i, 8 + j], self.rsem.at[i, 8 + j], dev))
+
+    def advance(self):
+        step = self.at
+        if step == 8:
+            return
+        for copy in self.copies:
+            copy.wait()
+        if step < 5:
+            n = (4, 2, 1, 1, 1)[step]
+            at = (0, 4, 6, 7, 8)[step]
+            for i in range(len(self.ids)):
+                buf, recv, base = self.bufs[i], self.recvs[i], self.base[i]
+                into = self.outs[i] if step == 4 else buf
+
+                def add(j, carry):
+                    into[base + j] = (buf[base + j].astype(F32) + recv[at + j].astype(F32)).astype(BF)
                     return carry
 
                 lax.fori_loop(0, n, add, 0)
+                if step == 4 and self.more:
+                    pair = recv[9, 0:80].astype(F32) + recv[10, 0:80].astype(F32)
+                    into[base, 0:80] = (buf[base, 0:80].astype(F32) + recv[8, 0:80].astype(F32) + pair).astype(BF)
+        self.at = step + 1
+        if self.at < 8:
+            self.start()
 
 
 NC = 4
@@ -151,66 +163,14 @@
     return g[...]
 
 
-class KeyValue:
-    def __init__(self, kv, work, recv, last, out, ssem, rsem, links, bits, across, sibling, beside, xl, core):
-        self.kv, self.work, self.recv, self.last, self.out, self.ssem, self.rsem = kv, work, recv, last, out, ssem, rsem
-        self.xl, self.core = xl, core
-        self.mine = core * 2 + xl
-        self.b0, self.b1 = bits[0], bits[1]
-        self.at = self.b0 * 2 + self.b1
-        self.devices = [sibling, beside, links[0], links[1], links[2], links[3], across, links[1], links[0], beside, sibling]
-
-    def start(self, step):
-        work, recv, last, out, at, b0, mine = self.work, self.recv, self.last, self.out, self.at, self.b0, self.mine
-        if step == 0:
-            src, dst = self.kv.at[pl.ds((1 - self.core) * 2, 2)], recv.at[pl.ds(0, 2)]
-        elif step == 1:
-            src, dst = work.at[1 - self.xl], recv.at[2]
-        elif step == 2:
-            src, dst = last.at[pl.ds((1 - b0) * 2, 2)], recv.at[3, pl.ds(0, 2)]
-        elif step == 3:
-            src, dst = last.at[b0 * 2 + 1 - self.b1], recv.at[3, 2]
-        elif step == 4:
-            src, dst = last.at[at], recv.at[3, 3]
-        elif step < 7:
-            src, dst = last.at[at], recv.at[4, step - 5]
-        elif step == 7:
-            src = dst = out.at[mine, at]
-        elif step == 8:
-            src = dst = out.at[mine, pl.ds(b0 * 2, 2)]
-        elif step == 9:
-            src = dst = out.at[mine]
-        else:
-            src = dst = out.at[pl.ds(self.core * 2, 2)]
-        self.copy = send(src, dst, self.ssem.at[step], self.rsem.at[step], self.devices[step])
-
-    def finish(self, step):
-        self.copy.wait()
-        kv, work, recv, last, at = self.kv, self.work, self.recv, self.last, self.at
-        if step == 0:
-            for i in range(2):
-                work[i] = (kv[self.core * 2 + i].astype(F32) + recv[i].astype(F32)).astype(BF)
-        elif step == 1:
-            last[...] = (work[self.xl].astype(F32) + recv[2].astype(F32)).astype(BF)
-        elif step == 2:
-            for i in range(2):
-                last[self.b0 * 2 + i] = (last[self.b0 * 2 + i].astype(F32) + recv[3, i].astype(F32)).astype(BF)
-        elif step < 5:
-            last[at] = (last[at].astype(F32) + recv[3, step - 1].astype(F32)).astype(BF)
-        elif step == 5:
-            last[at] = (last[at].astype(F32) + recv[4, 0].astype(F32)).astype(BF)
-        elif step == 6:
-            self.out[self.mine, at] = (last[at].astype(F32) + recv[4, 1].astype(F32)).astype(BF)
-
-
 def layer_kernel(x, cot, segs, cos_t, sin_t, wq, wk, wv, wo, wg, wu, wd, g_in, g_ao, g_fi, g_fo, g_q, g_k,
                  output, in_grad, a_out, o0, o1, o2, o3, kv_out, gains,
                  normed, q_raw, k_raw, q, k, v, prob, heads, part, ffn_g, dffn_g, dattn, hid, act_a, act_b, dgate, dup,
                  attn_own, mid_own, recv_a, recv_b, dk, dv, dqkv,
-                 a_buf, b0, b1, b2, b3, a_recv, r0, r1, r2, r3, kv, kv_work, kv_recv, kv_last, g_recv,
-                 ssem, rsem, a_ss, a_rs, b_ss, b_rs, k_ss, k_rs, g_ss, g_rs):
-    links, bits, across, sibling, beside, xl, core = neighbours()
-    greet(links + [across, sibling, beside])
+                 a_buf, b0, b1, b2, b3, a_recv, r0, r1, r2, r3, kv, kv_recv, g_recv,
+                 ssem, rsem, a_ss, a_rs, b_ss, b_rs, c_ss, c_rs, k_ss, k_rs, g_ss, g_rs):
+    links, bits, across, sibling, beside, corner, xl, core = neighbours()
+    greet(links + [across, sibling, beside, corner])
     own = core
     state = [dict() for _ in range(NC)]
     used = [0]
@@ -354,6 +314,9 @@
         raws.append(dv[rows].astype(BF))
         for j in range(3):
             dqkv[rows, 256 * j:256 * j + 256] = raws[j]
+        if i == 0:
+            weights_out()
+            weights_in()
         term = nt(raws[0], wq[...]) + nt(raws[1], wk[...]) + nt(raws[2], wv[...])
         part[3, i] = term.astype(BF).reshape(2, OW, 640)
         share(3, i)
@@ -371,7 +334,8 @@
         for s in range(8):
             for p in range(4):
                 a_buf[p, s, 160:224] = g[64 * s:64 * s + 64, 128 * p:128 * p + 128]
-            b2[s, 0:64] = g[64 * s:64 * s + 64, 512:640]
+            for p in range(4):
+                a_buf[p, s, 224:240] = g[128 * p + 16 * s:128 * p + 16 * s + 16, 512:640]
 
     def weights_ffn(source, at):
         g = tn(ffn_g[...].reshape(1024, 640), source[...].reshape(1024, 512)).astype(BF)
@@ -385,115 +349,109 @@
             rows = slice(32 * c, 32 * c + 32)
             b0[c, 80:112] = g[rows, 0:128]
             b1[c, 80:112] = g[rows, 128:256]
-            b2[c, 64:96] = g[rows, 256:384]
-            b3[c, 0:32] = g[rows, 384:512]
-            b3[c, 32:64] = g[rows, 512:640]
+            b1[c, 112:144] = g[rows, 256:384]
+            b2[c, 80:112] = g[rows, 384:512]
+            b3[c, 80:112] = g[rows, 512:640]
 
     def weights_in():
         g = tn(normed[...], dqkv[...]).astype(BF)
-        for j in range(4):
-            kv[j] = g[:, 256 + 128 * j:384 + 128 * j].reshape(4, 160, 128)
         for c in range(8):
-            b0[c, 0:80] = g[80 * c:80 * c + 80, 0:128]
-            b1[c, 0:80] = g[80 * c:80 * c + 80, 128:256]
-
-    bufs = [a_buf.at[p] for p in range(4)]
-    first = Reduction(bufs, bufs, [a_recv.at[p] for p in range(4)], [a_out.at[p] for p in range(4)], a_ss, a_rs, links, bits, across)
-    bufs = [b0, b1, b2, b3]
-    second = Reduction(bufs, bufs, [r0, r1, r2, r3], [o0, o1, o2, o3], b_ss, b_rs, links, bits, across)
-    third = KeyValue(kv, kv_work, kv_recv, kv_last, kv_out, k_ss, k_rs, links, bits, across, sibling, beside, xl, core)
-    done = {}
-
-    def begin(red):
-        red.start(0)
-        done[id(red)] = 0
-
-    def advance(red, steps):
-        at = done[id(red)]
-        if at < steps:
-            red.finish(at)
-            at += 1
-            if at < steps:
-                red.start(at)
-            done[id(red)] = at
-
+            rows = slice(80 * c, 80 * c + 80)
+            for j in range(4):
+                kv[j, c] = g[rows, 256 + 128 * j:384 + 128 * j]
+            b0[c, 0:80] = g[rows, 0:128]
+            b1[c, 0:80] = g[rows, 128:256]
+        extra["kv"] = send(kv.at[pl.ds((1 - core) * 2, 2)], kv_recv, k_ss.at[0], k_rs.at[0], sibling)
+        second.start()
+
+    def begin_third():
+        extra["kv"].wait()
+        for i, b in ((0, b2), (1, b3)):
+            for c in range(8):
+                b[c, 0:80] = (kv[core * 2 + i, c].astype(F32) + kv_recv[i, c].astype(F32)).astype(BF)
+        third.start()
+
+    extra = {}
+    first = Reduction((0, 1, 2, 3), [a_buf.at[p] for p in range(4)], [a_recv.at[p] for p in range(4)],
+                      [a_out.at[p] for p in range(4)], a_ss, a_rs, links, bits, across)
+    second = Reduction((0, 1), [b0, b1], [r0, r1], [o0, o1], b_ss, b_rs, links, bits, across)
+    third = Reduction((3, 0), [b2, b3], [r2, r3], [o2, o3], c_ss, c_rs, links, bits, across, (beside, corner))
+    jobs = {
+        "down": weights_down, "gate": lambda: weights_ffn(dgate, 0), "up": lambda: weights_ffn(dup, 80),
+        "first": first.start, "third": begin_third, "1": first.advance, "2": second.advance, "3": third.advance,
+    }
     gains[...] = jnp.zeros_like(gains)
     keys_stage()
     stages = [
         attention_stage, exchange(0), mid_stage, up_stage, exchange(1), out_stage, down_stage, exchange(2), attn_stage,
         back_stage, exchange(3), in_stage,
     ]
-    after = AFTER
     for tick in range(len(stages) + NC - 1):
         for p in range(NC):
             s = tick - p
             if 0 <= s < len(stages):
                 stages[s](NC - 1 - p)
-                for job in after.get((s, p), ()):
-                    if job == "down":
-                        weights_down()
-                    elif job == "gate":
-                        weights_ffn(dgate, 0)
-                    elif job == "up":
-                        weights_ffn(dup, 80)
-                        begin(first)
-                    elif job == "out":
-                        weights_out()
-                    elif job == "in":
-                        weights_in()
-                        begin(third)
-                        begin(second)
-                    elif job == "1":
-                        advance(first, 8)
-                    elif job == "2":
-                        advance(second, 8)
-                    elif job == "3":
-                        advance(third, 11)
+                for job in AFTER.get((s, p), ()):
+                    jobs[job]()
     gains[0:4, :] = gains[0:4, :] * 0.5
-    order = [sibling, beside] + links + [across]
-    for i in range(11):
-        if i < 7:
-            gc = send(gains, g_recv.at[i], g_ss.at[i], g_rs.at[i], order[i])
-        advance(third, 11)
-        advance(second, 8)
-        advance(first, 8)
-        if i < 7:
-            gc.wait()
-            gains[...] = gains[...] + g_recv[i]
+    order = [(sibling,), (beside, across, corner), (links[0],), (links[1],), (links[2],), (links[3],)]
+    slot, sent = 0, False
+    for i in range(10):
+        if i < len(order):
+            gc = []
+            for device in order[i]:
+                gc.append(send(gains, g_recv.at[slot], g_ss.at[slot], g_rs.at[slot], device))
+                slot += 1
+        third.advance()
+        if third.at == 8 and not sent:
+            sent = True
+            for j, o in ((0, o2), (1, o3)):
+                for c in range(8):
+                    kv_out[core * 2 + j, c] = o[c, 0:80]
+            kc = send(kv_out.at[pl.ds(core * 2, 2)], kv_out.at[pl.ds(core * 2, 2)], k_ss.at[1], k_rs.at[1], sibling)
+        second.advance()
+        first.advance()
+        if i < len(order):
+            for c in gc:
+                c.wait()
+            if i == 1:
+                gains[...] = (gains[...] + g_recv[slot - 2]) + (g_recv[slot - 3] + g_recv[slot - 1])
+            else:
+                gains[...] = gains[...] + g_recv[slot - 1]
+    kc.wait()
     for c in range(NC):
         state[c]["o"].wait()
         state[c]["g"].wait()
 
 
 AFTER = {
-    (6, 3): ("down", "gate", "up"),
-    (9, 1): ("1",),
-    (9, 2): ("1",),
-    (9, 3): ("out", "in", "1"),
-    (10, 3): ("1", "3"),
+    (6, 3): ("down", "gate", "up", "first"),
+    (7, 3): ("1",),
+    (10, 1): ("1",),
+    (8, 3): ("1",),
+    (10, 2): ("1",),
+    (9, 3): ("third", "1", "2"),
     (11, 2): ("2", "3"),
-    (11, 3): ("1", "2", "3"),
+    (10, 3): ("1",),
+    (11, 3): ("2", "3", "1"),
 }
 
 
 def unpack_kernel(a, b0, b1, b2, b3, kv, gains, query, key, value, out, gate, up, down, g0, g1, g2, g3, g4, g5):
-    for p in range(4):
-        cols = slice(128 * p, 128 * p + 128)
-        for c in range(8):
+    for c in range(8):
+        for p in range(4):
+            cols = slice(128 * p, 128 * p + 128)
             gate[80 * c:80 * c + 80, cols] = a[p, c, 0:80].astype(F32)
             up[80 * c:80 * c + 80, cols] = a[p, c, 80:160].astype(F32)
             down[64 * c:64 * c + 64, cols] = a[p, c, 160:224].astype(F32)
-    for c in range(8):
+            down[128 * p + 16 * c:128 * p + 16 * c + 16, 512:640] = a[p, c, 224:240].astype(F32)
         for p, b in ((0, b0), (1, b1)):
             query[80 * c:80 * c + 80, 128 * p:128 * p + 128] = b[c, 0:80].astype(F32)
-            out[32 * c:32 * c + 32, 128 * p:128 * p + 128] = b[c, 80:112].astype(F32)
-        out[32 * c:32 * c + 32, 256:384] = b2[c, 64:96].astype(F32)
-        down[64 * c:64 * c + 64, 512:640] = b2[c, 0:64].astype(F32)
-        out[32 * c:32 * c + 32, 384:512] = b3[c, 0:32].astype(F32)
-        out[32 * c:32 * c + 32, 512:640] = b3[c, 32:64].astype(F32)
-    for j in range(2):
-        key[:, 128 * j:128 * j + 128] = kv[j].reshape(640, 128).astype(F32)
-        value[:, 128 * j:128 * j + 128] = kv[2 + j].reshape(640, 128).astype(F32)
+        for p, b, at in ((0, b0, 80), (1, b1, 80), (2, b1, 112), (3, b2, 80), (4, b3, 80)):
+            out[32 * c:32 * c + 32, 128 * p:128 * p + 128] = b[c, at:at + 32].astype(F32)
+        for j in range(2):
+            key[80 * c:80 * c + 80, 128 * j:128 * j + 128] = kv[j, c].astype(F32)
+            value[80 * c:80 * c + 80, 128 * j:128 * j + 128] = kv[2 + j, c].astype(F32)
     for i, g in ((3, g0), (0, g1), (1, g2), (2, g3)):
         g[...] = gains[i, :]
     g4[...] = gains[4, 0:256]
@@ -509,8 +467,8 @@
     count = NC * 12
     stacks = pl.pallas_call(
         layer_kernel,
-        out_shape=(sds(blocks, BF), sds(blocks, BF), sds((4, 8, 224, 128), BF), sds((8, 112, 128), BF), sds((8, 112, 128), BF),
-                   sds((8, 96, 128), BF), sds((8, 64, 128), BF), sds((4, 4, 160, 128), BF), sds((8, 640), F32)),
+        out_shape=(sds(blocks, BF), sds(blocks, BF), sds((4, 8, 240, 128), BF), sds((8, 112, 128), BF), sds((8, 144, 128), BF),
+                   sds((8, 112, 128), BF), sds((8, 112, 128), BF), sds((4, 8, 80, 128), BF), sds((8, 640), F32)),
         in_specs=[VMEM] * len(operands),
         out_specs=[VMEM] * 9,
         scratch_shapes=[
@@ -519,14 +477,15 @@
             v(blocks, BF), v((NC, CR, 512), BF), v((NC, CR, 512), F32), v((NC, CR, 512), F32), v((NC, CR, 512), BF),
             v((NC, CR, 512), BF), v(half, F32), v(half, F32), v((4, *half), BF), v((4, *half), BF),
             v((1024, 256), F32), v((1024, 256), F32), v((1024, 768), BF),
-            v((4, 8, 224, 128), BF),
-            v((8, 112, 128), BF), v((8, 112, 128), BF), v((8, 96, 128), BF), v((8, 64, 128), BF),
-            v((4, 9, 224, 128), BF),
-            v((9, 112, 128), BF), v((9, 112, 128), BF), v((9, 96, 128), BF), v((9, 64, 128), BF),
-            v((4, 4, 160, 128), BF), v((2, 4, 160, 128), BF), v((5, 4, 160, 128), BF), v((4, 160, 128), BF),
-            v((7, 8, 640), F32),
+            v((4, 8, 240, 128), BF),
+            v((8, 112, 128), BF), v((8, 144, 128), BF), v((8, 112, 128), BF), v((8, 112, 128), BF),
+            v((4, 9, 240, 128), BF),
+            v((9, 112, 128), BF), v((9, 144, 128), BF), v((11, 112, 128), BF), v((11, 112, 128), BF),
+            v((4, 8, 80, 128), BF), v((2, 8, 80, 128), BF),
+            v((8, 8, 640), F32),
             dma((count + 16,)), dma((count + 16,)),
-            dma((4, 8)), dma((4, 8)), dma((4, 8)), dma((4, 8)), dma((11,)), dma((11,)), dma((7,)), dma((7,)),
+            dma((4, 8)), dma((4, 8)), dma((2, 8)), dma((2, 8)), dma((2, 10)), dma((2, 10)), dma((2,)), dma((2,)),
+            dma((8,)), dma((8,)),
         ],
         compiler_params=pltpu.CompilerParams(collective_id=7, has_side_effects=True, vmem_limit_bytes=VMEM_LIMIT),
         name="layer",

time: 145 us -> 139 us (0.959)
  Pallas kernels: 137 us -> 132 us
    pallas_call x1, Pallas kernels: 132 us -> 127 us  [layer(): pl.pallas_call(layer_kernel, out_shape=(sds(blocks, BF), sds(blocks, BF),...]
where the time goes in v5:
time: 139 us
  Pallas kernels  132 us (95%)
  other arithmetic  3.73 us (3%)
  local copies, waits for them, and re-layouts  2.84 us (2%)
    pallas_call x1, Pallas kernels, layer(): pl.pallas_call(layer_kernel, out_shape=(sds(blocks, BF), sds(blocks, BF),...  127 us
    pallas_call x1, Pallas kernels, layer(): pl.pallas_call(unpack_kernel, out_shape=(sds((640, 256), F32), sds((640,...  5.04 us
    sin x1, other arithmetic, rope_tables(): return (jnp.cos(angles), jnp.sin(angles))  3.03 us
    unnamed x6, local copies, waits for them, and re-layouts  2.84 us

profile of v5, /device:TPU:1, one launch (start us, length us, event | category | flops | bytes accessed | tf_op | source)
XLA Modules:
  0.0 138.8 jit_solution(9656934009260164867)
XLA Ops:
  0.7 0.7 convert_element_type.3
  1.4 3.0 %multiply_sine_fusion = (f32[1024,128]{1,0:T(8,128)}, f32[1024,128]{1,0:T(8,128)}) fusion(f32[128]{0:T(128)S(1)} %multiply_power_fusion, f32[1024]{0:T(1024)S(1)} %convert_element_type.3), kind=kLoop, calls=%fused_computation | loop fusion | flops 131072 | bytes 1053184 | tf_op jit(solution)/shard_map/sin | solution.py:511
  4.4 126.5 %layer.1 = (bf16[4,2,128,640]{3,2,1,0:T(8,128)(2,1)}, bf16[4,2,128,640]{3,2,1,0:T(8,128)(2,1)}, bf16[4,8,240,128]{3,2,1,0:T(8,128)(2,1)}, bf16[8,112,128]{2,1,0:...) custom-call(bf16[4,2,128,640]{3,2,1,0:T(8,128)(2,1)} %bitcast.7, ...), custom_call_target="tpu_custom_call" | custom-call | tf_op jit(solution)/shard_map/layer/pallas_call | solution.py:468
  130.9 0.0 copy-start.1
  130.9 5.0 %unpack_grads.1 = (f32[640,256]{1,0:T(8,128)}, f32[640,256]{1,0:T(8,128)}, f32[640,256]{1,0:T(8,128)}, f32[256,640]{1,0:T(8,128)}, f32[640,512]{1,0:T(8,128)}, /...) custom-call(bf16[4,8,240,128]{3,2,1,0:T(8,128)(2,1)} %get-tuple-elem, ...), custom_call_target="tpu_custom_call" | custom-call | tf_op jit(solution)/shard_map/unpack_grads/pallas_call | solution.py:493
  136.0 0.0 copy-done.1
  136.0 0.0 copy-start
  136.0 1.1 copy.34
  137.0 0.7 copy-done
  137.8 1.1 copy.35
  (1 shorter events, 0.0 us)
Async XLA Ops:
  130.9 5.1 %copy-start.1 = (bf16[4,2,128,640]{3,2,1,0:T(8,128)(2,1)S(1)}, bf16[4,2,128,640]{3,2,1,0:T(8,128)(2,1)}, u32[]{:S(2)}) copy-start(bf16[4,2,128,640]{3,2,1,0:T(8,128)(2,1)} %get-tuple-element.37) | copy-start | bytes 3932164
  136.0 1.8 %copy-start = (bf16[4,2,128,640]{3,2,1,0:T(8,128)(2,1)S(1)}, bf16[4,2,128,640]{3,2,1,0:T(8,128)(2,1)}, u32[]{:S(2)}) copy-start(bf16[4,2,128,640]{3,2,1,0:T(8,128)(2,1)} %get-tuple-element.38) | copy-start | bytes 3932164

commit v6 on v5

--- a/solution.py
+++ b/solution.py
@@ -167,7 +167,7 @@
                  output, in_grad, a_out, o0, o1, o2, o3, kv_out, gains,
                  normed, q_raw, k_raw, q, k, v, prob, heads, part, ffn_g, dffn_g, dattn, hid, act_a, act_b, dgate, dup,
                  attn_own, mid_own, recv_a, recv_b, dk, dv, dqkv,
-                 a_buf, b0, b1, b2, b3, a_recv, r0, r1, r2, r3, kv, kv_recv, g_recv,
+                 a_buf, b0, b1, b2, b3, a_recv, r0, r1, r2, r3, kv, kv_recv, g_recv, in_acc, out_acc, down_acc, up_acc,
                  ssem, rsem, a_ss, a_rs, b_ss, b_rs, c_ss, c_rs, k_ss, k_rs, g_ss, g_rs):
     links, bits, across, sibling, beside, corner, xl, core = neighbours()
     greet(links + [across, sibling, beside, corner])
@@ -318,6 +318,8 @@
             weights_out()
             weights_in()
         term = nt(raws[0], wq[...]) + nt(raws[1], wk[...]) + nt(raws[2], wv[...])
+        xv = x[i].reshape(CR, 640).astype(F32)
+        gains[3:4, :] = gains[3:4, :] + jnp.sum(term * (xv * inv_rms(xv)), axis=0, keepdims=True)
         part[3, i] = term.astype(BF).reshape(2, OW, 640)
         share(3, i)
 
@@ -325,12 +327,18 @@
         d = total(3, i)
         xv = x[i, own].astype(F32)
         r = inv_rms(xv)
-        gains[3:4, :] = gains[3:4, :] + jnp.sum(d * xv * r, axis=0, keepdims=True)
         in_grad[i, own] = (mid_own[i] + rms_back(xv, r, d * vec(g_in))).astype(BF)
         state[i]["g"] = give(in_grad, i)
 
+    def ffn_early():
+        n = 1024 - CR
+        f = ffn_g[1:].reshape(n, 640)
+        down_acc[...] = tn(hid[1:].reshape(n, 512), dffn_g[1:].reshape(n, 640))
+        up_acc[0] = tn(f, dgate[1:].reshape(n, 512))
+        up_acc[1] = tn(f, dup[1:].reshape(n, 512))
+
     def weights_down():
-        g = tn(hid[...].reshape(1024, 512), dffn_g[...].reshape(1024, 640)).astype(BF)
+        g = (down_acc[...] + tn(hid[0], dffn_g[0].reshape(CR, 640))).astype(BF)
         for s in range(8):
             for p in range(4):
                 a_buf[p, s, 160:224] = g[64 * s:64 * s + 64, 128 * p:128 * p + 128]
@@ -338,13 +346,17 @@
                 a_buf[p, s, 224:240] = g[128 * p + 16 * s:128 * p + 16 * s + 16, 512:640]
 
     def weights_ffn(source, at):
-        g = tn(ffn_g[...].reshape(1024, 640), source[...].reshape(1024, 512)).astype(BF)
+        g = (up_acc[at // 80] + tn(ffn_g[0].reshape(CR, 640), source[0])).astype(BF)
         for s in range(8):
             for p in range(4):
                 a_buf[p, s, at:at + 80] = g[80 * s:80 * s + 80, 128 * p:128 * p + 128]
 
+    def weights_early():
+        out_acc[...] = tn(heads[CR:], dattn[1:].reshape(1024 - CR, 640))
+        in_acc[...] = tn(normed[CR:], dqkv[CR:])
+
     def weights_out():
-        g = tn(heads[...], dattn[...].reshape(1024, 640)).astype(BF)
+        g = (out_acc[...] + tn(heads[0:CR], dattn[0].reshape(CR, 640))).astype(BF)
         for c in range(8):
             rows = slice(32 * c, 32 * c + 32)
             b0[c, 80:112] = g[rows, 0:128]
@@ -354,7 +366,7 @@
             b3[c, 80:112] = g[rows, 512:640]
 
     def weights_in():
-        g = tn(normed[...], dqkv[...]).astype(BF)
+        g = (in_acc[...] + tn(normed[0:CR], dqkv[0:CR])).astype(BF)
         for c in range(8):
             rows = slice(80 * c, 80 * c + 80)
             for j in range(4):
@@ -371,7 +383,32 @@
                 b[c, 0:80] = (kv[core * 2 + i, c].astype(F32) + kv_recv[i, c].astype(F32)).astype(BF)
         third.start()
 
-    extra = {}
+    extra = {"gain": 0}
+    order = [(sibling,), (beside, across, corner), (links[0],), (links[1],), (links[2],), (links[3],)]
+
+    def send_gains():
+        i = extra["gain"]
+        if i < 6:
+            at = (0, 1, 4, 5, 6, 7)[i]
+            extra["copies"] = [send(gains, g_recv.at[at + j], g_ss.at[at + j], g_rs.at[at + j], d) for j, d in enumerate(order[i])]
+
+    def begin_gains():
+        gains[0:3, :] = gains[0:3, :] * 0.5
+        send_gains()
+
+    def swap_gains():
+        i = extra["gain"]
+        if i == 6:
+            return
+        for copy in extra["copies"]:
+            copy.wait()
+        if i == 1:
+            gains[...] = (gains[...] + g_recv[2]) + (g_recv[1] + g_recv[3])
+        else:
+            gains[...] = gains[...] + g_recv[(0, 1, 4, 5, 6, 7)[i]]
+        extra["gain"] = i + 1
+        send_gains()
+
     first = Reduction((0, 1, 2, 3), [a_buf.at[p] for p in range(4)], [a_recv.at[p] for p in range(4)],
                       [a_out.at[p] for p in range(4)], a_ss, a_rs, links, bits, across)
     second = Reduction((0, 1), [b0, b1], [r0, r1], [o0, o1], b_ss, b_rs, links, bits, across)
@@ -379,6 +416,7 @@
     jobs = {
         "down": weights_down, "gate": lambda: weights_ffn(dgate, 0), "up": lambda: weights_ffn(dup, 80),
         "first": first.start, "third": begin_third, "1": first.advance, "2": second.advance, "3": third.advance,
+        "gains": begin_gains, "g": swap_gains, "acc": weights_early, "ffn": ffn_early,
     }
     gains[...] = jnp.zeros_like(gains)
     keys_stage()
@@ -393,15 +431,8 @@
                 stages[s](NC - 1 - p)
                 for job in AFTER.get((s, p), ()):
                     jobs[job]()
-    gains[0:4, :] = gains[0:4, :] * 0.5
-    order = [(sibling,), (beside, across, corner), (links[0],), (links[1],), (links[2],), (links[3],)]
-    slot, sent = 0, False
-    for i in range(10):
-        if i < len(order):
-            gc = []
-            for device in order[i]:
-                gc.append(send(gains, g_recv.at[slot], g_ss.at[slot], g_rs.at[slot], device))
-                slot += 1
+    sent = False
+    for i in range(9):
         third.advance()
         if third.at == 8 and not sent:
             sent = True
@@ -410,14 +441,9 @@
                     kv_out[core * 2 + j, c] = o[c, 0:80]
             kc = send(kv_out.at[pl.ds(core * 2, 2)], kv_out.at[pl.ds(core * 2, 2)], k_ss.at[1], k_rs.at[1], sibling)
         second.advance()
-        first.advance()
-        if i < len(order):
-            for c in gc:
-                c.wait()
-            if i == 1:
-                gains[...] = (gains[...] + g_recv[slot - 2]) + (g_recv[slot - 3] + g_recv[slot - 1])
-            else:
-                gains[...] = gains[...] + g_recv[slot - 1]
+        swap_gains()
+        if i in LATE:
+            first.advance()
     kc.wait()
     for c in range(NC):
         state[c]["o"].wait()
@@ -425,37 +451,64 @@
 
 
 AFTER = {
+    (6, 2): ("ffn",),
     (6, 3): ("down", "gate", "up", "first"),
-    (7, 3): ("1",),
+    (8, 2): ("1",),
     (10, 1): ("1",),
+    (9, 2): ("acc",),
     (8, 3): ("1",),
-    (10, 2): ("1",),
-    (9, 3): ("third", "1", "2"),
-    (11, 2): ("2", "3"),
+    (9, 3): ("gains", "third", "1", "2"),
+    (11, 2): ("2", "3", "g"),
     (10, 3): ("1",),
-    (11, 3): ("2", "3", "1"),
+    (11, 3): ("2", "3", "g"),
 }
-
-
-def unpack_kernel(a, b0, b1, b2, b3, kv, gains, query, key, value, out, gate, up, down, g0, g1, g2, g3, g4, g5):
+LATE = (0, 2, 5)
+
+
+def unpack_kernel(a, b0, b1, b2, b3, kv, gains, y, dx, query_o, key_o, value_o, out_o, gate_o, up_o, down_o, y_o, dx_o,
+                  g0, g1, g2, g3, g4, g5, query, key, value, out, gate, up, down, sems):
+    copies = []
+
+    def leave(src, dst):
+        copy = pltpu.make_async_copy(src, dst, sems.at[len(copies)])
+        copy.start()
+        copies.append(copy)
+
+    leave(y, y_o)
+    leave(dx, dx_o)
     for c in range(8):
         for p in range(4):
-            cols = slice(128 * p, 128 * p + 128)
-            gate[80 * c:80 * c + 80, cols] = a[p, c, 0:80].astype(F32)
-            up[80 * c:80 * c + 80, cols] = a[p, c, 80:160].astype(F32)
-            down[64 * c:64 * c + 64, cols] = a[p, c, 160:224].astype(F32)
+            gate[80 * c:80 * c + 80, 128 * p:128 * p + 128] = a[p, c, 0:80].astype(F32)
+    leave(gate, gate_o)
+    for c in range(8):
+        for p in range(4):
+            up[80 * c:80 * c + 80, 128 * p:128 * p + 128] = a[p, c, 80:160].astype(F32)
+    leave(up, up_o)
+    for c in range(8):
+        for p in range(4):
+            down[64 * c:64 * c + 64, 128 * p:128 * p + 128] = a[p, c, 160:224].astype(F32)
             down[128 * p + 16 * c:128 * p + 16 * c + 16, 512:640] = a[p, c, 224:240].astype(F32)
+    leave(down, down_o)
+    for c in range(8):
+        for p, b, at in ((0, b0, 80), (1, b1, 80), (2, b1, 112), (3, b2, 80), (4, b3, 80)):
+            out[32 * c:32 * c + 32, 128 * p:128 * p + 128] = b[c, at:at + 32].astype(F32)
+    leave(out, out_o)
+    for c in range(8):
         for p, b in ((0, b0), (1, b1)):
             query[80 * c:80 * c + 80, 128 * p:128 * p + 128] = b[c, 0:80].astype(F32)
-        for p, b, at in ((0, b0, 80), (1, b1, 80), (2, b1, 112), (3, b2, 80), (4, b3, 80)):
-            out[32 * c:32 * c + 32, 128 * p:128 * p + 128] = b[c, at:at + 32].astype(F32)
+    leave(query, query_o)
+    for c in range(8):
         for j in range(2):
             key[80 * c:80 * c + 80, 128 * j:128 * j + 128] = kv[j, c].astype(F32)
             value[80 * c:80 * c + 80, 128 * j:128 * j + 128] = kv[2 + j, c].astype(F32)
+    leave(key, key_o)
+    leave(value, value_o)
     for i, g in ((3, g0), (0, g1), (1, g2), (2, g3)):
         g[...] = gains[i, :]
     g4[...] = gains[4, 0:256]
     g5[...] = gains[4, 256:512]
+    for copy in copies:
+        copy.wait()
 
 
 def layer(*operands):
@@ -482,7 +535,7 @@
             v((4, 9, 240, 128), BF),
             v((9, 112, 128), BF), v((9, 144, 128), BF), v((11, 112, 128), BF), v((11, 112, 128), BF),
             v((4, 8, 80, 128), BF), v((2, 8, 80, 128), BF),
-            v((8, 8, 640), F32),
+            v((8, 8, 640), F32), v((640, 768), F32), v((256, 640), F32), v((512, 640), F32), v((2, 640, 512), F32),
             dma((count + 16,)), dma((count + 16,)),
             dma((4, 8)), dma((4, 8)), dma((2, 8)), dma((2, 8)), dma((2, 10)), dma((2, 10)), dma((2,)), dma((2,)),
             dma((8,)), dma((8,)),
@@ -490,18 +543,19 @@
         compiler_params=pltpu.CompilerParams(collective_id=7, has_side_effects=True, vmem_limit_bytes=VMEM_LIMIT),
         name="layer",
     )(*operands)
+    big = [(640, 256), (640, 256), (640, 256), (256, 640), (640, 512), (640, 512), (512, 640)]
+    small = [(640,), (640,), (640,), (640,), (256,), (256,)]
+    anywhere = pl.BlockSpec(memory_space=pl.ANY)
     outs = pl.pallas_call(
         unpack_kernel,
-        out_shape=(sds((640, 256), F32), sds((640, 256), F32), sds((640, 256), F32), sds((256, 640), F32),
-                   sds((640, 512), F32), sds((640, 512), F32), sds((512, 640), F32),
-                   sds((640,), F32), sds((640,), F32), sds((640,), F32), sds((640,), F32),
-                   sds((256,), F32), sds((256,), F32)),
-        in_specs=[VMEM] * 7,
-        out_specs=[VMEM] * 13,
+        out_shape=[sds(shape, F32) for shape in big] + [sds(blocks, BF)] * 2 + [sds(shape, F32) for shape in small],
+        in_specs=[VMEM] * 9,
+        out_specs=[anywhere] * 9 + [VMEM] * 6,
+        scratch_shapes=[v(shape, F32) for shape in big] + [dma((9,))],
         compiler_params=pltpu.CompilerParams(vmem_limit_bytes=VMEM_LIMIT),
         name="unpack_grads",
-    )(*stacks[2:])
-    return stacks[0], stacks[1], outs
+    )(*stacks[2:], stacks[0], stacks[1])
+    return outs[7], outs[8], (*outs[:7], *outs[9:])
 
 
 def rope_tables(positions, head_size):

time: 139 us -> 135 us (0.971)
  local copies, waits for them, and re-layouts: 2.84 us -> 0 us
  Pallas kernels: 132 us -> 130 us
    pallas_call x1, Pallas kernels: 127 us -> 123 us  [layer(): pl.pallas_call(layer_kernel, out_shape=(sds(blocks, BF), sds(blocks, BF),...]
    unnamed x6 -> x0, local copies, waits for them, and re-layouts: 2.84 us -> none
    pallas_call x1, Pallas kernels: 5.04 us -> 7.15 us  [layer(): pl.pallas_call(unpack_kernel, out_shape=[sds(shape, F32) for shape in big...]
where the time goes in v6:
time: 135 us
  Pallas kernels  130 us (96%)
  other arithmetic  3.73 us (3%)
    pallas_call x1, Pallas kernels, layer(): pl.pallas_call(layer_kernel, out_shape=(sds(blocks, BF), sds(blocks, BF),...  123 us
    pallas_call x1, Pallas kernels, layer(): pl.pallas_call(unpack_kernel, out_shape=[sds(shape, F32) for shape in big...  7.15 us
    sin x1, other arithmetic, rope_tables(): return (jnp.cos(angles), jnp.sin(angles))  3.03 us

profile of v6, /device:TPU:1, one launch (start us, length us, event | category | flops | bytes accessed | tf_op | source)
XLA Modules:
  0.0 134.9 jit_solution(3519156153173934124)
XLA Ops:
  0.7 0.7 convert_element_type.3
  1.4 3.0 %multiply_sine_fusion = (f32[1024,128]{1,0:T(8,128)}, f32[1024,128]{1,0:T(8,128)}) fusion(f32[128]{0:T(128)S(1)} %multiply_power_fusion, f32[1024]{0:T(1024)S(1)} %convert_element_type.3), kind=kLoop, calls=%fused_computation | loop fusion | flops 131072 | bytes 1053184 | tf_op jit(solution)/shard_map/sin | solution.py:565
  4.4 123.2 %layer.1 = (bf16[4,2,128,640]{3,2,1,0:T(8,128)(2,1)}, bf16[4,2,128,640]{3,2,1,0:T(8,128)(2,1)}, bf16[4,8,240,128]{3,2,1,0:T(8,128)(2,1)}, bf16[8,112,128]{2,1,0:...) custom-call(bf16[4,2,128,640]{3,2,1,0:T(8,128)(2,1)} %bitcast.5, ...), custom_call_target="tpu_custom_call" | custom-call | tf_op jit(solution)/shard_map/layer/pallas_call | solution.py:521
  127.6 7.1 %unpack_grads.1 = (f32[640,256]{1,0:T(8,128)}, f32[640,256]{1,0:T(8,128)}, f32[640,256]{1,0:T(8,128)}, f32[256,640]{1,0:T(8,128)}, f32[640,512]{1,0:T(8,128)}, /...) custom-call(bf16[4,8,240,128]{3,2,1,0:T(8,128)(2,1)} %get-tuple-elem, ...), custom_call_target="tpu_custom_call" | custom-call | tf_op jit(solution)/shard_map/unpack_grads/pallas_call | solution.py:549
  (1 shorter events, 0.0 us)

commit v7 on v6

--- a/solution.py
+++ b/solution.py
@@ -1,4 +1,6 @@
-import jax, jax.numpy as jnp
+import jax
+import jax.numpy as jnp
+import numpy as np
 from jax import lax
 from jax.experimental import pallas as pl
 from jax.experimental.pallas import tpu as pltpu
@@ -163,11 +165,11 @@
     return g[...]
 
 
-def layer_kernel(x, cot, segs, cos_t, sin_t, wq, wk, wv, wo, wg, wu, wd, g_in, g_ao, g_fi, g_fo, g_q, g_k,
+def layer_kernel(x, cot, segs, pos, far, near, wq, wk, wv, wo, wg, wu, wd, g_in, g_ao, g_fi, g_fo, g_q, g_k,
                  output, in_grad, a_out, o0, o1, o2, o3, kv_out, gains,
                  normed, q_raw, k_raw, q, k, v, prob, heads, part, ffn_g, dffn_g, dattn, hid, act_a, act_b, dgate, dup,
                  attn_own, mid_own, recv_a, recv_b, dk, dv, dqkv,
-                 a_buf, b0, b1, b2, b3, a_recv, r0, r1, r2, r3, kv, kv_recv, g_recv, in_acc, out_acc, down_acc, up_acc,
+                 a_buf, b0, b1, b2, b3, a_recv, r0, r1, r2, r3, kv, kv_recv, g_recv, in_acc, out_acc, down_acc, up_acc, cos_t, sin_t,
                  ssem, rsem, a_ss, a_rs, b_ss, b_rs, c_ss, c_rs, k_ss, k_rs, g_ss, g_rs):
     links, bits, across, sibling, beside, corner, xl, core = neighbours()
     greet(links + [across, sibling, beside, corner])
@@ -200,6 +202,15 @@
     def keys_stage():
         for c in range(NC - 1, -1, -1):
             rows = slice(c * CR, c * CR + CR)
+            at = pos[:, rows]
+            picked = []
+            for table, index in ((far, lax.shift_right_logical(at, 5)), (near, at & 31)):
+                hot = (lax.broadcasted_iota(jnp.int32, (table.shape[0], CR), 0) == index).astype(F32).astype(BF)
+                parts = tn(hot, table[...])
+                picked.append(parts[:, 0:256] + (parts[:, 256:512] + parts[:, 512:768]))
+            (c1, s1), (c2, s2) = ((t[:, :128], t[:, 128:]) for t in picked)
+            cos_t[rows] = c1 * c2 - s1 * s2
+            sin_t[rows] = s1 * c2 + c1 * s2
             xv = x[c].reshape(CR, 640).astype(F32)
             n = (xv * inv_rms(xv) * vec(g_in)).astype(BF)
             normed[rows] = n
@@ -536,6 +547,7 @@
             v((9, 112, 128), BF), v((9, 144, 128), BF), v((11, 112, 128), BF), v((11, 112, 128), BF),
             v((4, 8, 80, 128), BF), v((2, 8, 80, 128), BF),
             v((8, 8, 640), F32), v((640, 768), F32), v((256, 640), F32), v((512, 640), F32), v((2, 640, 512), F32),
+            v((1024, 128), F32), v((1024, 128), F32),
             dma((count + 16,)), dma((count + 16,)),
             dma((4, 8)), dma((4, 8)), dma((2, 8)), dma((2, 8)), dma((2, 10)), dma((2, 10)), dma((2,)), dma((2,)),
             dma((8,)), dma((8,)),
@@ -558,11 +570,14 @@
     return outs[7], outs[8], (*outs[:7], *outs[9:])
 
 
-def rope_tables(positions, head_size):
-    half_size = head_size // 2
-    inv_freq = ROPE_BASE ** (-2.0 * jnp.arange(half_size, dtype=jnp.float32) / head_size)
-    angles = positions.astype(jnp.float32)[:, None] * inv_freq[None, :]
-    return (jnp.cos(angles), jnp.sin(angles))
+def turn_table(count, step):
+    angles = np.arange(count)[:, None] * float(step) * ROPE_BASE ** (-2.0 * np.arange(128)[None, :] / 256)
+    rest = np.concatenate([np.cos(angles), np.sin(angles)], axis=1)
+    parts = []
+    for _ in range(3):
+        parts.append(rest.astype(np.float32).astype(BF))
+        rest = rest - parts[-1].astype(np.float64)
+    return jnp.asarray(np.concatenate(parts, axis=1))
 
 
 def local(
@@ -585,9 +600,9 @@
     g_key,
 ):
     blocks = (NC, 2, OW, 640)
-    cos_t, sin_t = rope_tables(positions, 256)
     output, input_grad, summed = layer(
-        inputs.reshape(blocks), cotangent.reshape(blocks), segments.reshape(1, 1024), cos_t, sin_t,
+        inputs.reshape(blocks), cotangent.reshape(blocks), segments.reshape(1, 1024), positions.reshape(1, 1024),
+        turn_table(64, 32), turn_table(32, 1),
         w_query, w_key, w_value, w_out, w_gate, w_up, w_down,
         g_attn_in, g_attn_out, g_ffn_in, g_ffn_out, g_query, g_key,
     )

time: 135 us -> 131 us (0.970)
  other arithmetic: 3.73 us -> 0 us
    sin x1 -> x0, other arithmetic: 3.03 us -> none  [rope_tables(): return (jnp.cos(angles), jnp.sin(angles))]
where the time goes in v7:
time: 131 us
  Pallas kernels  130 us (99%)
    pallas_call x1, Pallas kernels, layer(): pl.pallas_call(layer_kernel, out_shape=(sds(blocks, BF), sds(blocks, BF),...  123 us
    pallas_call x1, Pallas kernels, layer(): pl.pallas_call(unpack_kernel, out_shape=[sds(shape, F32) for shape in big...  7.15 us

profile of v7, /device:TPU:1, one launch (start us, length us, event | category | flops | bytes accessed | tf_op | source)
XLA Modules:
  0.0 131.0 jit_solution(2666972212608659200)
XLA Ops:
  0.7 123.0 %layer.1 = (bf16[4,2,128,640]{3,2,1,0:T(8,128)(2,1)}, bf16[4,2,128,640]{3,2,1,0:T(8,128)(2,1)}, bf16[4,8,240,128]{3,2,1,0:T(8,128)(2,1)}, bf16[8,112,128]{2,1,0:...) custom-call(bf16[4,2,128,640]{3,2,1,0:T(8,128)(2,1)} %bitcast.6, ...), custom_call_target="tpu_custom_call" | custom-call | tf_op jit(solution)/shard_map/layer/pallas_call | solution.py:532
  123.6 7.1 %unpack_grads.1 = (f32[640,256]{1,0:T(8,128)}, f32[640,256]{1,0:T(8,128)}, f32[640,256]{1,0:T(8,128)}, f32[256,640]{1,0:T(8,128)}, f32[640,512]{1,0:T(8,128)}, /...) custom-call(bf16[4,8,240,128]{3,2,1,0:T(8,128)(2,1)} %get-tuple-elem, ...), custom_call_target="tpu_custom_call" | custom-call | tf_op jit(solution)/shard_map/unpack_grads/pallas_call | solution.py:561
